TPU v7x, 256 devices: a whole 4x4x8 slice. The times are simulated.
256 devices in a mesh: row: 16 (over x, z_lo), col: 16 (over y, z_hi, core).
Axes of the slice: x: 4, y: 4, z: 8 (z_hi: 2, z_lo: 4; z = z_hi * 4 + z_lo), core: 2. Of those that a mesh axis runs over, the one named last changes fastest.
Arguments:
- left_edges: bfloat16 [128, 256, 128], P('row', 'col'), may hold values from -6 to 6
- right_edges: bfloat16 [256, 256, 128], P('row', 'col'), may hold values from -6 to 6
- left_mask: int32 [128, 256], P('row', 'col'), may hold values 0 or 1
- right_mask: int32 [256, 256], P('row', 'col'), may hold values 0 or 1
- cotangent: bfloat16 [128, 256, 128], P('row', 'col'), may hold values from -6 to 6
- query_weight: bfloat16 [128, 128], replicated, may hold values from -1 to 1
- key_weight: bfloat16 [128, 128], replicated, may hold values from -1 to 1
- left_weight: bfloat16 [128, 128], replicated, may hold values from -0.5 to 0.5
- right_weight: bfloat16 [128, 128], replicated, may hold values from -0.5 to 0.5
- out_weight: bfloat16 [128, 128], replicated, may hold values from -0.5 to 0.5
Outputs:
- left_grad: float32 [128, 256, 128], P('row', 'col')
- right_grad: float32 [256, 256, 128], P('row', 'col')
- proj_grads: float32 [4, 128, 128], replicated
- out_grad: float32 [128, 128], replicated
All inputs are finite; a program needn't handle non-finite values. No bound on the sum of `left_mask` or of `right_mask` on one device may be relied on, other than what follows from the above.
Results may differ from a plain program's by a relative error of at most 0.019.
The roundings to bfloat16 on the way count: a program that leaves them out, or rounds other values in their place, can miss the bound.
Values may be sent and summed in bfloat16 or wider, within the bound.
No kernel may reach another device: no remote copies, remote signals or barrier semaphores. Data moves between devices by JAX's collectives and lax.ppermute only.
A program may use at most 128 MiB of HBM per device.

v0:
```python
import math

import jax
import jax.numpy as jnp
from jax import lax
from jax.experimental import pallas as pl
from jax.experimental.pallas import tpu as pltpu
from jax.sharding import PartitionSpec as P

HEADS = 4
HEAD_DIM = 32
BF = jnp.bfloat16
F32 = jnp.float32


def flip(k):
    return [(i, i ^ k) for i in range(16)]


def gather_col(block):
    pair = jnp.stack([block, lax.ppermute(block, "col", flip(2))])
    quads = jnp.concatenate([pair] + [lax.ppermute(pair, "col", flip(k)) for k in (4, 8, 12)])
    return quads, lax.ppermute(quads, "col", flip(1))


def gather_row(block):
    line = jnp.stack([block] + [lax.ppermute(block, "row", flip(k)) for k in (1, 2, 3)])
    return [line] + [lax.ppermute(line, "row", flip(k)) for k in (4, 8, 12)]


def left_place(col, b):
    apart = col ^ b
    return (apart & 1) * 8 + (apart >> 2) * 2 + ((apart >> 1) & 1)


def add_up(own, others):
    total = own.astype(F32)
    for other in others:
        total = total + other.astype(F32)
    return total


def meet(own, axis, flips):
    came = [lax.ppermute(own, axis, flip(k)).astype(F32) for k in flips]
    return (own.astype(F32) + came[0]) + (came[1] + came[2])


def nt(a, b):
    return lax.dot_general(a, b, (((1,), (1,)), ((), ())), preferred_element_type=F32)


def nn(a, b):
    return jnp.dot(a, b, preferred_element_type=F32)


def tn(a, b):
    return lax.dot_general(a, b, (((0,), (0,)), ((), ())), preferred_element_type=F32)


def triple_kernel(
    at_ref,
    left0,
    left1,
    right0,
    right1,
    right2,
    right3,
    cot_ref,
    wl_ref,
    wr_ref,
    wo_ref,
    lout,
    rout,
    wout,
    xl,
    xr,
    ql,
    kr,
    gql,
    gkr,
    ub,
    ut,
    ts,
    tg,
    pb,
    sb,
    att,
    wsum,
    rp,
    rmask,
):
    scaling = 1.0 / math.sqrt(HEAD_DIM)
    row = at_ref[0]
    col = at_ref[1]
    lefts = (left0, left1)
    rights = (right0, right1, right2, right3)
    slots = [left_place(col, row ^ t) for t in range(16)]

    lane = lax.broadcasted_iota(jnp.int32, (16, 128), 1) // 16
    half0 = jnp.zeros((16, 128), F32)
    half1 = jnp.zeros((16, 128), F32)
    for t in range(16):
        slot = slots[t]
        block = rights[t // 4]
        for j in range(16):
            xr[j, slot] = block[t % 4, 16 * j : 16 * j + 16, :]
        came = block[t % 4, 256:272, :].astype(F32)
        half0 = jnp.where(lane == slot, came, half0)
        half1 = jnp.where(lane + 8 == slot, came, half1)
    right_allowed = jnp.concatenate([half0, half1], axis=1)
    spread4 = (
        lax.broadcasted_iota(jnp.int32, (64, 16), 0) // 4
        == lax.broadcasted_iota(jnp.int32, (64, 16), 1)
    ).astype(BF)
    rmask[...] = nn(spread4, right_allowed.astype(BF))
    halves = []
    for half in range(2):
        total = jnp.zeros((16, 128), F32)
        for s in range(8):
            total = jnp.where(lane == s, lefts[half][s, 128:144, :].astype(F32), total)
        halves.append(total)
    left_allowed = jnp.concatenate(halves, axis=1)

    wl = wl_ref[...]
    wr = wr_ref[...]
    for i in range(8):
        for s in range(16):
            xl[i, s] = lefts[s // 8][s % 8, 16 * i : 16 * i + 16, :]

    def project_left(i, _):
        ql[i] = nt(wl, xl[i].reshape(256, 128)).astype(BF).astype(F32)
        return 0

    lax.fori_loop(0, 8, project_left, 0)

    def project_right(j, _):
        kr[j] = nt(wr, xr[j].reshape(256, 128)).astype(BF).astype(F32)
        return 0

    lax.fori_loop(0, 16, project_right, 0)
    cot = cot_ref[...]
    ut[...] = nt(wo_ref[...], cot).astype(BF).astype(F32)

    def spread_upstream(t, _):
        rows = pl.ds(pl.multiple_of(t * 8, 8), 8)
        tile = ut[rows, :]
        for ij in range(128):
            ub[ij, rows, :] = jnp.broadcast_to(tile[:, ij : ij + 1], (8, 128))
        return 0

    lax.fori_loop(0, 16, spread_upstream, 0)

    fold8 = (
        lax.broadcasted_iota(jnp.int32, (64, 512), 1) // 8
        == lax.broadcasted_iota(jnp.int32, (64, 512), 0)
    ).astype(BF)
    spread8 = (
        lax.broadcasted_iota(jnp.int32, (512, 64), 0) // 8
        == lax.broadcasted_iota(jnp.int32, (512, 64), 1)
    ).astype(BF)

    for i2 in range(4):
        pair = (2 * i2, 2 * i2 + 1)

        def score_head(h, _, pair=pair):
            tiles = [pl.ds(pl.multiple_of(h * 32 + 8 * e, 8), 8) for e in range(4)]
            lower = [pl.ds(pl.multiple_of(128 + h * 32 + 8 * e, 8), 8) for e in range(4)]
            q = [[ql[i, r, :] for r in tiles] for i in pair]
            v = [[ql[i, r, :] for r in lower] for i in pair]
            for j in range(16):
                k = [kr[j, r, :] for r in tiles]
                w = [kr[j, r, :] for r in lower]
                out = pl.ds(pl.multiple_of((j * 4 + h) * 8, 8), 8)
                for n in range(2):
                    u = [ub[pair[n] * 16 + j, r, :] for r in tiles]
                    u = [jnp.concatenate([x, x], axis=1) for x in u]
                    ts[n, out, :] = (q[n][0] * k[0] + q[n][1] * k[1]) + (
                        q[n][2] * k[2] + q[n][3] * k[3]
                    )
                    tg[n, out, :] = (u[0] * (v[n][0] * w[0]) + u[1] * (v[n][1] * w[1])) + (
                        u[2] * (v[n][2] * w[2]) + u[3] * (v[n][3] * w[3])
                    )
            return 0

        lax.fori_loop(0, 4, score_head, 0)
        for n in range(2):
            i = pair[n]
            part = ts[n]
            high = part.astype(BF)
            low = (part - high.astype(F32)).astype(BF)
            score = (nn(fold8, high) + nn(fold8, low)) * scaling
            grad = nn(fold8, tg[n].astype(BF))
            allowed = rmask[...] * left_allowed[i : i + 1, :] > 0.5
            score = jnp.where(allowed, score, -1000000000.0)
            top = jnp.max(score, axis=1, keepdims=True)
            raw = jnp.exp(score - top)
            prob = raw / jnp.sum(raw, axis=1, keepdims=True)
            mean = jnp.sum(prob * grad, axis=1, keepdims=True)
            grad = prob * (grad - mean) * scaling
            pb[i] = nn(spread8, prob.astype(BF))
            sb[i] = nn(spread8, grad.astype(BF))

    column = lax.broadcasted_iota(jnp.int32, (8, 128), 1)

    def gradients(t, _):
        h = t // 4
        rows = pl.ds(pl.multiple_of(t * 8, 8), 8)
        lower = pl.ds(pl.multiple_of(128 + t * 8, 8), 8)
        seen = jnp.zeros((8, 128), F32)
        for ib in range(2):
            group = range(4 * ib, 4 * ib + 4)
            q = [ql[i, rows, :] for i in group]
            v = [ql[i, lower, :] for i in group]
            gq = [jnp.zeros((8, 256), F32) for _ in group]
            gl = [jnp.zeros((8, 256), F32) for _ in group]
            for j in range(16):
                k = kr[j, rows, :]
                w = kr[j, lower, :]
                at = pl.ds(pl.multiple_of((j * 4 + h) * 8, 8), 8)
                if ib == 0:
                    gk = jnp.zeros((8, 256), F32)
                    gr = jnp.zeros((8, 256), F32)
                else:
                    gk = gkr[j, rows, :]
                    gr = gkr[j, lower, :]
                for n, i in enumerate(group):
                    p = pb[i, at, :]
                    s = sb[i, at, :]
                    u = ub[i * 16 + j, rows, :]
                    pu = p * jnp.concatenate([u, u], axis=1)
                    gl[n] = gl[n] + pu * w
                    gr = gr + pu * v[n]
                    gq[n] = gq[n] + s * k
                    gk = gk + s * q[n]
                    a = p * (v[n] * w)
                    a = jnp.sum(a[:, :128] + a[:, 128:], axis=1, keepdims=True)
                    seen = jnp.where(column == i * 16 + j, a, seen)
                gkr[j, rows, :] = gk
                gkr[j, lower, :] = gr
            for n, i in enumerate(group):
                gql[i, rows, :] = gq[n]
                gql[i, lower, :] = gl[n]
        att[rows, :] = seen
        return 0

    lax.fori_loop(0, 16, gradients, 0)

    wsum[...] = jnp.zeros((512, 128), F32)

    def finish_left(i, _):
        g = gql[i].astype(BF)
        wsum[:256, :] += nn(g, xl[i].reshape(256, 128))
        part = tn(g, wl).astype(BF).reshape(16, 16, 128)
        rows = pl.ds(pl.multiple_of(i * 16, 16), 16)
        for s in range(16):
            lout[s, rows, :] = part[s]
        return 0

    lax.fori_loop(0, 8, finish_left, 0)

    def finish_right(j, _):
        g = gkr[j].astype(BF)
        wsum[256:, :] += nn(g, xr[j].reshape(256, 128))
        rp[...] = tn(g, wr).astype(BF).reshape(16, 16, 128)
        rows = pl.ds(pl.multiple_of(j * 16, 16), 16)
        for t in range(16):
            rout[t, rows, :] = rp[slots[t]]
        return 0

    lax.fori_loop(0, 16, finish_right, 0)
    wout[0:128, :] = wsum[0:128, :].T.astype(BF)
    wout[128:256, :] = wsum[256:384, :].T.astype(BF)
    wout[256:384, :] = wsum[128:256, :].T.astype(BF)
    wout[384:512, :] = wsum[384:512, :].T.astype(BF)
    wout[512:640, :] = nn(att[...].astype(BF), cot).astype(BF)


def triples(at, lefts, rights, cot, wl, wr, wo):
    vmem = pl.BlockSpec(memory_space=pltpu.VMEM)
    return pl.pallas_call(
        triple_kernel,
        out_shape=(
            jax.ShapeDtypeStruct((16, 128, 128), BF),
            jax.ShapeDtypeStruct((16, 256, 128), BF),
            jax.ShapeDtypeStruct((640, 128), BF),
        ),
        in_specs=[pl.BlockSpec(memory_space=pltpu.SMEM)] + [vmem] * 10,
        out_specs=(vmem, vmem, vmem),
        scratch_shapes=[
            pltpu.VMEM((8, 16, 16, 128), BF),
            pltpu.VMEM((16, 16, 16, 128), BF),
            pltpu.VMEM((8, 256, 256), F32),
            pltpu.VMEM((16, 256, 256), F32),
            pltpu.VMEM((8, 256, 256), F32),
            pltpu.VMEM((16, 256, 256), F32),
            pltpu.VMEM((128, 128, 128), F32),
            pltpu.VMEM((128, 128), F32),
            pltpu.VMEM((2, 512, 256), F32),
            pltpu.VMEM((2, 512, 256), F32),
            pltpu.VMEM((8, 512, 256), F32),
            pltpu.VMEM((8, 512, 256), F32),
            pltpu.VMEM((128, 128), F32),
            pltpu.VMEM((512, 128), F32),
            pltpu.VMEM((16, 16, 128), BF),
            pltpu.VMEM((64, 256), F32),
        ],
        compiler_params=pltpu.CompilerParams(vmem_limit_bytes=48 * 1024 * 1024),
        cost_estimate=pl.CostEstimate(
            flops=800_000_000, bytes_accessed=5_000_000, transcendentals=131072
        ),
    )(at, *lefts, *rights, cot, wl, wr, wo)


def body(
    left_edges,
    right_edges,
    left_mask,
    right_mask,
    cotangent,
    query_weight,
    key_weight,
    left_weight,
    right_weight,
    out_weight,
):
    width = left_edges.shape[2]
    row = lax.axis_index("row")
    col = lax.axis_index("col")
    left_rows = jnp.concatenate(
        [
            left_edges.reshape(-1, width),
            jnp.pad(jnp.tile(left_mask.astype(BF), (1, 8)), ((0, 8), (0, 0))),
        ]
    )
    right_rows = jnp.concatenate(
        [
            jnp.swapaxes(right_edges, 0, 1).reshape(-1, width),
            jnp.tile(right_mask.T.astype(BF), (1, 8)),
        ]
    )
    lefts = gather_col(left_rows)
    rights = gather_row(right_rows)
    left_part, right_part, weight_part = triples(
        jnp.stack([row, col]).astype(jnp.int32),
        lefts,
        rights,
        cotangent.reshape(-1, width),
        jnp.concatenate([query_weight.T, left_weight.T]),
        jnp.concatenate([key_weight.T, right_weight.T]),
        out_weight,
    )

    chunks = right_part.reshape(4, 1024, width)
    total = add_up(chunks[0], [lax.ppermute(chunks[k], "row", flip(4 * k)) for k in (1, 2, 3)])
    chunks = total.astype(BF).reshape(4, 256, width)
    right_grad = add_up(
        total[:256], [lax.ppermute(chunks[k], "row", flip(k)) for k in (1, 2, 3)]
    )
    right_grad = jnp.swapaxes(right_grad.reshape(16, 16, width), 0, 1)

    core = col & 1
    halves = weight_part.reshape(2, 320, width)
    mine = lax.dynamic_index_in_dim(halves, core, 0, keepdims=False)
    other = lax.dynamic_index_in_dim(halves, 1 - core, 0, keepdims=False)
    sent = jnp.concatenate([left_part[8:].reshape(1024, width), other])
    kept = jnp.concatenate([left_part[:8].reshape(1024, width), mine])
    total = add_up(kept, [lax.ppermute(sent, "col", flip(1))])
    low = total.astype(BF)
    came = [
        lax.ppermute(
            jnp.concatenate([low[256 * k : 256 * k + 256], low[1024:]]), "col", flip(4 * k)
        ).astype(F32)
        for k in (1, 2, 3)
    ]
    kept = jnp.concatenate([total[:256], low[1024:].astype(F32)])
    total = (kept + came[0]) + (came[1] + came[2])
    low = total[128:].astype(BF)
    came = lax.ppermute(low, "col", flip(2)).astype(F32)
    left_grad = total[:128] + came[:128]
    weights = low[128:].astype(F32) + came[128:]
    weights = meet(weights.astype(BF), "row", (4, 8, 12))
    weights = meet(weights.astype(BF), "row", (1, 2, 3))
    mine = weights.astype(BF)
    other = lax.ppermute(mine, "col", flip(1))
    first = jnp.where(core == 0, mine, other)
    second = jnp.where(core == 0, other, mine)
    weights = jnp.concatenate([first, second]).astype(F32)
    proj_grads = weights[:512].reshape(4, 128, width)
    return (left_grad.reshape(left_edges.shape), right_grad, proj_grads, weights[512:])


def solution(mesh):
    return jax.shard_map(
        body,
        mesh=mesh,
        in_specs=(
            P("row", "col", None),
            P("row", "col", None),
            P("row", "col"),
            P("row", "col"),
            P("row", "col", None),
            P(),
            P(),
            P(),
            P(),
            P(),
        ),
        out_specs=(P("row", "col", None), P("row", "col", None), P(), P()),
        check_vma=False,
    )
```

profile of v0, /device:TPU:1, one launch (start us, length us, event | category | flops | bytes accessed | tf_op | source)
XLA Modules:
  0.0 132.1 jit_solution(18062353232429630372)
XLA Ops:
  0.6 0.9 copy.20
  1.5 0.1 copy.21
  1.6 0.1 tile.21
  1.7 0.0 copy-start.2
  1.8 3.9 %collective-permute-start.6 = (bf16[272,128]{1,0:T(8,128)(2,1)S(1)}, bf16[272,128]{1,0:T(8,128)(2,1)S(1)}, u32[]{:S(2)}, u32[]{:S(2)}) collective-permute-start(bf16[272,128]{1,0:T(8,128)(2,1)S(1)} %get-tuple-element.40), channel_id=1, source_target_pairs={{0,32},{16,48},{32,0},{48,16},{64,96},{80,112},{96,64},{112,80},{1... | collective-permute-start | bytes 208904 | tf_op jit(solution)/shard_map/ppermute | solution.py:27
  5.7 1.5 %collective-permute-start.7 = (bf16[272,128]{1,0:T(8,128)(2,1)S(1)}, bf16[272,128]{1,0:T(8,128)(2,1)S(1)}, u32[]{:S(2)}, u32[]{:S(2)}) collective-permute-start(bf16[272,128]{1,0:T(8,128)(2,1)S(1)} %get-tuple-element.40), channel_id=1, source_target_pairs={{0,48},{16,32},{32,16},{48,0},{64,112},{80,96},{96,80},{112,64},{1... | collective-permute-start | bytes 208904 | tf_op jit(solution)/shard_map/ppermute | solution.py:27
  7.1 0.2 collective-permute-start.5
  7.3 0.1 tile.9
  7.4 5.2 %collective-permute-start = (bf16[144,128]{1,0:T(8,128)(2,1)S(1)}, bf16[144,128]{1,0:T(8,128)(2,1)S(1)}, u32[]{:S(2)}, u32[]{:S(2)}) collective-permute-start(bf16[144,128]{1,0:T(8,128)(2,1)S(1)} %get-tuple-element.42), channel_id=1, source_target_pairs={{0,2},{1,3},{2,0},{3,1},{4,6},{5,7},{6,4},{7,5},{8,10},{9,11},{10,... | collective-permute-start | bytes 110600 | tf_op jit(solution)/shard_map/ppermute | solution.py:21
  12.6 3.6 %collective-permute-done = bf16[144,128]{1,0:T(8,128)(2,1)S(1)} collective-permute-done((bf16[144,128]{1,0:T(8,128)(2,1)S(1)}, bf16[144,128]{1,0:T(8,128)(2,1)S(1)}, u32[]{:S(2)}, u32[]{:S(2)}) %collective-permute-start) | collective-permute-done | bytes 36896 | tf_op jit(solution)/shard_map/ppermute | solution.py:21
  16.3 1.4 %collective-permute-start.1 = (bf16[2,144,128]{2,1,0:T(8,128)(2,1)S(1)}, bf16[2,144,128]{2,1,0:T(8,128)(2,1)S(1)}, u32[]{:S(2)}, u32[]{:S(2)}) collective-permute-start(bf16[2,144,128]{2,1,0:T(8,128)(2,1)S(1)} %pad_maximum_fusion.4), channel_id=1, source_target_pairs={{0,4},{1,5},{2,6},{3,7},{4,0},{5,1},{6,2},{7,3},{8,12},{9,13},{10,... | collective-permute-start | bytes 221192 | tf_op jit(solution)/shard_map/ppermute | solution.py:22
  17.7 2.6 %collective-permute-start.2 = (bf16[2,144,128]{2,1,0:T(8,128)(2,1)S(1)}, bf16[2,144,128]{2,1,0:T(8,128)(2,1)S(1)}, u32[]{:S(2)}, u32[]{:S(2)}) collective-permute-start(bf16[2,144,128]{2,1,0:T(8,128)(2,1)S(1)} %pad_maximum_fusion.4), channel_id=1, source_target_pairs={{0,8},{1,9},{2,10},{3,11},{4,12},{5,13},{6,14},{7,15},{8,0},{9,1},... | collective-permute-start | bytes 221192 | tf_op jit(solution)/shard_map/ppermute | solution.py:22
  20.3 2.0 %collective-permute-start.3 = (bf16[2,144,128]{2,1,0:T(8,128)(2,1)S(1)}, bf16[2,144,128]{2,1,0:T(8,128)(2,1)S(1)}, u32[]{:S(2)}, u32[]{:S(2)}) collective-permute-start(bf16[2,144,128]{2,1,0:T(8,128)(2,1)S(1)} %pad_maximum_fusion.4), channel_id=1, source_target_pairs={{0,12},{1,13},{2,14},{3,15},{4,8},{5,9},{6,10},{7,11},{8,4},{9,5},... | collective-permute-start | bytes 221192 | tf_op jit(solution)/shard_map/ppermute | solution.py:22
  22.3 0.5 collective-permute-done.2
  22.8 2.8 %collective-permute-done.3 = bf16[2,144,128]{2,1,0:T(8,128)(2,1)S(1)} collective-permute-done((bf16[2,144,128]{2,1,0:T(8,128)(2,1)S(1)}, bf16[2,144,128]{2,1,0:T(8,128)(2,1)S(1)}, u32[]{:S(2)}, u32[]{:S(2)}) %collective-permute-start.3) | collective-permute-done | bytes 73760 | tf_op jit(solution)/shard_map/ppermute | solution.py:22
  25.6 3.4 %collective-permute-start.4 = (bf16[8,144,128]{2,1,0:T(8,128)(2,1)S(1)}, bf16[8,144,128]{2,1,0:T(8,128)(2,1)S(1)}, u32[]{:S(2)}, u32[]{:S(2)}) collective-permute-start(bf16[8,144,128]{2,1,0:T(8,128)(2,1)S(1)} %constant_dynamic-update-slice_fusion.left0), channel_id=1, source_target_pairs={{0,1},{1,0},{2,3},{3,2},{4,5},{5,4},{6,7},{7,6},{8,9},{9,8},{10,11... | collective-permute-start | bytes 884744 | tf_op jit(solution)/shard_map/ppermute | solution.py:23
  29.1 2.6 %collective-permute-start.10 = (bf16[4,272,128]{2,1,0:T(8,128)(2,1)S(1)}, bf16[4,272,128]{2,1,0:T(8,128)(2,1)S(1)}, u32[]{:S(2)}, u32[]{:S(2)}) collective-permute-start(bf16[4,272,128]{2,1,0:T(8,128)(2,1)S(1)} %pad_maximum_fusion.1.right0), channel_id=1, source_target_pairs={{0,192},{16,208},{32,224},{48,240},{64,128},{80,144},{96,160},{112... | collective-permute-start | bytes 835592 | tf_op jit(solution)/shard_map/ppermute | solution.py:28
  31.7 1.4 %collective-permute-start.9 = (bf16[4,272,128]{2,1,0:T(8,128)(2,1)S(1)}, bf16[4,272,128]{2,1,0:T(8,128)(2,1)S(1)}, u32[]{:S(2)}, u32[]{:S(2)}) collective-permute-start(bf16[4,272,128]{2,1,0:T(8,128)(2,1)S(1)} %pad_maximum_fusion.1.right0), channel_id=1, source_target_pairs={{0,128},{16,144},{32,160},{48,176},{64,192},{80,208},{96,224},{112... | collective-permute-start | bytes 835592 | tf_op jit(solution)/shard_map/ppermute | solution.py:28
  33.0 0.1 copy.22
  33.2 0.6 copy-done.4
  33.8 0.1 copy.23
  33.9 0.6 copy-done.5
  34.6 0.1 copy.24
  34.7 0.6 copy-done.6
  35.3 0.1 copy.25
  35.4 0.1 pad_add_fusion.at_ref
  35.5 3.1 %collective-permute-done.10.right3 = bf16[4,272,128]{2,1,0:T(8,128)(2,1)S(1)} collective-permute-done((bf16[4,272,128]{2,1,0:T(8,128)(2,1)S(1)}, bf16[4,272,128]{2,1,0:T(8,128)(2,1)S(1)}, u32[]{:S(2)}, u32[]{:S(2)}) %collective-permute-start.10) | collective-permute-done | bytes 278560 | tf_op jit(solution)/shard_map/ppermute | solution.py:28
  38.6 0.9 collective-permute-done.8.right1
  39.6 5.9 %collective-permute-done.9.right2 = bf16[4,272,128]{2,1,0:T(8,128)(2,1)S(1)} collective-permute-done((bf16[4,272,128]{2,1,0:T(8,128)(2,1)S(1)}, bf16[4,272,128]{2,1,0:T(8,128)(2,1)S(1)}, u32[]{:S(2)}, u32[]{:S(2)}) %collective-permute-start.9) | collective-permute-done | bytes 278560 | tf_op jit(solution)/shard_map/ppermute | solution.py:28
  45.5 36.2 %shard_map.129 = (bf16[16,128,128]{2,1,0:T(8,128)(2,1)S(1)}, bf16[16,256,128]{2,1,0:T(8,128)(2,1)S(1)}, bf16[640,128]{1,0:T(8,128)(2,1)S(1)}) custom-call(s32[2]{0:T(128)S(1)} %pad_add_fusion.at_ref, bf16[8,144,128]{2,1,0:T(8,128)(2,1)S(1)} %constant_dynamic-update-slice_fusion.left0, bf16[8,144,128]{2,1,0:T(8,128)(2,1)S(1)} %collective-permute-done.4.left1, ...), custom_call_target="tpu_custom_call" | custom-call | flops 800000000 | bytes 5000000 | tf_op jit(solution)/shard_map/pallas_call | solution.py:280
  81.8 1.2 collective-permute-start.11
  83.0 1.3 collective-permute-done.11
  84.3 0.1 convert_add_fusion
  84.5 0.1 collective-permute-start.12
  84.6 3.2 %collective-permute-start.13 = (bf16[576,128]{1,0:T(8,128)(2,1)S(1)}, bf16[576,128]{1,0:T(8,128)(2,1)S(1)}, u32[]{:S(2)}, u32[]{:S(2)}) collective-permute-start(bf16[576,128]{1,0:T(8,128)(2,1)S(1)} %get-tuple-element.38), channel_id=1, source_target_pairs={{0,8},{1,9},{2,10},{3,11},{4,12},{5,13},{6,14},{7,15},{8,0},{9,1},... | collective-permute-start | bytes 442376 | tf_op jit(solution)/shard_map/ppermute | solution.py:370
  87.8 0.6 collective-permute-start.14
  88.4 0.1 fusion.15
  88.5 0.1 collective-permute-start.16
  88.6 3.7 %collective-permute-start.17 = (bf16[1024,128]{1,0:T(8,128)(2,1)S(1)}, bf16[1024,128]{1,0:T(8,128)(2,1)S(1)}, u32[]{:S(2)}, u32[]{:S(2)}) collective-permute-start(bf16[1024,128]{1,0:T(8,128)(2,1)S(1)} %bitcast.49), channel_id=1, source_target_pairs={{0,128},{16,144},{32,160},{48,176},{64,192},{80,208},{96,224},{112... | collective-permute-start | bytes 786440 | tf_op jit(solution)/shard_map/ppermute | solution.py:354
  92.3 0.1 collective-permute-start.18
  92.5 2.1 %collective-permute-done.13 = bf16[576,128]{1,0:T(8,128)(2,1)S(1)} collective-permute-done((bf16[576,128]{1,0:T(8,128)(2,1)S(1)}, bf16[576,128]{1,0:T(8,128)(2,1)S(1)}, u32[]{:S(2)}, u32[]{:S(2)}) %collective-permute-start.13) | collective-permute-done | bytes 147488 | tf_op jit(solution)/shard_map/ppermute | solution.py:370
  94.6 2.5 %collective-permute-done.14 = bf16[576,128]{1,0:T(8,128)(2,1)S(1)} collective-permute-done((bf16[576,128]{1,0:T(8,128)(2,1)S(1)}, bf16[576,128]{1,0:T(8,128)(2,1)S(1)}, u32[]{:S(2)}, u32[]{:S(2)}) %collective-permute-start.14) | collective-permute-done | bytes 147488 | tf_op jit(solution)/shard_map/ppermute | solution.py:370
  97.1 0.1 fusion.13
  97.2 3.8 %collective-permute-start.15 = (bf16[448,128]{1,0:T(8,128)(2,1)S(1)}, bf16[448,128]{1,0:T(8,128)(2,1)S(1)}, u32[]{:S(2)}, u32[]{:S(2)}) collective-permute-start(bf16[448,128]{1,0:T(8,128)(2,1)S(1)} %slice.103), channel_id=1, source_target_pairs={{0,2},{1,3},{2,0},{3,1},{4,6},{5,7},{6,4},{7,5},{8,10},{9,11},{10,... | collective-permute-start | bytes 344072 | tf_op jit(solution)/shard_map/ppermute | solution.py:378
  101.0 2.1 %collective-permute-done.17 = bf16[1024,128]{1,0:T(8,128)(2,1)S(1)} collective-permute-done((bf16[1024,128]{1,0:T(8,128)(2,1)S(1)}, bf16[1024,128]{1,0:T(8,128)(2,1)S(1)}, u32[]{:S(2)}, u32[]{:S(2)}) %collective-permute-start.17) | collective-permute-done | bytes 262176 | tf_op jit(solution)/shard_map/ppermute | solution.py:354
  103.1 2.6 %collective-permute-done.18 = bf16[1024,128]{1,0:T(8,128)(2,1)S(1)} collective-permute-done((bf16[1024,128]{1,0:T(8,128)(2,1)S(1)}, bf16[1024,128]{1,0:T(8,128)(2,1)S(1)}, u32[]{:S(2)}, u32[]{:S(2)}) %collective-permute-start.18) | collective-permute-done | bytes 262176 | tf_op jit(solution)/shard_map/ppermute | solution.py:354
  105.7 0.2 fusion.11
  105.9 0.1 collective-permute-start.22
  106.0 2.6 %collective-permute-start.23 = (bf16[320,128]{1,0:T(8,128)(2,1)S(1)}, bf16[320,128]{1,0:T(8,128)(2,1)S(1)}, u32[]{:S(2)}, u32[]{:S(2)}) collective-permute-start(bf16[320,128]{1,0:T(8,128)(2,1)S(1)} %fusion.3), channel_id=1, source_target_pairs={{0,128},{16,144},{32,160},{48,176},{64,192},{80,208},{96,224},{112... | collective-permute-start | bytes 245768 | tf_op jit(solution)/shard_map/ppermute | solution.py:44
  108.6 1.3 collective-permute-start.24
  109.9 4.2 %collective-permute-start.19 = (bf16[256,128]{1,0:T(8,128)(2,1)S(1)}, bf16[256,128]{1,0:T(8,128)(2,1)S(1)}, u32[]{:S(2)}, u32[]{:S(2)}) collective-permute-start(bf16[256,128]{1,0:T(8,128)(2,1)S(1)} %get-tuple-element.30), channel_id=1, source_target_pairs={{0,16},{16,0},{32,48},{48,32},{64,80},{80,64},{96,112},{112,96},{1... | collective-permute-start | bytes 196616 | tf_op jit(solution)/shard_map/ppermute | solution.py:357
  114.1 0.5 collective-permute-start.20
  114.6 1.6 %collective-permute-start.21 = (bf16[256,128]{1,0:T(8,128)(2,1)S(1)}, bf16[256,128]{1,0:T(8,128)(2,1)S(1)}, u32[]{:S(2)}, u32[]{:S(2)}) collective-permute-start(bf16[256,128]{1,0:T(8,128)(2,1)S(1)} %get-tuple-element.31), channel_id=1, source_target_pairs={{0,48},{16,32},{32,16},{48,0},{64,112},{80,96},{96,80},{112,64},{1... | collective-permute-start | bytes 196616 | tf_op jit(solution)/shard_map/ppermute | solution.py:357
  116.3 2.8 %collective-permute-start.25 = (bf16[320,128]{1,0:T(8,128)(2,1)S(1)}, bf16[320,128]{1,0:T(8,128)(2,1)S(1)}, u32[]{:S(2)}, u32[]{:S(2)}) collective-permute-start(bf16[320,128]{1,0:T(8,128)(2,1)S(1)} %add_convert_fusion.1), channel_id=1, source_target_pairs={{0,16},{16,0},{32,48},{48,32},{64,80},{80,64},{96,112},{112,96},{1... | collective-permute-start | bytes 245768 | tf_op jit(solution)/shard_map/ppermute | solution.py:44
  119.2 0.6 collective-permute-start.26
  119.7 1.6 %collective-permute-start.27 = (bf16[320,128]{1,0:T(8,128)(2,1)S(1)}, bf16[320,128]{1,0:T(8,128)(2,1)S(1)}, u32[]{:S(2)}, u32[]{:S(2)}) collective-permute-start(bf16[320,128]{1,0:T(8,128)(2,1)S(1)} %add_convert_fusion.1), channel_id=1, source_target_pairs={{0,48},{16,32},{32,16},{48,0},{64,112},{80,96},{96,80},{112,64},{1... | collective-permute-start | bytes 245768 | tf_op jit(solution)/shard_map/ppermute | solution.py:44
  121.4 0.7 copy.26
  122.1 0.5 collective-permute-done.25
  122.6 5.3 %collective-permute-done.26 = bf16[320,128]{1,0:T(8,128)(2,1)S(1)} collective-permute-done((bf16[320,128]{1,0:T(8,128)(2,1)S(1)}, bf16[320,128]{1,0:T(8,128)(2,1)S(1)}, u32[]{:S(2)}, u32[]{:S(2)}) %collective-permute-start.26) | collective-permute-done | bytes 81952 | tf_op jit(solution)/shard_map/ppermute | solution.py:44
  128.0 1.7 %collective-permute-start.28 = (bf16[320,128]{1,0:T(8,128)(2,1)S(1)}, bf16[320,128]{1,0:T(8,128)(2,1)S(1)}, u32[]{:S(2)}, u32[]{:S(2)}) collective-permute-start(bf16[320,128]{1,0:T(8,128)(2,1)S(1)} %add_convert_fusion), channel_id=1, source_target_pairs={{0,1},{1,0},{2,3},{3,2},{4,5},{5,4},{6,7},{7,6},{8,9},{9,8},{10,11... | collective-permute-start | bytes 245768 | tf_op jit(solution)/shard_map/ppermute | solution.py:384
  129.7 0.6 slice_add_fusion.2
  130.4 0.3 collective-permute-done.28
  130.7 0.6 maximum_convert_fusion.1
  131.3 0.7 slice.111
  (61 shorter events, 0.6 us)
Async XLA Ops:
  0.6 0.9 copy-start.7
  1.7 5.6 %copy-start.8 = (s32[8,16]{1,0:T(8,128)S(1)}, s32[8,16]{1,0:T(8,128)}, u32[]{:S(2)}) copy-start(s32[8,16]{1,0:T(8,128)} %param.12) | copy-start | bytes 1540
  1.7 5.7 %copy-start.2 = (bf16[8,16,128]{2,1,0:T(8,128)(2,1)S(1)}, bf16[8,16,128]{2,1,0:T(8,128)(2,1)}, u32[]{:S(2)}) copy-start(bf16[8,16,128]{2,1,0:T(8,128)(2,1)} %param.10) | copy-start | bytes 98308
  1.8 27.3 %collective-permute-start.6 = (bf16[272,128]{1,0:T(8,128)(2,1)S(1)}, bf16[272,128]{1,0:T(8,128)(2,1)S(1)}, u32[]{:S(2)}, u32[]{:S(2)}) collective-permute-start(bf16[272,128]{1,0:T(8,128)(2,1)S(1)} %get-tuple-element.40), channel_id=1, source_target_pairs={{0,32},{16,48},{32,0},{48,16},{64,96},{80,112},{96,64},{112,80},{1... | collective-permute-start | bytes 208904 | tf_op jit(solution)/shard_map/ppermute | solution.py:27
  5.7 23.4 %collective-permute-start.7 = (bf16[272,128]{1,0:T(8,128)(2,1)S(1)}, bf16[272,128]{1,0:T(8,128)(2,1)S(1)}, u32[]{:S(2)}, u32[]{:S(2)}) collective-permute-start(bf16[272,128]{1,0:T(8,128)(2,1)S(1)} %get-tuple-element.40), channel_id=1, source_target_pairs={{0,48},{16,32},{32,16},{48,0},{64,112},{80,96},{96,80},{112,64},{1... | collective-permute-start | bytes 208904 | tf_op jit(solution)/shard_map/ppermute | solution.py:27
  7.1 21.9 %collective-permute-start.5 = (bf16[272,128]{1,0:T(8,128)(2,1)S(1)}, bf16[272,128]{1,0:T(8,128)(2,1)S(1)}, u32[]{:S(2)}, u32[]{:S(2)}) collective-permute-start(bf16[272,128]{1,0:T(8,128)(2,1)S(1)} %get-tuple-element.40), channel_id=1, source_target_pairs={{0,16},{16,0},{32,48},{48,32},{64,80},{80,64},{96,112},{112,96},{1... | collective-permute-start | bytes 208904 | tf_op jit(solution)/shard_map/ppermute | solution.py:27
  7.4 8.8 %collective-permute-start = (bf16[144,128]{1,0:T(8,128)(2,1)S(1)}, bf16[144,128]{1,0:T(8,128)(2,1)S(1)}, u32[]{:S(2)}, u32[]{:S(2)}) collective-permute-start(bf16[144,128]{1,0:T(8,128)(2,1)S(1)} %get-tuple-element.42), channel_id=1, source_target_pairs={{0,2},{1,3},{2,0},{3,1},{4,6},{5,7},{6,4},{7,5},{8,10},{9,11},{10,... | collective-permute-start | bytes 110600 | tf_op jit(solution)/shard_map/ppermute | solution.py:21
  16.3 4.0 %collective-permute-start.1 = (bf16[2,144,128]{2,1,0:T(8,128)(2,1)S(1)}, bf16[2,144,128]{2,1,0:T(8,128)(2,1)S(1)}, u32[]{:S(2)}, u32[]{:S(2)}) collective-permute-start(bf16[2,144,128]{2,1,0:T(8,128)(2,1)S(1)} %pad_maximum_fusion.4), channel_id=1, source_target_pairs={{0,4},{1,5},{2,6},{3,7},{4,0},{5,1},{6,2},{7,3},{8,12},{9,13},{10,... | collective-permute-start | bytes 221192 | tf_op jit(solution)/shard_map/ppermute | solution.py:22
  17.7 5.1 %collective-permute-start.2 = (bf16[2,144,128]{2,1,0:T(8,128)(2,1)S(1)}, bf16[2,144,128]{2,1,0:T(8,128)(2,1)S(1)}, u32[]{:S(2)}, u32[]{:S(2)}) collective-permute-start(bf16[2,144,128]{2,1,0:T(8,128)(2,1)S(1)} %pad_maximum_fusion.4), channel_id=1, source_target_pairs={{0,8},{1,9},{2,10},{3,11},{4,12},{5,13},{6,14},{7,15},{8,0},{9,1},... | collective-permute-start | bytes 221192 | tf_op jit(solution)/shard_map/ppermute | solution.py:22
  20.3 5.3 %collective-permute-start.3 = (bf16[2,144,128]{2,1,0:T(8,128)(2,1)S(1)}, bf16[2,144,128]{2,1,0:T(8,128)(2,1)S(1)}, u32[]{:S(2)}, u32[]{:S(2)}) collective-permute-start(bf16[2,144,128]{2,1,0:T(8,128)(2,1)S(1)} %pad_maximum_fusion.4), channel_id=1, source_target_pairs={{0,12},{1,13},{2,14},{3,15},{4,8},{5,9},{6,10},{7,11},{8,4},{9,5},... | collective-permute-start | bytes 221192 | tf_op jit(solution)/shard_map/ppermute | solution.py:22
  25.6 19.9 %collective-permute-start.4 = (bf16[8,144,128]{2,1,0:T(8,128)(2,1)S(1)}, bf16[8,144,128]{2,1,0:T(8,128)(2,1)S(1)}, u32[]{:S(2)}, u32[]{:S(2)}) collective-permute-start(bf16[8,144,128]{2,1,0:T(8,128)(2,1)S(1)} %constant_dynamic-update-slice_fusion.left0), channel_id=1, source_target_pairs={{0,1},{1,0},{2,3},{3,2},{4,5},{5,4},{6,7},{7,6},{8,9},{9,8},{10,11... | collective-permute-start | bytes 884744 | tf_op jit(solution)/shard_map/ppermute | solution.py:23
  29.0 4.0 %copy-start.3 = (bf16[128,128]{1,0:T(8,128)(2,1)S(1)}, bf16[128,128]{1,0:T(8,128)(2,1)}, u32[]{:S(2)}) copy-start(bf16[128,128]{1,0:T(8,128)(2,1)} %param.15) | copy-start | bytes 98308
  29.1 9.6 %collective-permute-start.10 = (bf16[4,272,128]{2,1,0:T(8,128)(2,1)S(1)}, bf16[4,272,128]{2,1,0:T(8,128)(2,1)S(1)}, u32[]{:S(2)}, u32[]{:S(2)}) collective-permute-start(bf16[4,272,128]{2,1,0:T(8,128)(2,1)S(1)} %pad_maximum_fusion.1.right0), channel_id=1, source_target_pairs={{0,192},{16,208},{32,224},{48,240},{64,128},{80,144},{96,160},{112... | collective-permute-start | bytes 835592 | tf_op jit(solution)/shard_map/ppermute | solution.py:28
  31.7 7.9 %collective-permute-start.8 = (bf16[4,272,128]{2,1,0:T(8,128)(2,1)S(1)}, bf16[4,272,128]{2,1,0:T(8,128)(2,1)S(1)}, u32[]{:S(2)}, u32[]{:S(2)}) collective-permute-start(bf16[4,272,128]{2,1,0:T(8,128)(2,1)S(1)} %pad_maximum_fusion.1.right0), channel_id=1, source_target_pairs={{0,64},{16,80},{32,96},{48,112},{64,0},{80,16},{96,32},{112,48},{1... | collective-permute-start | bytes 835592 | tf_op jit(solution)/shard_map/ppermute | solution.py:28
  31.7 13.8 %collective-permute-start.9 = (bf16[4,272,128]{2,1,0:T(8,128)(2,1)S(1)}, bf16[4,272,128]{2,1,0:T(8,128)(2,1)S(1)}, u32[]{:S(2)}, u32[]{:S(2)}) collective-permute-start(bf16[4,272,128]{2,1,0:T(8,128)(2,1)S(1)} %pad_maximum_fusion.1.right0), channel_id=1, source_target_pairs={{0,128},{16,144},{32,160},{48,176},{64,192},{80,208},{96,224},{112... | collective-permute-start | bytes 835592 | tf_op jit(solution)/shard_map/ppermute | solution.py:28
  33.0 0.8 copy-start.4
  33.8 0.8 copy-start.5
  34.6 0.8 copy-start.6
  35.5 10.0 %copy-start = (bf16[8,16,128]{2,1,0:T(8,128)(2,1)S(1)}, bf16[8,16,128]{2,1,0:T(8,128)(2,1)}, u32[]{:S(2)}) copy-start(bf16[8,16,128]{2,1,0:T(8,128)(2,1)} %param.14) | copy-start | bytes 98308
  35.5 10.0 %copy-start.1 = (bf16[128,128]{1,0:T(8,128)(2,1)S(1)}, bf16[128,128]{1,0:T(8,128)(2,1)}, u32[]{:S(2)}) copy-start(bf16[128,128]{1,0:T(8,128)(2,1)} %wo_ref.1) | copy-start | bytes 98308
  81.8 2.5 %collective-permute-start.11 = (bf16[1344,128]{1,0:T(8,128)(2,1)S(1)}, bf16[1344,128]{1,0:T(8,128)(2,1)S(1)}, u32[]{:S(2)}, u32[]{:S(2)}) collective-permute-start(bf16[1344,128]{1,0:T(8,128)(2,1)S(1)} %pad_maximum_fusion), channel_id=1, source_target_pairs={{0,1},{1,0},{2,3},{3,2},{4,5},{5,4},{6,7},{7,6},{8,9},{9,8},{10,11... | collective-permute-start | bytes 1032200 | tf_op jit(solution)/shard_map/ppermute | solution.py:367
  84.5 7.8 %collective-permute-start.12 = (bf16[576,128]{1,0:T(8,128)(2,1)S(1)}, bf16[576,128]{1,0:T(8,128)(2,1)S(1)}, u32[]{:S(2)}, u32[]{:S(2)}) collective-permute-start(bf16[576,128]{1,0:T(8,128)(2,1)S(1)} %get-tuple-element.37), channel_id=1, source_target_pairs={{0,4},{1,5},{2,6},{3,7},{4,0},{5,1},{6,2},{7,3},{8,12},{9,13},{10,... | collective-permute-start | bytes 442376 | tf_op jit(solution)/shard_map/ppermute | solution.py:370
  84.6 10.0 %collective-permute-start.13 = (bf16[576,128]{1,0:T(8,128)(2,1)S(1)}, bf16[576,128]{1,0:T(8,128)(2,1)S(1)}, u32[]{:S(2)}, u32[]{:S(2)}) collective-permute-start(bf16[576,128]{1,0:T(8,128)(2,1)S(1)} %get-tuple-element.38), channel_id=1, source_target_pairs={{0,8},{1,9},{2,10},{3,11},{4,12},{5,13},{6,14},{7,15},{8,0},{9,1},... | collective-permute-start | bytes 442376 | tf_op jit(solution)/shard_map/ppermute | solution.py:370
  87.8 9.3 %collective-permute-start.14 = (bf16[576,128]{1,0:T(8,128)(2,1)S(1)}, bf16[576,128]{1,0:T(8,128)(2,1)S(1)}, u32[]{:S(2)}, u32[]{:S(2)}) collective-permute-start(bf16[576,128]{1,0:T(8,128)(2,1)S(1)} %concatenate.49), channel_id=1, source_target_pairs={{0,12},{1,13},{2,14},{3,15},{4,8},{5,9},{6,10},{7,11},{8,4},{9,5},... | collective-permute-start | bytes 442376 | tf_op jit(solution)/shard_map/ppermute | solution.py:370
  88.5 12.5 %collective-permute-start.16 = (bf16[1024,128]{1,0:T(8,128)(2,1)S(1)}, bf16[1024,128]{1,0:T(8,128)(2,1)S(1)}, u32[]{:S(2)}, u32[]{:S(2)}) collective-permute-start(bf16[1024,128]{1,0:T(8,128)(2,1)S(1)} %bitcast.50), channel_id=1, source_target_pairs={{0,64},{16,80},{32,96},{48,112},{64,0},{80,16},{96,32},{112,48},{1... | collective-permute-start | bytes 786440 | tf_op jit(solution)/shard_map/ppermute | solution.py:354
  88.6 14.5 %collective-permute-start.17 = (bf16[1024,128]{1,0:T(8,128)(2,1)S(1)}, bf16[1024,128]{1,0:T(8,128)(2,1)S(1)}, u32[]{:S(2)}, u32[]{:S(2)}) collective-permute-start(bf16[1024,128]{1,0:T(8,128)(2,1)S(1)} %bitcast.49), channel_id=1, source_target_pairs={{0,128},{16,144},{32,160},{48,176},{64,192},{80,208},{96,224},{112... | collective-permute-start | bytes 786440 | tf_op jit(solution)/shard_map/ppermute | solution.py:354
  92.3 13.4 %collective-permute-start.18 = (bf16[1024,128]{1,0:T(8,128)(2,1)S(1)}, bf16[1024,128]{1,0:T(8,128)(2,1)S(1)}, u32[]{:S(2)}, u32[]{:S(2)}) collective-permute-start(bf16[1024,128]{1,0:T(8,128)(2,1)S(1)} %bitcast.48), channel_id=1, source_target_pairs={{0,192},{16,208},{32,224},{48,240},{64,128},{80,144},{96,160},{112... | collective-permute-start | bytes 786440 | tf_op jit(solution)/shard_map/ppermute | solution.py:354
  97.2 8.7 %collective-permute-start.15 = (bf16[448,128]{1,0:T(8,128)(2,1)S(1)}, bf16[448,128]{1,0:T(8,128)(2,1)S(1)}, u32[]{:S(2)}, u32[]{:S(2)}) collective-permute-start(bf16[448,128]{1,0:T(8,128)(2,1)S(1)} %slice.103), channel_id=1, source_target_pairs={{0,2},{1,3},{2,0},{3,1},{4,6},{5,7},{6,4},{7,5},{8,10},{9,11},{10,... | collective-permute-start | bytes 344072 | tf_op jit(solution)/shard_map/ppermute | solution.py:378
  105.9 8.7 %collective-permute-start.22 = (bf16[320,128]{1,0:T(8,128)(2,1)S(1)}, bf16[320,128]{1,0:T(8,128)(2,1)S(1)}, u32[]{:S(2)}, u32[]{:S(2)}) collective-permute-start(bf16[320,128]{1,0:T(8,128)(2,1)S(1)} %fusion.3), channel_id=1, source_target_pairs={{0,64},{16,80},{32,96},{48,112},{64,0},{80,16},{96,32},{112,48},{1... | collective-permute-start | bytes 245768 | tf_op jit(solution)/shard_map/ppermute | solution.py:44
  106.0 10.2 %collective-permute-start.23 = (bf16[320,128]{1,0:T(8,128)(2,1)S(1)}, bf16[320,128]{1,0:T(8,128)(2,1)S(1)}, u32[]{:S(2)}, u32[]{:S(2)}) collective-permute-start(bf16[320,128]{1,0:T(8,128)(2,1)S(1)} %fusion.3), channel_id=1, source_target_pairs={{0,128},{16,144},{32,160},{48,176},{64,192},{80,208},{96,224},{112... | collective-permute-start | bytes 245768 | tf_op jit(solution)/shard_map/ppermute | solution.py:44
  108.6 7.7 %collective-permute-start.24 = (bf16[320,128]{1,0:T(8,128)(2,1)S(1)}, bf16[320,128]{1,0:T(8,128)(2,1)S(1)}, u32[]{:S(2)}, u32[]{:S(2)}) collective-permute-start(bf16[320,128]{1,0:T(8,128)(2,1)S(1)} %fusion.3), channel_id=1, source_target_pairs={{0,192},{16,208},{32,224},{48,240},{64,128},{80,144},{96,160},{112... | collective-permute-start | bytes 245768 | tf_op jit(solution)/shard_map/ppermute | solution.py:44
  109.9 9.8 %collective-permute-start.19 = (bf16[256,128]{1,0:T(8,128)(2,1)S(1)}, bf16[256,128]{1,0:T(8,128)(2,1)S(1)}, u32[]{:S(2)}, u32[]{:S(2)}) collective-permute-start(bf16[256,128]{1,0:T(8,128)(2,1)S(1)} %get-tuple-element.30), channel_id=1, source_target_pairs={{0,16},{16,0},{32,48},{48,32},{64,80},{80,64},{96,112},{112,96},{1... | collective-permute-start | bytes 196616 | tf_op jit(solution)/shard_map/ppermute | solution.py:357
  114.1 7.3 %collective-permute-start.20 = (bf16[256,128]{1,0:T(8,128)(2,1)S(1)}, bf16[256,128]{1,0:T(8,128)(2,1)S(1)}, u32[]{:S(2)}, u32[]{:S(2)}) collective-permute-start(bf16[256,128]{1,0:T(8,128)(2,1)S(1)} %get-tuple-element.32), channel_id=1, source_target_pairs={{0,32},{16,48},{32,0},{48,16},{64,96},{80,112},{96,64},{112,80},{1... | collective-permute-start | bytes 196616 | tf_op jit(solution)/shard_map/ppermute | solution.py:357
  114.6 6.7 %collective-permute-start.21 = (bf16[256,128]{1,0:T(8,128)(2,1)S(1)}, bf16[256,128]{1,0:T(8,128)(2,1)S(1)}, u32[]{:S(2)}, u32[]{:S(2)}) collective-permute-start(bf16[256,128]{1,0:T(8,128)(2,1)S(1)} %get-tuple-element.31), channel_id=1, source_target_pairs={{0,48},{16,32},{32,16},{48,0},{64,112},{80,96},{96,80},{112,64},{1... | collective-permute-start | bytes 196616 | tf_op jit(solution)/shard_map/ppermute | solution.py:357
  116.3 6.3 %collective-permute-start.25 = (bf16[320,128]{1,0:T(8,128)(2,1)S(1)}, bf16[320,128]{1,0:T(8,128)(2,1)S(1)}, u32[]{:S(2)}, u32[]{:S(2)}) collective-permute-start(bf16[320,128]{1,0:T(8,128)(2,1)S(1)} %add_convert_fusion.1), channel_id=1, source_target_pairs={{0,16},{16,0},{32,48},{48,32},{64,80},{80,64},{96,112},{112,96},{1... | collective-permute-start | bytes 245768 | tf_op jit(solution)/shard_map/ppermute | solution.py:44
  119.2 8.8 %collective-permute-start.26 = (bf16[320,128]{1,0:T(8,128)(2,1)S(1)}, bf16[320,128]{1,0:T(8,128)(2,1)S(1)}, u32[]{:S(2)}, u32[]{:S(2)}) collective-permute-start(bf16[320,128]{1,0:T(8,128)(2,1)S(1)} %add_convert_fusion.1), channel_id=1, source_target_pairs={{0,32},{16,48},{32,0},{48,16},{64,96},{80,112},{96,64},{112,80},{1... | collective-permute-start | bytes 245768 | tf_op jit(solution)/shard_map/ppermute | solution.py:44
  119.7 8.2 %collective-permute-start.27 = (bf16[320,128]{1,0:T(8,128)(2,1)S(1)}, bf16[320,128]{1,0:T(8,128)(2,1)S(1)}, u32[]{:S(2)}, u32[]{:S(2)}) collective-permute-start(bf16[320,128]{1,0:T(8,128)(2,1)S(1)} %add_convert_fusion.1), channel_id=1, source_target_pairs={{0,48},{16,32},{32,16},{48,0},{64,112},{80,96},{96,80},{112,64},{1... | collective-permute-start | bytes 245768 | tf_op jit(solution)/shard_map/ppermute | solution.py:44
  128.0 2.6 %collective-permute-start.28 = (bf16[320,128]{1,0:T(8,128)(2,1)S(1)}, bf16[320,128]{1,0:T(8,128)(2,1)S(1)}, u32[]{:S(2)}, u32[]{:S(2)}) collective-permute-start(bf16[320,128]{1,0:T(8,128)(2,1)S(1)} %add_convert_fusion), channel_id=1, source_target_pairs={{0,1},{1,0},{2,3},{3,2},{4,5},{5,4},{6,7},{7,6},{8,9},{9,8},{10,11... | collective-permute-start | bytes 245768 | tf_op jit(solution)/shard_map/ppermute | solution.py:384
where the time goes:
time: 132 us
  starting transfers between devices  54.1 us (41%)
  Pallas kernels  36.2 us (27%)
  waiting for transfers between devices  33.6 us (25%)
  local copies, waits for them, and re-layouts  5.21 us (4%)
  other arithmetic  2.05 us (2%)
    pallas_call x1, Pallas kernels, triples(): pl.pallas_call(triple_kernel, out_shape=(jax.ShapeDtypeStruct((16, 128, 1...  36.2 us
    ppermute x3, waiting for transfers between devices, gather_row(): return [line] + [lax.ppermute(line, 'row', flip(k)) for k in (4, 8, 12)]  9.94 us
    ppermute x6, starting transfers between devices, meet(): came = [lax.ppermute(own, axis, flip(k)).astype(F32) for k in flips]  8.95 us
    ppermute x3, starting transfers between devices, body(): lax.ppermute(chunks[k], 'row', flip(k))  6.38 us
    ppermute x3, starting transfers between devices, gather_col(): lax.ppermute(pair, 'col', flip(k))  6.01 us
    ppermute x6, waiting for transfers between devices, meet(): came = [lax.ppermute(own, axis, flip(k)).astype(F32) for k in flips]  5.87 us
    ppermute x3, starting transfers between devices, gather_row(): lax.ppermute(block, 'row', flip(k))  5.55 us
    ppermute x1, starting transfers between devices, gather_col(): pair = jnp.stack([block, lax.ppermute(block, 'col', flip(2))])  5.19 us
  transfers between devices with their start and end apart: 29, of which 14 were waited for; matrix products, arithmetic and copies ran while one was open for 2% of the time, Pallas kernels for 0%

commit v1 on v0

v1 whole, which is shorter than its diff:
```python
import math

import jax
import jax.numpy as jnp
from jax import lax
from jax.experimental import pallas as pl
from jax.experimental.pallas import tpu as pltpu
from jax.sharding import PartitionSpec as P

HEADS = 4
HEAD_DIM = 32
BF = jnp.bfloat16
F32 = jnp.float32


def flip(k):
    return [(i, i ^ k) for i in range(16)]


def send(block, axis, k):
    with jax.named_scope("s_" + axis + str(k)):
        return lax.ppermute(block, axis, flip(k))


def gather(left, right):
    line = jnp.stack([right] + [send(right, "row", k) for k in (1, 2, 3)])
    line, left = lax.optimization_barrier((line, left))
    near = send(line, "row", 4)
    far = send(line, "row", 12)
    pair = jnp.stack([left, send(left, "col", 2)])
    near, far, pair = lax.optimization_barrier((near, far, pair))
    first = send(far[:2], "row", 4)
    second = send(near[2:], "row", 12)
    quads = jnp.concatenate([pair] + [send(pair, "col", k) for k in (4, 8, 12)])
    first, second, quads = lax.optimization_barrier((first, second, quads))
    return (quads, send(quads, "col", 1)), (line, near, far, first, second)


def left_place(col, b):
    apart = col ^ b
    return (apart & 1) * 8 + (apart >> 2) * 2 + ((apart >> 1) & 1)


def add_up(own, others):
    total = own.astype(F32)
    for other in others:
        total = total + other.astype(F32)
    return total


def meet(own, axis, flips):
    came = [send(own, axis, k).astype(F32) for k in flips]
    return (own.astype(F32) + came[0]) + (came[1] + came[2])


def nt(a, b):
    return lax.dot_general(a, b, (((1,), (1,)), ((), ())), preferred_element_type=F32)


def nn(a, b):
    return jnp.dot(a, b, preferred_element_type=F32)


def tn(a, b):
    return lax.dot_general(a, b, (((0,), (0,)), ((), ())), preferred_element_type=F32)


def fold(tiles):
    place = lax.broadcasted_iota(jnp.int32, tiles[0].shape, 0)
    low = place < 4
    fours = [
        jnp.where(low, tiles[n], tiles[n + 4])
        + pltpu.roll(jnp.where(low, tiles[n + 4], tiles[n]), 4, 0)
        for n in range(4)
    ]
    low = (place & 2) == 0
    twos = [
        jnp.where(
            low,
            fours[n] + pltpu.roll(fours[n], 6, 0),
            fours[n + 2] + pltpu.roll(fours[n + 2], 2, 0),
        )
        for n in range(2)
    ]
    return jnp.where(
        (place & 1) == 0,
        twos[0] + pltpu.roll(twos[0], 7, 0),
        twos[1] + pltpu.roll(twos[1], 1, 0),
    )


def triple_kernel(
    at_ref,
    left0,
    left1,
    right0,
    right1,
    right3,
    right2a,
    right2b,
    cot_hbm,
    wq_hbm,
    wk_hbm,
    wl_hbm,
    wr_hbm,
    wo_hbm,
    lkeep,
    lsend,
    akeep,
    asend,
    bkeep,
    bsend,
    xl,
    xr,
    ql,
    kr,
    gql,
    gkr,
    ub,
    ts,
    tg,
    pb,
    sb,
    att,
    lb,
    rb,
    rp,
    vr,
    up,
    cot_ref,
    weights,
    arrived,
):
    scaling = 1.0 / math.sqrt(HEAD_DIM)
    copies = [
        pltpu.make_async_copy(ref, weights.at[n], arrived.at[n])
        for n, ref in enumerate((wq_hbm, wl_hbm, wk_hbm, wr_hbm, wo_hbm))
    ]
    copies.append(pltpu.make_async_copy(cot_hbm, cot_ref, arrived.at[5]))
    for copy in copies:
        copy.start()
    row = at_ref[0]
    col = at_ref[1]
    lefts = (left0, left1)
    rights = (
        [(right0, z) for z in range(4)]
        + [(right1, z) for z in range(4)]
        + [(right2a, 0), (right2a, 1), (right2b, 0), (right2b, 1)]
        + [(right3, z) for z in range(4)]
    )
    outs = [None] * 16
    for z in range(2):
        outs[z], outs[12 + z] = (akeep, z), (akeep, 2 + z)
        outs[4 + z], outs[8 + z] = (asend, z), (asend, 2 + z)
        outs[2 + z], outs[6 + z] = (bkeep, z), (bkeep, 2 + z)
        outs[14 + z], outs[10 + z] = (bsend, z), (bsend, 2 + z)
    slots = [left_place(col, row ^ t) for t in range(16)]

    lane = lax.broadcasted_iota(jnp.int32, (16, 128), 1) // 16
    half0 = jnp.zeros((16, 128), F32)
    half1 = jnp.zeros((16, 128), F32)
    for t in range(16):
        slot = slots[t]
        block, z = rights[t]
        for j in range(16):
            xr[j, slot] = block[z, 16 * j : 16 * j + 16, :]
        came = block[z, 256:272, :].astype(F32)
        half0 = jnp.where(lane == slot, came, half0)
        half1 = jnp.where(lane + 8 == slot, came, half1)
    right_allowed = jnp.concatenate([half0, half1], axis=1)
    spread4 = (
        lax.broadcasted_iota(jnp.int32, (64, 16), 0) // 4
        == lax.broadcasted_iota(jnp.int32, (64, 16), 1)
    ).astype(BF)
    right_allowed = nn(spread4, right_allowed.astype(BF))
    halves = []
    for half in range(2):
        total = jnp.zeros((16, 128), F32)
        for s in range(8):
            total = jnp.where(lane == s, lefts[half][s, 128:144, :].astype(F32), total)
        halves.append(total)
    left_allowed = jnp.concatenate(halves, axis=1)

    for i in range(8):
        for s in range(16):
            xl[i, s] = lefts[s // 8][s % 8, 16 * i : 16 * i + 16, :]
    for copy in copies:
        copy.wait()
    wl = jnp.concatenate([weights[0].T, weights[1].T])
    wr = jnp.concatenate([weights[2].T, weights[3].T])

    def project_left(i, _):
        ql[i] = nt(wl, xl[i].reshape(256, 128)).astype(BF).astype(F32)
        return 0

    lax.fori_loop(0, 8, project_left, 0, unroll=4)

    def project_right(j, _):
        kr[j] = nt(wr, xr[j].reshape(256, 128)).astype(BF).astype(F32)
        return 0

    lax.fori_loop(0, 16, project_right, 0, unroll=4)
    cot = cot_ref[...]
    pick = (
        lax.broadcasted_iota(jnp.int32, (16, 2048), 1) // 128
        == lax.broadcasted_iota(jnp.int32, (16, 2048), 0)
    ).astype(BF)
    wo = weights[4]

    up[...] = nt(cot, wo).astype(BF).astype(F32)
    place = lax.broadcasted_iota(jnp.int32, (8, 256), 0)
    heads = lax.broadcasted_iota(jnp.int32, (8, 256), 1) // 32
    agree = place == heads

    def grad_row(i):
        for jj in range(8):
            both = jnp.concatenate(
                [
                    jnp.broadcast_to(up[pl.ds(i * 16 + 2 * jj + n, 1), :], (8, 128))
                    for n in range(2)
                ],
                axis=1,
            )
            both = jnp.where(agree, both, 0.0).astype(BF)
            tg[i, pl.ds(8 * jj, 8), :] = nn(both, vr[i, jj])

    def score_row(i, _):
        mine = cot_ref[pl.ds(pl.multiple_of(i * 16, 16), 16), :]
        spread = nn(nt(wo, mine).astype(BF), pick)
        for j in range(16):
            ub[i * 16 + j] = spread[:, 128 * j : 128 * j + 128]
        grad_row(jnp.maximum(i - 1, 0))
        for h in range(4):
            tiles = [pl.ds(h * 32 + 8 * e, 8) for e in range(4)]
            q = [ql[i, r, :] for r in tiles]
            v = ql[i, pl.ds(128 + h * 32, 32), :]
            for half in range(2):
                scores = []
                for j in range(8 * half, 8 * half + 8):
                    k = [kr[j, r, :] for r in tiles]
                    scores.append((q[0] * k[0] + q[1] * k[1]) + (q[2] * k[2] + q[3] * k[3]))
                    w = kr[j, pl.ds(128 + h * 32, 32), :]
                    vr[i, j // 2, pl.ds(j % 2 * 128 + h * 32, 32), :] = (v * w).astype(BF)
                score = fold(scores)
                for side in range(2):
                    ts[i, side, pl.ds(32 * half + h, 8, stride=4), :] = score[
                        :, 128 * side : 128 * side + 128
                    ]
        return 0

    lax.fori_loop(0, 8, score_row, 0)
    grad_row(7)

    for i in range(8):
        for part in range(2):
            rows = pl.ds(32 * part, 32)
            allowed = right_allowed[32 * part : 32 * part + 32] * left_allowed[i : i + 1, :] > 0.5
            score = jnp.concatenate([ts[i, 0, rows, :], ts[i, 1, rows, :]], axis=1)
            score = jnp.where(allowed, score * scaling, -1000000000.0)
            grad = tg[i, rows, :]
            top = jnp.max(score, axis=1, keepdims=True)
            raw = jnp.exp(score - top)
            prob = raw / jnp.sum(raw, axis=1, keepdims=True)
            mean = jnp.sum(prob * grad, axis=1, keepdims=True)
            grad = prob * (grad - mean) * scaling
            pb[i, rows, :] = prob.astype(BF).astype(F32)
            sb[i, rows, :] = grad.astype(BF).astype(F32)

    agree = agree[:, :128], agree[:, 128:]

    def gradients(t, _):
        h = t // 4
        rows = pl.ds(pl.multiple_of(t * 8, 8), 8)
        lower = pl.ds(pl.multiple_of(128 + t * 8, 8), 8)
        seen = []
        for n in range(8):
            jj = t % 2 * 4 + n // 2
            prob = pb[t // 2, pl.ds(pl.multiple_of(8 * jj, 8), 8), :].astype(BF)
            part = nt(prob, vr[t // 2, jj, pl.ds(n % 2 * 128, 128), :])
            seen.append(jnp.where(agree[n % 2], part, 0.0))
        att[rows, :] = fold(seen)
        for ib in range(2):
            group = range(4 * ib, 4 * ib + 4)
            q = [ql[i, rows, :] for i in group]
            v = [ql[i, lower, :] for i in group]
            gq = [jnp.zeros((8, 256), F32) for _ in group]
            gl = [jnp.zeros((8, 256), F32) for _ in group]
            for j in range(16):
                k = kr[j, rows, :]
                w = kr[j, lower, :]
                at = pl.ds(j * 4 + h, 1)
                if ib == 0:
                    gk = jnp.zeros((8, 256), F32)
                    gr = jnp.zeros((8, 256), F32)
                else:
                    gk = gkr[j, rows, :]
                    gr = gkr[j, lower, :]
                for n, i in enumerate(group):
                    p = jnp.broadcast_to(pb[i, at, :], (8, 256))
                    s = jnp.broadcast_to(sb[i, at, :], (8, 256))
                    u = ub[i * 16 + j, rows, :]
                    pu = p * jnp.concatenate([u, u], axis=1)
                    gl[n] = gl[n] + pu * w
                    gr = gr + pu * v[n]
                    gq[n] = gq[n] + s * k
                    gk = gk + s * q[n]
                gkr[j, rows, :] = gk
                gkr[j, lower, :] = gr
            for n, i in enumerate(group):
                gql[i, rows, :] = gq[n]
                gql[i, lower, :] = gl[n]
        return 0

    lax.fori_loop(0, 16, gradients, 0)

    def finish(n, _):
        g = gql[n].astype(BF)
        lb[:, pl.ds(pl.multiple_of(n * 256, 256), 256)] = g
        part = tn(g, wl).astype(BF).reshape(16, 16, 128)
        for s in range(16):
            rows = pl.ds(pl.multiple_of(s % 8 * 128 + n * 16, 16), 16)
            (lkeep, lsend)[s // 8][rows, :] = part[s]
        for m in range(2):
            j = 2 * n + m
            g = gkr[j].astype(BF)
            rb[:, pl.ds(pl.multiple_of(j * 256, 256), 256)] = g
            rp[j] = tn(g, wr).astype(BF).reshape(16, 16, 128)
            rows = pl.ds(pl.multiple_of(j * 16, 16), 16)
            for t in range(16):
                out, z = outs[t]
                out[z, rows, :] = rp[j, slots[t]]
        return 0

    lax.fori_loop(0, 8, finish, 0, unroll=2)
    lsum = nn(lb[...], xl[...].reshape(2048, 128))
    rsum = nn(rb[...], xr[...].reshape(4096, 128))
    sums = jnp.concatenate(
        [
            lsum[:128].T,
            rsum[:128].T,
            lsum[128:].T,
            rsum[128:].T,
            tn(att[...].astype(BF), cot),
        ]
    )
    even = (col & 1) == 0
    lkeep[1024:1344, :] = jnp.where(even, sums[:320], sums[320:]).astype(BF)
    lsend[1024:1344, :] = jnp.where(even, sums[320:], sums[:320]).astype(BF)


def triples(at, lefts, rights, cot, wq, wk, wl, wr, wo):
    vmem = pl.BlockSpec(memory_space=pltpu.VMEM)
    return pl.pallas_call(
        triple_kernel,
        out_shape=(
            jax.ShapeDtypeStruct((1344, 128), BF),
            jax.ShapeDtypeStruct((1344, 128), BF),
            jax.ShapeDtypeStruct((4, 256, 128), BF),
            jax.ShapeDtypeStruct((4, 256, 128), BF),
            jax.ShapeDtypeStruct((4, 256, 128), BF),
            jax.ShapeDtypeStruct((4, 256, 128), BF),
        ),
        in_specs=[pl.BlockSpec(memory_space=pltpu.SMEM)]
        + [vmem] * 7
        + [pl.BlockSpec(memory_space=pl.ANY)] * 6,
        out_specs=(vmem,) * 6,
        scratch_shapes=[
            pltpu.VMEM((8, 16, 16, 128), BF),
            pltpu.VMEM((16, 16, 16, 128), BF),
            pltpu.VMEM((8, 256, 256), F32),
            pltpu.VMEM((16, 256, 256), F32),
            pltpu.VMEM((8, 256, 256), F32),
            pltpu.VMEM((16, 256, 256), F32),
            pltpu.VMEM((128, 128, 128), F32),
            pltpu.VMEM((8, 2, 64, 128), F32),
            pltpu.VMEM((8, 64, 256), F32),
            pltpu.VMEM((8, 64, 256), F32),
            pltpu.VMEM((8, 64, 256), F32),
            pltpu.VMEM((128, 128), F32),
            pltpu.VMEM((256, 2048), BF),
            pltpu.VMEM((256, 4096), BF),
            pltpu.VMEM((16, 16, 16, 128), BF),
            pltpu.VMEM((8, 8, 256, 256), BF),
            pltpu.VMEM((128, 128), F32),
            pltpu.VMEM((128, 128), BF),
            pltpu.VMEM((5, 128, 128), BF),
            pltpu.SemaphoreType.DMA((6,)),
        ],
        compiler_params=pltpu.CompilerParams(vmem_limit_bytes=48 * 1024 * 1024),
        cost_estimate=pl.CostEstimate(
            flops=800_000_000, bytes_accessed=5_000_000, transcendentals=131072
        ),
    )(at, *lefts, *rights, cot, wq, wk, wl, wr, wo)


def body(
    left_edges,
    right_edges,
    left_mask,
    right_mask,
    cotangent,
    query_weight,
    key_weight,
    left_weight,
    right_weight,
    out_weight,
):
    width = left_edges.shape[2]
    row = lax.axis_index("row")
    col = lax.axis_index("col")
    left_rows = jnp.concatenate(
        [
            left_edges.reshape(-1, width),
            jnp.pad(jnp.tile(left_mask.astype(BF), (1, 8)), ((0, 8), (0, 0))),
        ]
    )
    right_rows = jnp.concatenate(
        [
            jnp.swapaxes(right_edges, 0, 1).reshape(-1, width),
            jnp.tile(right_mask.T.astype(BF), (1, 8)),
        ]
    )
    lefts, rights = gather(left_rows, right_rows)
    left_keep, left_send, first_keep, first_send, second_keep, second_send = triples(
        jnp.stack([row, col]).astype(jnp.int32),
        lefts,
        rights,
        cotangent.reshape(-1, width),
        query_weight,
        key_weight,
        left_weight,
        right_weight,
        out_weight,
    )

    core = col & 1
    first_came = send(first_send, "row", 4)
    second_came = send(second_send, "row", 12)
    left_total = add_up(left_keep, [send(left_send, "col", 1)])
    low = left_total.astype(BF)
    came = [
        send(jnp.concatenate([low[256 * k : 256 * k + 256], low[1024:]]), "col", 4 * k).astype(F32)
        for k in (1, 2, 3)
    ]
    first_came, second_came, came[0] = lax.optimization_barrier((first_came, second_came, came[0]))
    kept = jnp.concatenate([left_total[:256], low[1024:].astype(F32)])
    total = (kept + came[0]) + (came[1] + came[2])
    low = total[128:].astype(BF)
    first = add_up(first_keep, [first_came])
    second = add_up(second_keep, [second_came])
    first_low, second_low, low = lax.optimization_barrier(
        (first[2:].astype(BF), second[2:].astype(BF), low)
    )
    first_came = send(first_low, "row", 12)
    second_came = send(second_low, "row", 4)
    came = send(low, "col", 2).astype(F32)
    left_grad = total[:128] + came[:128]
    weights = low[128:].astype(F32) + came[128:]
    right_total = jnp.concatenate(
        [add_up(first[:2], [first_came]), add_up(second[:2], [second_came])]
    )
    low = right_total.astype(BF)
    weights, low = lax.optimization_barrier((weights.astype(BF), low))
    weights = meet(weights, "row", (4, 8, 12)).astype(BF)
    weights, low = lax.optimization_barrier((weights, low))
    right_came = [send(low[k], "row", k) for k in (2, 1, 3)]
    weights = meet(weights, "row", (1, 2, 3))
    right_grad = right_total[0] + right_came[1].astype(F32) + right_came[0].astype(F32)
    right_grad = right_grad + right_came[2].astype(F32)
    right_grad = jnp.swapaxes(right_grad.reshape(16, 16, width), 0, 1)
    mine = weights.astype(BF)
    other = send(mine, "col", 1)
    first = jnp.where(core == 0, mine, other)
    second = jnp.where(core == 0, other, mine)
    weights = jnp.concatenate([first, second]).astype(F32)
    proj_grads = weights[:512].reshape(4, 128, width)
    return (left_grad.reshape(left_edges.shape), right_grad, proj_grads, weights[512:])


def solution(mesh):
    return jax.shard_map(
        body,
        mesh=mesh,
        in_specs=(
            P("row", "col", None),
            P("row", "col", None),
            P("row", "col"),
            P("row", "col"),
            P("row", "col", None),
            P(),
            P(),
            P(),
            P(),
            P(),
        ),
        out_specs=(P("row", "col", None), P("row", "col", None), P(), P()),
        check_vma=False,
    )
```

time: 132 us -> 105 us (0.80)
  Pallas kernels: 36.2 us -> 19.5 us
  waiting for transfers between devices: 33.6 us -> 25.8 us
  local copies, waits for them, and re-layouts: 5.21 us -> 1.9 us
    pallas_call x1, Pallas kernels: 36.2 us -> 19.5 us  [triples(): pl.pallas_call(triple_kernel, out_shape=(jax.ShapeDtypeStruct((1344, 128)...]
    ppermute x29 -> x31, waiting for transfers between devices: 33.6 us -> 25.8 us  [send(): return lax.ppermute(block, axis, flip(k))]
    unnamed x26 -> x18, local copies, waits for them, and re-layouts: 3.13 us -> 0.05 us
    ppermute x29 -> x31, starting transfers between devices: 54.1 us -> 53.3 us  [send(): return lax.ppermute(block, axis, flip(k))]
  transfers between devices with their start and end apart: 29 -> 31, of which waited for: 14 -> 17; matrix products, arithmetic and copies ran while one was open for 2% -> 2% of each run, Pallas kernels for 0% -> 0%
where the time goes in v1:
time: 105 us; the launch traced here: 104 us
  starting transfers between devices  53.3 us (51%)
  waiting for transfers between devices  25.8 us (25%)
  Pallas kernels  19.5 us (19%)
  other arithmetic  2.81 us (3%)
  local copies, waits for them, and re-layouts  1.9 us (2%)
    ppermute x31, starting transfers between devices, send(): return lax.ppermute(block, axis, flip(k))  53.3 us
    ppermute x31, waiting for transfers between devices, send(): return lax.ppermute(block, axis, flip(k))  25.8 us
    pallas_call x1, Pallas kernels, triples(): pl.pallas_call(triple_kernel, out_shape=(jax.ShapeDtypeStruct((1344, 128)...  19.5 us
  transfers between devices with their start and end apart: 31, of which 17 were waited for; matrix products, arithmetic and copies ran while one was open for 2% of the time, Pallas kernels for 0%

profile of v1, /device:TPU:1, one launch (start us, length us, event | category | flops | bytes accessed | tf_op | source)
XLA Modules:
  0.0 104.3 jit_solution(4111482249422317616)
XLA Ops:
  0.6 0.7 convert_bitcast_fusion
  1.4 0.1 copy.15
  1.5 0.1 tile.9
  1.6 0.0 copy-start.8
  1.6 0.0 copy-start.7
  1.6 3.9 %collective-permute-start.1 = (bf16[272,128]{1,0:T(8,128)(2,1)S(1)}, bf16[272,128]{1,0:T(8,128)(2,1)S(1)}, u32[]{:S(2)}, u32[]{:S(2)}) collective-permute-start(bf16[272,128]{1,0:T(8,128)(2,1)S(1)} %get-tuple-element.68), channel_id=1, source_target_pairs={{0,32},{16,48},{32,0},{48,16},{64,96},{80,112},{96,64},{112,80},{1... | collective-permute-start | bytes 208904 | tf_op jit(solution)/shard_map/s_row2/ppermute | solution.py:22
  5.5 1.6 %collective-permute-start = (bf16[272,128]{1,0:T(8,128)(2,1)S(1)}, bf16[272,128]{1,0:T(8,128)(2,1)S(1)}, u32[]{:S(2)}, u32[]{:S(2)}) collective-permute-start(bf16[272,128]{1,0:T(8,128)(2,1)S(1)} %get-tuple-element.68), channel_id=1, source_target_pairs={{0,16},{16,0},{32,48},{48,32},{64,80},{80,64},{96,112},{112,96},{1... | collective-permute-start | bytes 208904 | tf_op jit(solution)/shard_map/s_row1/ppermute | solution.py:22
  7.2 0.1 tile.21
  7.3 2.0 %collective-permute-done = bf16[272,128]{1,0:T(8,128)(2,1)S(1)} collective-permute-done((bf16[272,128]{1,0:T(8,128)(2,1)S(1)}, bf16[272,128]{1,0:T(8,128)(2,1)S(1)}, u32[]{:S(2)}, u32[]{:S(2)}) %collective-permute-start) | collective-permute-done | bytes 69664 | tf_op jit(solution)/shard_map/s_row1/ppermute | solution.py:22
  9.3 2.9 %collective-permute-done.2 = bf16[272,128]{1,0:T(8,128)(2,1)S(1)} collective-permute-done((bf16[272,128]{1,0:T(8,128)(2,1)S(1)}, bf16[272,128]{1,0:T(8,128)(2,1)S(1)}, u32[]{:S(2)}, u32[]{:S(2)}) %collective-permute-start.2) | collective-permute-done | bytes 69664 | tf_op jit(solution)/shard_map/s_row3/ppermute | solution.py:22
  12.3 2.6 %collective-permute-start.4 = (bf16[4,272,128]{2,1,0:T(8,128)(2,1)S(1)}, bf16[4,272,128]{2,1,0:T(8,128)(2,1)S(1)}, u32[]{:S(2)}, u32[]{:S(2)}) collective-permute-start(bf16[4,272,128]{2,1,0:T(8,128)(2,1)S(1)} %pad_maximum_fusion.1.right0), channel_id=1, source_target_pairs={{0,192},{16,208},{32,224},{48,240},{64,128},{80,144},{96,160},{112... | collective-permute-start | bytes 835592 | tf_op jit(solution)/shard_map/s_row12/ppermute | solution.py:22
  14.9 4.7 %collective-permute-start.5 = (bf16[144,128]{1,0:T(8,128)(2,1)S(1)}, bf16[144,128]{1,0:T(8,128)(2,1)S(1)}, u32[]{:S(2)}, u32[]{:S(2)}) collective-permute-start(bf16[144,128]{1,0:T(8,128)(2,1)S(1)} %fusion.7), channel_id=1, source_target_pairs={{0,2},{1,3},{2,0},{3,1},{4,6},{5,7},{6,4},{7,5},{8,10},{9,11},{10,... | collective-permute-start | bytes 110600 | tf_op jit(solution)/shard_map/s_col2/ppermute | solution.py:22
  19.6 2.0 %collective-permute-done.5 = bf16[144,128]{1,0:T(8,128)(2,1)S(1)} collective-permute-done((bf16[144,128]{1,0:T(8,128)(2,1)S(1)}, bf16[144,128]{1,0:T(8,128)(2,1)S(1)}, u32[]{:S(2)}, u32[]{:S(2)}) %collective-permute-start.5) | collective-permute-done | bytes 36896 | tf_op jit(solution)/shard_map/s_col2/ppermute | solution.py:22
  21.6 2.8 %collective-permute-start.10 = (bf16[2,144,128]{2,1,0:T(8,128)(2,1)S(1)}, bf16[2,144,128]{2,1,0:T(8,128)(2,1)S(1)}, u32[]{:S(2)}, u32[]{:S(2)}) collective-permute-start(bf16[2,144,128]{2,1,0:T(8,128)(2,1)S(1)} %pad_maximum_fusion.5), channel_id=1, source_target_pairs={{0,12},{1,13},{2,14},{3,15},{4,8},{5,9},{6,10},{7,11},{8,4},{9,5},... | collective-permute-start | bytes 221192 | tf_op jit(solution)/shard_map/s_col12/ppermute | solution.py:22
  24.4 0.3 collective-permute-start.9
  24.8 0.3 collective-permute-start.8
  25.2 0.0 copy-start.1
  25.2 0.0 copy-start.2
  25.2 0.0 copy-start.4
  25.2 0.0 copy-start.5
  25.2 0.9 collective-permute-start.7
  26.1 0.8 collective-permute-start.6
  26.9 2.3 %collective-permute-done.9 = bf16[2,144,128]{2,1,0:T(8,128)(2,1)S(1)} collective-permute-done((bf16[2,144,128]{2,1,0:T(8,128)(2,1)S(1)}, bf16[2,144,128]{2,1,0:T(8,128)(2,1)S(1)}, u32[]{:S(2)}, u32[]{:S(2)}) %collective-permute-start.9) | collective-permute-done | bytes 73760 | tf_op jit(solution)/shard_map/s_col8/ppermute | solution.py:22
  29.2 1.5 %collective-permute-done.7.right2b = bf16[2,272,128]{2,1,0:T(8,128)(2,1)S(1)} collective-permute-done((bf16[2,272,128]{2,1,0:T(8,128)(2,1)S(1)}, bf16[2,272,128]{2,1,0:T(8,128)(2,1)S(1)}, u32[]{:S(2)}, u32[]{:S(2)}) %collective-permute-start.7) | collective-permute-done | bytes 139296 | tf_op jit(solution)/shard_map/s_row12/ppermute | solution.py:22
  30.7 5.5 %collective-permute-start.11 = (bf16[8,144,128]{2,1,0:T(8,128)(2,1)S(1)}, bf16[8,144,128]{2,1,0:T(8,128)(2,1)S(1)}, u32[]{:S(2)}, u32[]{:S(2)}) collective-permute-start(bf16[8,144,128]{2,1,0:T(8,128)(2,1)S(1)} %pad_maximum_fusion.left0), channel_id=1, source_target_pairs={{0,1},{1,0},{2,3},{3,2},{4,5},{5,4},{6,7},{7,6},{8,9},{9,8},{10,11... | collective-permute-start | bytes 884744 | tf_op jit(solution)/shard_map/s_col1/ppermute | solution.py:22
  36.2 0.1 pad_add_fusion.at_ref
  36.3 1.1 %collective-permute-done.11.left1 = bf16[8,144,128]{2,1,0:T(8,128)(2,1)S(1)} collective-permute-done((bf16[8,144,128]{2,1,0:T(8,128)(2,1)S(1)}, bf16[8,144,128]{2,1,0:T(8,128)(2,1)S(1)}, u32[]{:S(2)}, u32[]{:S(2)}) %collective-permute-start.11) | collective-permute-done | bytes 294944 | tf_op jit(solution)/shard_map/s_col1/ppermute | solution.py:22
  37.4 19.5 %shard_map.129 = (bf16[1344,128]{1,0:T(8,128)(2,1)S(1)}, bf16[1344,128]{1,0:T(8,128)(2,1)S(1)}, bf16[4,256,128]{2,1,0:T(8,128)(2,1)S(1)}, bf16[4,256,128]{2,1,0:...) custom-call(s32[2]{0:T(128)S(1)} %pad_add_fusion.at_ref, ...), custom_call_target="tpu_custom_call" | custom-call | flops 800000000 | bytes 5000000 | tf_op jit(solution)/shard_map/pallas_call | solution.py:353
  57.0 0.5 collective-permute-start.12
  57.4 0.4 collective-permute-start.13
  57.8 2.3 %collective-permute-start.14 = (bf16[4,256,128]{2,1,0:T(8,128)(2,1)S(1)}, bf16[4,256,128]{2,1,0:T(8,128)(2,1)S(1)}, u32[]{:S(2)}, u32[]{:S(2)}) collective-permute-start(bf16[4,256,128]{2,1,0:T(8,128)(2,1)S(1)} %get-tuple-element.39), channel_id=1, source_target_pairs={{0,192},{16,208},{32,224},{48,240},{64,128},{80,144},{96,160},{112... | collective-permute-start | bytes 786440 | tf_op jit(solution)/shard_map/s_row12/ppermute | solution.py:22
  60.1 0.1 convert_add_fusion
  60.3 1.4 %collective-permute-start.15 = (bf16[576,128]{1,0:T(8,128)(2,1)S(1)}, bf16[576,128]{1,0:T(8,128)(2,1)S(1)}, u32[]{:S(2)}, u32[]{:S(2)}) collective-permute-start(bf16[576,128]{1,0:T(8,128)(2,1)S(1)} %get-tuple-element.66), channel_id=1, source_target_pairs={{0,4},{1,5},{2,6},{3,7},{4,0},{5,1},{6,2},{7,3},{8,12},{9,13},{10,... | collective-permute-start | bytes 442376 | tf_op jit(solution)/shard_map/s_col4/ppermute | solution.py:22
  61.7 2.0 %collective-permute-start.17 = (bf16[576,128]{1,0:T(8,128)(2,1)S(1)}, bf16[576,128]{1,0:T(8,128)(2,1)S(1)}, u32[]{:S(2)}, u32[]{:S(2)}) collective-permute-start(bf16[576,128]{1,0:T(8,128)(2,1)S(1)} %concatenate.37), channel_id=1, source_target_pairs={{0,12},{1,13},{2,14},{3,15},{4,8},{5,9},{6,10},{7,11},{8,4},{9,5},... | collective-permute-start | bytes 442376 | tf_op jit(solution)/shard_map/s_col12/ppermute | solution.py:22
  63.6 0.8 collective-permute-start.16
  64.5 0.6 collective-permute-done.15
  65.1 0.1 collective-permute-done.13
  65.2 1.3 %collective-permute-done.14 = bf16[4,256,128]{2,1,0:T(8,128)(2,1)S(1)} collective-permute-done((bf16[4,256,128]{2,1,0:T(8,128)(2,1)S(1)}, bf16[4,256,128]{2,1,0:T(8,128)(2,1)S(1)}, u32[]{:S(2)}, u32[]{:S(2)}) %collective-permute-start.14) | collective-permute-done | bytes 262176 | tf_op jit(solution)/shard_map/s_row12/ppermute | solution.py:22
  66.5 2.6 %collective-permute-done.17 = bf16[576,128]{1,0:T(8,128)(2,1)S(1)} collective-permute-done((bf16[576,128]{1,0:T(8,128)(2,1)S(1)}, bf16[576,128]{1,0:T(8,128)(2,1)S(1)}, u32[]{:S(2)}, u32[]{:S(2)}) %collective-permute-start.17) | collective-permute-done | bytes 147488 | tf_op jit(solution)/shard_map/s_col12/ppermute | solution.py:22
  69.1 1.8 %collective-permute-done.16 = bf16[576,128]{1,0:T(8,128)(2,1)S(1)} collective-permute-done((bf16[576,128]{1,0:T(8,128)(2,1)S(1)}, bf16[576,128]{1,0:T(8,128)(2,1)S(1)}, u32[]{:S(2)}, u32[]{:S(2)}) %collective-permute-start.16) | collective-permute-done | bytes 147488 | tf_op jit(solution)/shard_map/s_col8/ppermute | solution.py:22
  70.9 0.1 fusion
  70.9 0.1 convert_add_fusion.1
  71.1 4.5 %collective-permute-start.18 = (bf16[448,128]{1,0:T(8,128)(2,1)S(1)}, bf16[448,128]{1,0:T(8,128)(2,1)S(1)}, u32[]{:S(2)}, u32[]{:S(2)}) collective-permute-start(bf16[448,128]{1,0:T(8,128)(2,1)S(1)} %slice.132), channel_id=1, source_target_pairs={{0,2},{1,3},{2,0},{3,1},{4,6},{5,7},{6,4},{7,5},{8,10},{9,11},{10,... | collective-permute-start | bytes 344072 | tf_op jit(solution)/shard_map/s_col2/ppermute | solution.py:22
  75.6 0.4 collective-permute-start.19
  76.0 0.5 collective-permute-start.20
  76.5 2.4 %collective-permute-done.18 = bf16[448,128]{1,0:T(8,128)(2,1)S(1)} collective-permute-done((bf16[448,128]{1,0:T(8,128)(2,1)S(1)}, bf16[448,128]{1,0:T(8,128)(2,1)S(1)}, u32[]{:S(2)}, u32[]{:S(2)}) %collective-permute-start.18) | collective-permute-done | bytes 114720 | tf_op jit(solution)/shard_map/s_col2/ppermute | solution.py:22
  78.9 2.0 %collective-permute-done.19 = bf16[2,256,128]{2,1,0:T(8,128)(2,1)S(1)} collective-permute-done((bf16[2,256,128]{2,1,0:T(8,128)(2,1)S(1)}, bf16[2,256,128]{2,1,0:T(8,128)(2,1)S(1)}, u32[]{:S(2)}, u32[]{:S(2)}) %collective-permute-start.19) | collective-permute-done | bytes 131104 | tf_op jit(solution)/shard_map/s_row12/ppermute | solution.py:22
  81.1 1.5 %collective-permute-start.23 = (bf16[320,128]{1,0:T(8,128)(2,1)S(1)}, bf16[320,128]{1,0:T(8,128)(2,1)S(1)}, u32[]{:S(2)}, u32[]{:S(2)}) collective-permute-start(bf16[320,128]{1,0:T(8,128)(2,1)S(1)} %fusion.2), channel_id=1, source_target_pairs={{0,192},{16,208},{32,224},{48,240},{64,128},{80,144},{96,160},{112... | collective-permute-start | bytes 245768 | tf_op jit(solution)/shard_map/s_row12/ppermute | solution.py:22
  82.6 1.8 %collective-permute-start.21 = (bf16[320,128]{1,0:T(8,128)(2,1)S(1)}, bf16[320,128]{1,0:T(8,128)(2,1)S(1)}, u32[]{:S(2)}, u32[]{:S(2)}) collective-permute-start(bf16[320,128]{1,0:T(8,128)(2,1)S(1)} %fusion.2), channel_id=1, source_target_pairs={{0,64},{16,80},{32,96},{48,112},{64,0},{80,16},{96,32},{112,48},{1... | collective-permute-start | bytes 245768 | tf_op jit(solution)/shard_map/s_row4/ppermute | solution.py:22
  84.4 0.6 slice_add_fusion.3
  85.0 0.6 collective-permute-done.23
  85.6 1.7 %collective-permute-done.22 = bf16[320,128]{1,0:T(8,128)(2,1)S(1)} collective-permute-done((bf16[320,128]{1,0:T(8,128)(2,1)S(1)}, bf16[320,128]{1,0:T(8,128)(2,1)S(1)}, u32[]{:S(2)}, u32[]{:S(2)}) %collective-permute-start.22) | collective-permute-done | bytes 81952 | tf_op jit(solution)/shard_map/s_row8/ppermute | solution.py:22
  87.4 1.6 %collective-permute-start.29 = (bf16[320,128]{1,0:T(8,128)(2,1)S(1)}, bf16[320,128]{1,0:T(8,128)(2,1)S(1)}, u32[]{:S(2)}, u32[]{:S(2)}) collective-permute-start(bf16[320,128]{1,0:T(8,128)(2,1)S(1)} %add_convert_fusion.1), channel_id=1, source_target_pairs={{0,48},{16,32},{32,16},{48,0},{64,112},{80,96},{96,80},{112,64},{1... | collective-permute-start | bytes 245768 | tf_op jit(solution)/shard_map/s_row3/ppermute | solution.py:22
  89.0 0.5 collective-permute-start.28
  89.5 1.5 %collective-permute-start.27 = (bf16[320,128]{1,0:T(8,128)(2,1)S(1)}, bf16[320,128]{1,0:T(8,128)(2,1)S(1)}, u32[]{:S(2)}, u32[]{:S(2)}) collective-permute-start(bf16[320,128]{1,0:T(8,128)(2,1)S(1)} %add_convert_fusion.1), channel_id=1, source_target_pairs={{0,16},{16,0},{32,48},{48,32},{64,80},{80,64},{96,112},{112,96},{1... | collective-permute-start | bytes 245768 | tf_op jit(solution)/shard_map/s_row1/ppermute | solution.py:22
  91.1 0.1 collective-permute-start.24
  91.2 1.6 %collective-permute-start.26 = (bf16[256,128]{1,0:T(8,128)(2,1)S(1)}, bf16[256,128]{1,0:T(8,128)(2,1)S(1)}, u32[]{:S(2)}, u32[]{:S(2)}) collective-permute-start(bf16[256,128]{1,0:T(8,128)(2,1)S(1)} %get-tuple-element.61), channel_id=1, source_target_pairs={{0,48},{16,32},{32,16},{48,0},{64,112},{80,96},{96,80},{112,64},{1... | collective-permute-start | bytes 196616 | tf_op jit(solution)/shard_map/s_row3/ppermute | solution.py:22
  92.7 1.1 %collective-permute-start.25 = (bf16[256,128]{1,0:T(8,128)(2,1)S(1)}, bf16[256,128]{1,0:T(8,128)(2,1)S(1)}, u32[]{:S(2)}, u32[]{:S(2)}) collective-permute-start(bf16[256,128]{1,0:T(8,128)(2,1)S(1)} %get-tuple-element.62), channel_id=1, source_target_pairs={{0,32},{16,48},{32,0},{48,16},{64,96},{80,112},{96,64},{112,80},{1... | collective-permute-start | bytes 196616 | tf_op jit(solution)/shard_map/s_row2/ppermute | solution.py:22
  93.8 0.6 collective-permute-done.28
  94.5 7.5 %collective-permute-start.30 = (bf16[320,128]{1,0:T(8,128)(2,1)S(1)}, bf16[320,128]{1,0:T(8,128)(2,1)S(1)}, u32[]{:S(2)}, u32[]{:S(2)}) collective-permute-start(bf16[320,128]{1,0:T(8,128)(2,1)S(1)} %add_convert_fusion), channel_id=1, source_target_pairs={{0,1},{1,0},{2,3},{3,2},{4,5},{5,4},{6,7},{7,6},{8,9},{9,8},{10,11... | collective-permute-start | bytes 245768 | tf_op jit(solution)/shard_map/s_col1/ppermute | solution.py:22
  102.0 0.7 copy.18
  102.7 0.2 collective-permute-done.30
  102.9 0.6 maximum_convert_fusion.1
  103.6 0.7 slice.105
  (60 shorter events, 0.7 us)
Async XLA Ops:
  0.6 0.9 copy-start.6
  1.6 5.6 %copy-start.8 = (s32[8,16]{1,0:T(8,128)S(1)}, s32[8,16]{1,0:T(8,128)}, u32[]{:S(2)}) copy-start(s32[8,16]{1,0:T(8,128)} %param.12) | copy-start | bytes 1540
  1.6 5.7 %copy-start.7 = (bf16[8,16,128]{2,1,0:T(8,128)(2,1)S(1)}, bf16[8,16,128]{2,1,0:T(8,128)(2,1)}, u32[]{:S(2)}) copy-start(bf16[8,16,128]{2,1,0:T(8,128)(2,1)} %param.10) | copy-start | bytes 98308
  1.6 5.7 %collective-permute-start.1 = (bf16[272,128]{1,0:T(8,128)(2,1)S(1)}, bf16[272,128]{1,0:T(8,128)(2,1)S(1)}, u32[]{:S(2)}, u32[]{:S(2)}) collective-permute-start(bf16[272,128]{1,0:T(8,128)(2,1)S(1)} %get-tuple-element.68), channel_id=1, source_target_pairs={{0,32},{16,48},{32,0},{48,16},{64,96},{80,112},{96,64},{112,80},{1... | collective-permute-start | bytes 208904 | tf_op jit(solution)/shard_map/s_row2/ppermute | solution.py:22
  5.5 3.8 %collective-permute-start = (bf16[272,128]{1,0:T(8,128)(2,1)S(1)}, bf16[272,128]{1,0:T(8,128)(2,1)S(1)}, u32[]{:S(2)}, u32[]{:S(2)}) collective-permute-start(bf16[272,128]{1,0:T(8,128)(2,1)S(1)} %get-tuple-element.68), channel_id=1, source_target_pairs={{0,16},{16,0},{32,48},{48,32},{64,80},{80,64},{96,112},{112,96},{1... | collective-permute-start | bytes 208904 | tf_op jit(solution)/shard_map/s_row1/ppermute | solution.py:22
  7.2 5.1 %collective-permute-start.2 = (bf16[272,128]{1,0:T(8,128)(2,1)S(1)}, bf16[272,128]{1,0:T(8,128)(2,1)S(1)}, u32[]{:S(2)}, u32[]{:S(2)}) collective-permute-start(bf16[272,128]{1,0:T(8,128)(2,1)S(1)} %get-tuple-element.68), channel_id=1, source_target_pairs={{0,48},{16,32},{32,16},{48,0},{64,112},{80,96},{96,80},{112,64},{1... | collective-permute-start | bytes 208904 | tf_op jit(solution)/shard_map/s_row3/ppermute | solution.py:22
  12.3 9.3 %collective-permute-start.4 = (bf16[4,272,128]{2,1,0:T(8,128)(2,1)S(1)}, bf16[4,272,128]{2,1,0:T(8,128)(2,1)S(1)}, u32[]{:S(2)}, u32[]{:S(2)}) collective-permute-start(bf16[4,272,128]{2,1,0:T(8,128)(2,1)S(1)} %pad_maximum_fusion.1.right0), channel_id=1, source_target_pairs={{0,192},{16,208},{32,224},{48,240},{64,128},{80,144},{96,160},{112... | collective-permute-start | bytes 835592 | tf_op jit(solution)/shard_map/s_row12/ppermute | solution.py:22
  14.9 6.7 %collective-permute-start.3 = (bf16[4,272,128]{2,1,0:T(8,128)(2,1)S(1)}, bf16[4,272,128]{2,1,0:T(8,128)(2,1)S(1)}, u32[]{:S(2)}, u32[]{:S(2)}) collective-permute-start(bf16[4,272,128]{2,1,0:T(8,128)(2,1)S(1)} %pad_maximum_fusion.1.right0), channel_id=1, source_target_pairs={{0,64},{16,80},{32,96},{48,112},{64,0},{80,16},{96,32},{112,48},{1... | collective-permute-start | bytes 835592 | tf_op jit(solution)/shard_map/s_row4/ppermute | solution.py:22
  14.9 6.7 %collective-permute-start.5 = (bf16[144,128]{1,0:T(8,128)(2,1)S(1)}, bf16[144,128]{1,0:T(8,128)(2,1)S(1)}, u32[]{:S(2)}, u32[]{:S(2)}) collective-permute-start(bf16[144,128]{1,0:T(8,128)(2,1)S(1)} %fusion.7), channel_id=1, source_target_pairs={{0,2},{1,3},{2,0},{3,1},{4,6},{5,7},{6,4},{7,5},{8,10},{9,11},{10,... | collective-permute-start | bytes 110600 | tf_op jit(solution)/shard_map/s_col2/ppermute | solution.py:22
  21.6 5.3 %collective-permute-start.10 = (bf16[2,144,128]{2,1,0:T(8,128)(2,1)S(1)}, bf16[2,144,128]{2,1,0:T(8,128)(2,1)S(1)}, u32[]{:S(2)}, u32[]{:S(2)}) collective-permute-start(bf16[2,144,128]{2,1,0:T(8,128)(2,1)S(1)} %pad_maximum_fusion.5), channel_id=1, source_target_pairs={{0,12},{1,13},{2,14},{3,15},{4,8},{5,9},{6,10},{7,11},{8,4},{9,5},... | collective-permute-start | bytes 221192 | tf_op jit(solution)/shard_map/s_col12/ppermute | solution.py:22
  24.4 4.7 %collective-permute-start.9 = (bf16[2,144,128]{2,1,0:T(8,128)(2,1)S(1)}, bf16[2,144,128]{2,1,0:T(8,128)(2,1)S(1)}, u32[]{:S(2)}, u32[]{:S(2)}) collective-permute-start(bf16[2,144,128]{2,1,0:T(8,128)(2,1)S(1)} %pad_maximum_fusion.5), channel_id=1, source_target_pairs={{0,8},{1,9},{2,10},{3,11},{4,12},{5,13},{6,14},{7,15},{8,0},{9,1},... | collective-permute-start | bytes 221192 | tf_op jit(solution)/shard_map/s_col8/ppermute | solution.py:22
  24.8 4.4 %collective-permute-start.8 = (bf16[2,144,128]{2,1,0:T(8,128)(2,1)S(1)}, bf16[2,144,128]{2,1,0:T(8,128)(2,1)S(1)}, u32[]{:S(2)}, u32[]{:S(2)}) collective-permute-start(bf16[2,144,128]{2,1,0:T(8,128)(2,1)S(1)} %pad_maximum_fusion.5), channel_id=1, source_target_pairs={{0,4},{1,5},{2,6},{3,7},{4,0},{5,1},{6,2},{7,3},{8,12},{9,13},{10,... | collective-permute-start | bytes 221192 | tf_op jit(solution)/shard_map/s_col4/ppermute | solution.py:22
  25.1 12.3 %copy-start = (bf16[8,16,128]{2,1,0:T(8,128)(2,1)S(1)}, bf16[8,16,128]{2,1,0:T(8,128)(2,1)}, u32[]{:S(2)}) copy-start(bf16[8,16,128]{2,1,0:T(8,128)(2,1)} %param.14) | copy-start | bytes 98308
  25.2 12.2 %copy-start.1 = (bf16[128,128]{1,0:T(8,128)(2,1)S(1)}, bf16[128,128]{1,0:T(8,128)(2,1)}, u32[]{:S(2)}) copy-start(bf16[128,128]{1,0:T(8,128)(2,1)} %wq_hbm.1) | copy-start | bytes 98308
  25.2 12.2 %copy-start.2 = (bf16[128,128]{1,0:T(8,128)(2,1)S(1)}, bf16[128,128]{1,0:T(8,128)(2,1)}, u32[]{:S(2)}) copy-start(bf16[128,128]{1,0:T(8,128)(2,1)} %wk_hbm.1) | copy-start | bytes 98308
  25.2 12.2 %copy-start.3 = (bf16[128,128]{1,0:T(8,128)(2,1)S(1)}, bf16[128,128]{1,0:T(8,128)(2,1)}, u32[]{:S(2)}) copy-start(bf16[128,128]{1,0:T(8,128)(2,1)} %wl_hbm.1) | copy-start | bytes 98308
  25.2 12.2 %copy-start.4 = (bf16[128,128]{1,0:T(8,128)(2,1)S(1)}, bf16[128,128]{1,0:T(8,128)(2,1)}, u32[]{:S(2)}) copy-start(bf16[128,128]{1,0:T(8,128)(2,1)} %wr_hbm.1) | copy-start | bytes 98308
  25.2 12.2 %copy-start.5 = (bf16[128,128]{1,0:T(8,128)(2,1)S(1)}, bf16[128,128]{1,0:T(8,128)(2,1)}, u32[]{:S(2)}) copy-start(bf16[128,128]{1,0:T(8,128)(2,1)} %wo_hbm.1) | copy-start | bytes 98308
  25.2 5.5 %collective-permute-start.7 = (bf16[2,272,128]{2,1,0:T(8,128)(2,1)S(1)}, bf16[2,272,128]{2,1,0:T(8,128)(2,1)S(1)}, u32[]{:S(2)}, u32[]{:S(2)}) collective-permute-start(bf16[2,272,128]{2,1,0:T(8,128)(2,1)S(1)} %slice.72), channel_id=1, source_target_pairs={{0,192},{16,208},{32,224},{48,240},{64,128},{80,144},{96,160},{112... | collective-permute-start | bytes 417800 | tf_op jit(solution)/shard_map/s_row12/ppermute | solution.py:22
  26.1 4.6 %collective-permute-start.6 = (bf16[2,272,128]{2,1,0:T(8,128)(2,1)S(1)}, bf16[2,272,128]{2,1,0:T(8,128)(2,1)S(1)}, u32[]{:S(2)}, u32[]{:S(2)}) collective-permute-start(bf16[2,272,128]{2,1,0:T(8,128)(2,1)S(1)} %slice.71), channel_id=1, source_target_pairs={{0,64},{16,80},{32,96},{48,112},{64,0},{80,16},{96,32},{112,48},{1... | collective-permute-start | bytes 417800 | tf_op jit(solution)/shard_map/s_row4/ppermute | solution.py:22
  30.7 6.7 %collective-permute-start.11 = (bf16[8,144,128]{2,1,0:T(8,128)(2,1)S(1)}, bf16[8,144,128]{2,1,0:T(8,128)(2,1)S(1)}, u32[]{:S(2)}, u32[]{:S(2)}) collective-permute-start(bf16[8,144,128]{2,1,0:T(8,128)(2,1)S(1)} %pad_maximum_fusion.left0), channel_id=1, source_target_pairs={{0,1},{1,0},{2,3},{3,2},{4,5},{5,4},{6,7},{7,6},{8,9},{9,8},{10,11... | collective-permute-start | bytes 884744 | tf_op jit(solution)/shard_map/s_col1/ppermute | solution.py:22
  57.0 3.1 %collective-permute-start.12 = (bf16[1344,128]{1,0:T(8,128)(2,1)S(1)}, bf16[1344,128]{1,0:T(8,128)(2,1)S(1)}, u32[]{:S(2)}, u32[]{:S(2)}) collective-permute-start(bf16[1344,128]{1,0:T(8,128)(2,1)S(1)} %get-tuple-element.37), channel_id=1, source_target_pairs={{0,1},{1,0},{2,3},{3,2},{4,5},{5,4},{6,7},{7,6},{8,9},{9,8},{10,11... | collective-permute-start | bytes 1032200 | tf_op jit(solution)/shard_map/s_col1/ppermute | solution.py:22
  57.4 7.8 %collective-permute-start.13 = (bf16[4,256,128]{2,1,0:T(8,128)(2,1)S(1)}, bf16[4,256,128]{2,1,0:T(8,128)(2,1)S(1)}, u32[]{:S(2)}, u32[]{:S(2)}) collective-permute-start(bf16[4,256,128]{2,1,0:T(8,128)(2,1)S(1)} %get-tuple-element.38), channel_id=1, source_target_pairs={{0,64},{16,80},{32,96},{48,112},{64,0},{80,16},{96,32},{112,48},{1... | collective-permute-start | bytes 786440 | tf_op jit(solution)/shard_map/s_row4/ppermute | solution.py:22
  57.8 8.7 %collective-permute-start.14 = (bf16[4,256,128]{2,1,0:T(8,128)(2,1)S(1)}, bf16[4,256,128]{2,1,0:T(8,128)(2,1)S(1)}, u32[]{:S(2)}, u32[]{:S(2)}) collective-permute-start(bf16[4,256,128]{2,1,0:T(8,128)(2,1)S(1)} %get-tuple-element.39), channel_id=1, source_target_pairs={{0,192},{16,208},{32,224},{48,240},{64,128},{80,144},{96,160},{112... | collective-permute-start | bytes 786440 | tf_op jit(solution)/shard_map/s_row12/ppermute | solution.py:22
  60.3 4.8 %collective-permute-start.15 = (bf16[576,128]{1,0:T(8,128)(2,1)S(1)}, bf16[576,128]{1,0:T(8,128)(2,1)S(1)}, u32[]{:S(2)}, u32[]{:S(2)}) collective-permute-start(bf16[576,128]{1,0:T(8,128)(2,1)S(1)} %get-tuple-element.66), channel_id=1, source_target_pairs={{0,4},{1,5},{2,6},{3,7},{4,0},{5,1},{6,2},{7,3},{8,12},{9,13},{10,... | collective-permute-start | bytes 442376 | tf_op jit(solution)/shard_map/s_col4/ppermute | solution.py:22
  61.7 7.4 %collective-permute-start.17 = (bf16[576,128]{1,0:T(8,128)(2,1)S(1)}, bf16[576,128]{1,0:T(8,128)(2,1)S(1)}, u32[]{:S(2)}, u32[]{:S(2)}) collective-permute-start(bf16[576,128]{1,0:T(8,128)(2,1)S(1)} %concatenate.37), channel_id=1, source_target_pairs={{0,12},{1,13},{2,14},{3,15},{4,8},{5,9},{6,10},{7,11},{8,4},{9,5},... | collective-permute-start | bytes 442376 | tf_op jit(solution)/shard_map/s_col12/ppermute | solution.py:22
  63.6 7.2 %collective-permute-start.16 = (bf16[576,128]{1,0:T(8,128)(2,1)S(1)}, bf16[576,128]{1,0:T(8,128)(2,1)S(1)}, u32[]{:S(2)}, u32[]{:S(2)}) collective-permute-start(bf16[576,128]{1,0:T(8,128)(2,1)S(1)} %get-tuple-element.65), channel_id=1, source_target_pairs={{0,8},{1,9},{2,10},{3,11},{4,12},{5,13},{6,14},{7,15},{8,0},{9,1},... | collective-permute-start | bytes 442376 | tf_op jit(solution)/shard_map/s_col8/ppermute | solution.py:22
  71.1 7.7 %collective-permute-start.18 = (bf16[448,128]{1,0:T(8,128)(2,1)S(1)}, bf16[448,128]{1,0:T(8,128)(2,1)S(1)}, u32[]{:S(2)}, u32[]{:S(2)}) collective-permute-start(bf16[448,128]{1,0:T(8,128)(2,1)S(1)} %slice.132), channel_id=1, source_target_pairs={{0,2},{1,3},{2,0},{3,1},{4,6},{5,7},{6,4},{7,5},{8,10},{9,11},{10,... | collective-permute-start | bytes 344072 | tf_op jit(solution)/shard_map/s_col2/ppermute | solution.py:22
  75.6 5.3 %collective-permute-start.19 = (bf16[2,256,128]{2,1,0:T(8,128)(2,1)S(1)}, bf16[2,256,128]{2,1,0:T(8,128)(2,1)S(1)}, u32[]{:S(2)}, u32[]{:S(2)}) collective-permute-start(bf16[2,256,128]{2,1,0:T(8,128)(2,1)S(1)} %slice.131), channel_id=1, source_target_pairs={{0,192},{16,208},{32,224},{48,240},{64,128},{80,144},{96,160},{112... | collective-permute-start | bytes 393224 | tf_op jit(solution)/shard_map/s_row12/ppermute | solution.py:22
  76.0 5.0 %collective-permute-start.20 = (bf16[2,256,128]{2,1,0:T(8,128)(2,1)S(1)}, bf16[2,256,128]{2,1,0:T(8,128)(2,1)S(1)}, u32[]{:S(2)}, u32[]{:S(2)}) collective-permute-start(bf16[2,256,128]{2,1,0:T(8,128)(2,1)S(1)} %slice.130), channel_id=1, source_target_pairs={{0,64},{16,80},{32,96},{48,112},{64,0},{80,16},{96,32},{112,48},{1... | collective-permute-start | bytes 393224 | tf_op jit(solution)/shard_map/s_row4/ppermute | solution.py:22
  81.1 4.6 %collective-permute-start.23 = (bf16[320,128]{1,0:T(8,128)(2,1)S(1)}, bf16[320,128]{1,0:T(8,128)(2,1)S(1)}, u32[]{:S(2)}, u32[]{:S(2)}) collective-permute-start(bf16[320,128]{1,0:T(8,128)(2,1)S(1)} %fusion.2), channel_id=1, source_target_pairs={{0,192},{16,208},{32,224},{48,240},{64,128},{80,144},{96,160},{112... | collective-permute-start | bytes 245768 | tf_op jit(solution)/shard_map/s_row12/ppermute | solution.py:22
  82.6 4.8 %collective-permute-start.22 = (bf16[320,128]{1,0:T(8,128)(2,1)S(1)}, bf16[320,128]{1,0:T(8,128)(2,1)S(1)}, u32[]{:S(2)}, u32[]{:S(2)}) collective-permute-start(bf16[320,128]{1,0:T(8,128)(2,1)S(1)} %fusion.2), channel_id=1, source_target_pairs={{0,128},{16,144},{32,160},{48,176},{64,192},{80,208},{96,224},{112... | collective-permute-start | bytes 245768 | tf_op jit(solution)/shard_map/s_row8/ppermute | solution.py:22
  82.6 4.8 %collective-permute-start.21 = (bf16[320,128]{1,0:T(8,128)(2,1)S(1)}, bf16[320,128]{1,0:T(8,128)(2,1)S(1)}, u32[]{:S(2)}, u32[]{:S(2)}) collective-permute-start(bf16[320,128]{1,0:T(8,128)(2,1)S(1)} %fusion.2), channel_id=1, source_target_pairs={{0,64},{16,80},{32,96},{48,112},{64,0},{80,16},{96,32},{112,48},{1... | collective-permute-start | bytes 245768 | tf_op jit(solution)/shard_map/s_row4/ppermute | solution.py:22
  87.4 5.3 %collective-permute-start.29 = (bf16[320,128]{1,0:T(8,128)(2,1)S(1)}, bf16[320,128]{1,0:T(8,128)(2,1)S(1)}, u32[]{:S(2)}, u32[]{:S(2)}) collective-permute-start(bf16[320,128]{1,0:T(8,128)(2,1)S(1)} %add_convert_fusion.1), channel_id=1, source_target_pairs={{0,48},{16,32},{32,16},{48,0},{64,112},{80,96},{96,80},{112,64},{1... | collective-permute-start | bytes 245768 | tf_op jit(solution)/shard_map/s_row3/ppermute | solution.py:22
  89.0 5.4 %collective-permute-start.28 = (bf16[320,128]{1,0:T(8,128)(2,1)S(1)}, bf16[320,128]{1,0:T(8,128)(2,1)S(1)}, u32[]{:S(2)}, u32[]{:S(2)}) collective-permute-start(bf16[320,128]{1,0:T(8,128)(2,1)S(1)} %add_convert_fusion.1), channel_id=1, source_target_pairs={{0,32},{16,48},{32,0},{48,16},{64,96},{80,112},{96,64},{112,80},{1... | collective-permute-start | bytes 245768 | tf_op jit(solution)/shard_map/s_row2/ppermute | solution.py:22
  89.5 4.9 %collective-permute-start.27 = (bf16[320,128]{1,0:T(8,128)(2,1)S(1)}, bf16[320,128]{1,0:T(8,128)(2,1)S(1)}, u32[]{:S(2)}, u32[]{:S(2)}) collective-permute-start(bf16[320,128]{1,0:T(8,128)(2,1)S(1)} %add_convert_fusion.1), channel_id=1, source_target_pairs={{0,16},{16,0},{32,48},{48,32},{64,80},{80,64},{96,112},{112,96},{1... | collective-permute-start | bytes 245768 | tf_op jit(solution)/shard_map/s_row1/ppermute | solution.py:22
  91.1 10.9 %collective-permute-start.24 = (bf16[256,128]{1,0:T(8,128)(2,1)S(1)}, bf16[256,128]{1,0:T(8,128)(2,1)S(1)}, u32[]{:S(2)}, u32[]{:S(2)}) collective-permute-start(bf16[256,128]{1,0:T(8,128)(2,1)S(1)} %get-tuple-element.60), channel_id=1, source_target_pairs={{0,16},{16,0},{32,48},{48,32},{64,80},{80,64},{96,112},{112,96},{1... | collective-permute-start | bytes 196616 | tf_op jit(solution)/shard_map/s_row1/ppermute | solution.py:22
  91.2 10.8 %collective-permute-start.26 = (bf16[256,128]{1,0:T(8,128)(2,1)S(1)}, bf16[256,128]{1,0:T(8,128)(2,1)S(1)}, u32[]{:S(2)}, u32[]{:S(2)}) collective-permute-start(bf16[256,128]{1,0:T(8,128)(2,1)S(1)} %get-tuple-element.61), channel_id=1, source_target_pairs={{0,48},{16,32},{32,16},{48,0},{64,112},{80,96},{96,80},{112,64},{1... | collective-permute-start | bytes 196616 | tf_op jit(solution)/shard_map/s_row3/ppermute | solution.py:22
  92.7 9.3 %collective-permute-start.25 = (bf16[256,128]{1,0:T(8,128)(2,1)S(1)}, bf16[256,128]{1,0:T(8,128)(2,1)S(1)}, u32[]{:S(2)}, u32[]{:S(2)}) collective-permute-start(bf16[256,128]{1,0:T(8,128)(2,1)S(1)} %get-tuple-element.62), channel_id=1, source_target_pairs={{0,32},{16,48},{32,0},{48,16},{64,96},{80,112},{96,64},{112,80},{1... | collective-permute-start | bytes 196616 | tf_op jit(solution)/shard_map/s_row2/ppermute | solution.py:22
  94.5 8.5 %collective-permute-start.30 = (bf16[320,128]{1,0:T(8,128)(2,1)S(1)}, bf16[320,128]{1,0:T(8,128)(2,1)S(1)}, u32[]{:S(2)}, u32[]{:S(2)}) collective-permute-start(bf16[320,128]{1,0:T(8,128)(2,1)S(1)} %add_convert_fusion), channel_id=1, source_target_pairs={{0,1},{1,0},{2,3},{3,2},{4,5},{5,4},{6,7},{7,6},{8,9},{9,8},{10,11... | collective-permute-start | bytes 245768 | tf_op jit(solution)/shard_map/s_col1/ppermute | solution.py:22

commit v2 on v1

--- a/solution.py
+++ b/solution.py
@@ -11,6 +11,9 @@
 HEAD_DIM = 32
 BF = jnp.bfloat16
 F32 = jnp.float32
+
+
+LINES = [[4 * x + z for z in range(4)] for x in range(4)]
 
 
 def flip(k):
@@ -193,13 +196,13 @@
         ql[i] = nt(wl, xl[i].reshape(256, 128)).astype(BF).astype(F32)
         return 0
 
-    lax.fori_loop(0, 8, project_left, 0, unroll=4)
+    lax.fori_loop(0, 8, project_left, 0, unroll=8)
 
     def project_right(j, _):
         kr[j] = nt(wr, xr[j].reshape(256, 128)).astype(BF).astype(F32)
         return 0
 
-    lax.fori_loop(0, 16, project_right, 0, unroll=4)
+    lax.fori_loop(0, 16, project_right, 0, unroll=8)
     cot = cot_ref[...]
     pick = (
         lax.broadcasted_iota(jnp.int32, (16, 2048), 1) // 128
@@ -266,18 +269,16 @@
             pb[i, rows, :] = prob.astype(BF).astype(F32)
             sb[i, rows, :] = grad.astype(BF).astype(F32)
 
-    agree = agree[:, :128], agree[:, 128:]
-
     def gradients(t, _):
         h = t // 4
         rows = pl.ds(pl.multiple_of(t * 8, 8), 8)
         lower = pl.ds(pl.multiple_of(128 + t * 8, 8), 8)
         seen = []
-        for n in range(8):
-            jj = t % 2 * 4 + n // 2
+        for n in range(4):
+            jj = t % 2 * 4 + n
             prob = pb[t // 2, pl.ds(pl.multiple_of(8 * jj, 8), 8), :].astype(BF)
-            part = nt(prob, vr[t // 2, jj, pl.ds(n % 2 * 128, 128), :])
-            seen.append(jnp.where(agree[n % 2], part, 0.0))
+            part = jnp.where(agree, nt(prob, vr[t // 2, jj]), 0.0)
+            seen += [part[:, :128], part[:, 128:]]
         att[rows, :] = fold(seen)
         for ib in range(2):
             group = range(4 * ib, 4 * ib + 4)
@@ -328,10 +329,10 @@
             rows = pl.ds(pl.multiple_of(j * 16, 16), 16)
             for t in range(16):
                 out, z = outs[t]
-                out[z, rows, :] = rp[j, slots[t]]
+                out[z, rows, :] = rp[j, left_place(col, row // 4 * 4 ^ t)]
         return 0
 
-    lax.fori_loop(0, 8, finish, 0, unroll=2)
+    lax.fori_loop(0, 8, finish, 0, unroll=4)
     lsum = nn(lb[...], xl[...].reshape(2048, 128))
     rsum = nn(rb[...], xr[...].reshape(4096, 128))
     sums = jnp.concatenate(
@@ -448,11 +449,9 @@
     low = total[128:].astype(BF)
     first = add_up(first_keep, [first_came])
     second = add_up(second_keep, [second_came])
-    first_low, second_low, low = lax.optimization_barrier(
-        (first[2:].astype(BF), second[2:].astype(BF), low)
-    )
-    first_came = send(first_low, "row", 12)
-    second_came = send(second_low, "row", 4)
+    first_came = send(first[2:].astype(BF), "row", 12)
+    second_came = send(second[2:].astype(BF), "row", 4)
+    first_came, second_came, low = lax.optimization_barrier((first_came, second_came, low))
     came = send(low, "col", 2).astype(F32)
     left_grad = total[:128] + came[:128]
     weights = low[128:].astype(F32) + came[128:]
@@ -460,13 +459,11 @@
         [add_up(first[:2], [first_came]), add_up(second[:2], [second_came])]
     )
     low = right_total.astype(BF)
-    weights, low = lax.optimization_barrier((weights.astype(BF), low))
-    weights = meet(weights, "row", (4, 8, 12)).astype(BF)
-    weights, low = lax.optimization_barrier((weights, low))
-    right_came = [send(low[k], "row", k) for k in (2, 1, 3)]
+    right_came = lax.all_to_all(low, "row", 0, 0, axis_index_groups=LINES)
+    weights = meet(weights.astype(BF), "row", (4, 8, 12)).astype(BF)
+    right_came, weights = lax.optimization_barrier((right_came, weights))
     weights = meet(weights, "row", (1, 2, 3))
-    right_grad = right_total[0] + right_came[1].astype(F32) + right_came[0].astype(F32)
-    right_grad = right_grad + right_came[2].astype(F32)
+    right_grad = jnp.sum(right_came.astype(F32), axis=0)
     right_grad = jnp.swapaxes(right_grad.reshape(16, 16, width), 0, 1)
     mine = weights.astype(BF)
     other = send(mine, "col", 1)

time: 105 us -> 104 us (level)
  waiting for transfers between devices: 25.8 us -> 24.1 us
  starting transfers between devices: 53.3 us -> 54.5 us
    all_to_all x0 -> x1, starting transfers between devices: none -> 3.41 us  [body(): right_came = lax.all_to_all(low, 'row', 0, 0, axis_index_groups=LINES)]
    ppermute x31 -> x28, starting transfers between devices: 53.3 us -> 51.1 us  [send(): return lax.ppermute(block, axis, flip(k))]
    ppermute x31 -> x28, waiting for transfers between devices: 25.8 us -> 24.1 us  [send(): return lax.ppermute(block, axis, flip(k))]
  transfers between devices with their start and end apart: 31 -> 29, of which waited for: 17 -> 19; matrix products, arithmetic and copies ran while one was open for 2% -> 3% of each run, Pallas kernels for 0% -> 0%
where the time goes in v2:
time: 104 us
  starting transfers between devices  54.5 us (52%)
  waiting for transfers between devices  24.1 us (23%)
  Pallas kernels  18.7 us (18%)
  other arithmetic  3.49 us (3%)
  local copies, waits for them, and re-layouts  1.89 us (2%)
    ppermute x28, starting transfers between devices, send(): return lax.ppermute(block, axis, flip(k))  51.1 us
    ppermute x28, waiting for transfers between devices, send(): return lax.ppermute(block, axis, flip(k))  24.1 us
    pallas_call x1, Pallas kernels, triples(): pl.pallas_call(triple_kernel, out_shape=(jax.ShapeDtypeStruct((1344, 128)...  18.7 us
    all_to_all x1, starting transfers between devices, body(): right_came = lax.all_to_all(low, 'row', 0, 0, axis_index_groups=LINES)  3.41 us
  transfers between devices with their start and end apart: 29, of which 19 were waited for; matrix products, arithmetic and copies ran while one was open for 3% of the time, Pallas kernels for 0%

profile of v2, /device:TPU:1, one launch (start us, length us, event | category | flops | bytes accessed | tf_op | source)
XLA Modules:
  0.0 103.7 jit_solution(1920218951526581160)
XLA Ops:
  0.6 0.7 convert_bitcast_fusion
  1.4 0.1 copy.17
  1.5 0.1 tile.9
  1.6 0.0 copy-start.7
  1.6 3.9 %collective-permute-start.1 = (bf16[272,128]{1,0:T(8,128)(2,1)S(1)}, bf16[272,128]{1,0:T(8,128)(2,1)S(1)}, u32[]{:S(2)}, u32[]{:S(2)}) collective-permute-start(bf16[272,128]{1,0:T(8,128)(2,1)S(1)} %get-tuple-element.63), channel_id=1, source_target_pairs={{0,32},{16,48},{32,0},{48,16},{64,96},{80,112},{96,64},{112,80},{1... | collective-permute-start | bytes 208904 | tf_op jit(solution)/shard_map/s_row2/ppermute | solution.py:25
  5.5 1.6 %collective-permute-start = (bf16[272,128]{1,0:T(8,128)(2,1)S(1)}, bf16[272,128]{1,0:T(8,128)(2,1)S(1)}, u32[]{:S(2)}, u32[]{:S(2)}) collective-permute-start(bf16[272,128]{1,0:T(8,128)(2,1)S(1)} %get-tuple-element.63), channel_id=1, source_target_pairs={{0,16},{16,0},{32,48},{48,32},{64,80},{80,64},{96,112},{112,96},{1... | collective-permute-start | bytes 208904 | tf_op jit(solution)/shard_map/s_row1/ppermute | solution.py:25
  7.2 0.1 tile.21
  7.3 2.0 %collective-permute-done = bf16[272,128]{1,0:T(8,128)(2,1)S(1)} collective-permute-done((bf16[272,128]{1,0:T(8,128)(2,1)S(1)}, bf16[272,128]{1,0:T(8,128)(2,1)S(1)}, u32[]{:S(2)}, u32[]{:S(2)}) %collective-permute-start) | collective-permute-done | bytes 69664 | tf_op jit(solution)/shard_map/s_row1/ppermute | solution.py:25
  9.3 2.9 %collective-permute-done.2 = bf16[272,128]{1,0:T(8,128)(2,1)S(1)} collective-permute-done((bf16[272,128]{1,0:T(8,128)(2,1)S(1)}, bf16[272,128]{1,0:T(8,128)(2,1)S(1)}, u32[]{:S(2)}, u32[]{:S(2)}) %collective-permute-start.2) | collective-permute-done | bytes 69664 | tf_op jit(solution)/shard_map/s_row3/ppermute | solution.py:25
  12.3 2.6 %collective-permute-start.4 = (bf16[4,272,128]{2,1,0:T(8,128)(2,1)S(1)}, bf16[4,272,128]{2,1,0:T(8,128)(2,1)S(1)}, u32[]{:S(2)}, u32[]{:S(2)}) collective-permute-start(bf16[4,272,128]{2,1,0:T(8,128)(2,1)S(1)} %pad_maximum_fusion.1.right0), channel_id=1, source_target_pairs={{0,192},{16,208},{32,224},{48,240},{64,128},{80,144},{96,160},{112... | collective-permute-start | bytes 835592 | tf_op jit(solution)/shard_map/s_row12/ppermute | solution.py:25
  14.9 4.7 %collective-permute-start.5 = (bf16[144,128]{1,0:T(8,128)(2,1)S(1)}, bf16[144,128]{1,0:T(8,128)(2,1)S(1)}, u32[]{:S(2)}, u32[]{:S(2)}) collective-permute-start(bf16[144,128]{1,0:T(8,128)(2,1)S(1)} %fusion.5), channel_id=1, source_target_pairs={{0,2},{1,3},{2,0},{3,1},{4,6},{5,7},{6,4},{7,5},{8,10},{9,11},{10,... | collective-permute-start | bytes 110600 | tf_op jit(solution)/shard_map/s_col2/ppermute | solution.py:25
  19.6 2.0 %collective-permute-done.5 = bf16[144,128]{1,0:T(8,128)(2,1)S(1)} collective-permute-done((bf16[144,128]{1,0:T(8,128)(2,1)S(1)}, bf16[144,128]{1,0:T(8,128)(2,1)S(1)}, u32[]{:S(2)}, u32[]{:S(2)}) %collective-permute-start.5) | collective-permute-done | bytes 36896 | tf_op jit(solution)/shard_map/s_col2/ppermute | solution.py:25
  21.6 2.8 %collective-permute-start.10 = (bf16[2,144,128]{2,1,0:T(8,128)(2,1)S(1)}, bf16[2,144,128]{2,1,0:T(8,128)(2,1)S(1)}, u32[]{:S(2)}, u32[]{:S(2)}) collective-permute-start(bf16[2,144,128]{2,1,0:T(8,128)(2,1)S(1)} %pad_maximum_fusion.5), channel_id=1, source_target_pairs={{0,12},{1,13},{2,14},{3,15},{4,8},{5,9},{6,10},{7,11},{8,4},{9,5},... | collective-permute-start | bytes 221192 | tf_op jit(solution)/shard_map/s_col12/ppermute | solution.py:25
  24.4 0.3 collective-permute-start.9
  24.8 0.3 collective-permute-start.8
  25.1 0.0 copy-start
  25.2 0.0 copy-start.1
  25.2 0.9 collective-permute-start.7
  26.1 0.8 collective-permute-start.6
  26.9 2.3 %collective-permute-done.9 = bf16[2,144,128]{2,1,0:T(8,128)(2,1)S(1)} collective-permute-done((bf16[2,144,128]{2,1,0:T(8,128)(2,1)S(1)}, bf16[2,144,128]{2,1,0:T(8,128)(2,1)S(1)}, u32[]{:S(2)}, u32[]{:S(2)}) %collective-permute-start.9) | collective-permute-done | bytes 73760 | tf_op jit(solution)/shard_map/s_col8/ppermute | solution.py:25
  29.2 1.5 %collective-permute-done.7.right2b = bf16[2,272,128]{2,1,0:T(8,128)(2,1)S(1)} collective-permute-done((bf16[2,272,128]{2,1,0:T(8,128)(2,1)S(1)}, bf16[2,272,128]{2,1,0:T(8,128)(2,1)S(1)}, u32[]{:S(2)}, u32[]{:S(2)}) %collective-permute-start.7) | collective-permute-done | bytes 139296 | tf_op jit(solution)/shard_map/s_row12/ppermute | solution.py:25
  30.7 5.5 %collective-permute-start.11 = (bf16[8,144,128]{2,1,0:T(8,128)(2,1)S(1)}, bf16[8,144,128]{2,1,0:T(8,128)(2,1)S(1)}, u32[]{:S(2)}, u32[]{:S(2)}) collective-permute-start(bf16[8,144,128]{2,1,0:T(8,128)(2,1)S(1)} %pad_maximum_fusion.left0), channel_id=1, source_target_pairs={{0,1},{1,0},{2,3},{3,2},{4,5},{5,4},{6,7},{7,6},{8,9},{9,8},{10,11... | collective-permute-start | bytes 884744 | tf_op jit(solution)/shard_map/s_col1/ppermute | solution.py:25
  36.2 0.1 pad_add_fusion.at_ref
  36.3 1.1 %collective-permute-done.11.left1 = bf16[8,144,128]{2,1,0:T(8,128)(2,1)S(1)} collective-permute-done((bf16[8,144,128]{2,1,0:T(8,128)(2,1)S(1)}, bf16[8,144,128]{2,1,0:T(8,128)(2,1)S(1)}, u32[]{:S(2)}, u32[]{:S(2)}) %collective-permute-start.11) | collective-permute-done | bytes 294944 | tf_op jit(solution)/shard_map/s_col1/ppermute | solution.py:25
  37.4 18.7 %shard_map.129 = (bf16[1344,128]{1,0:T(8,128)(2,1)S(1)}, bf16[1344,128]{1,0:T(8,128)(2,1)S(1)}, bf16[4,256,128]{2,1,0:T(8,128)(2,1)S(1)}, bf16[4,256,128]{2,1,0:...) custom-call(s32[2]{0:T(128)S(1)} %pad_add_fusion.at_ref, ...), custom_call_target="tpu_custom_call" | custom-call | flops 800000000 | bytes 5000000 | tf_op jit(solution)/shard_map/pallas_call | solution.py:354
  56.2 0.5 collective-permute-start.12
  56.6 0.4 collective-permute-start.13
  57.0 2.3 %collective-permute-start.14 = (bf16[4,256,128]{2,1,0:T(8,128)(2,1)S(1)}, bf16[4,256,128]{2,1,0:T(8,128)(2,1)S(1)}, u32[]{:S(2)}, u32[]{:S(2)}) collective-permute-start(bf16[4,256,128]{2,1,0:T(8,128)(2,1)S(1)} %get-tuple-element.37), channel_id=1, source_target_pairs={{0,192},{16,208},{32,224},{48,240},{64,128},{80,144},{96,160},{112... | collective-permute-start | bytes 786440 | tf_op jit(solution)/shard_map/s_row12/ppermute | solution.py:25
  59.3 0.1 convert_add_fusion
  59.5 1.4 %collective-permute-start.15 = (bf16[576,128]{1,0:T(8,128)(2,1)S(1)}, bf16[576,128]{1,0:T(8,128)(2,1)S(1)}, u32[]{:S(2)}, u32[]{:S(2)}) collective-permute-start(bf16[576,128]{1,0:T(8,128)(2,1)S(1)} %get-tuple-element.61), channel_id=1, source_target_pairs={{0,4},{1,5},{2,6},{3,7},{4,0},{5,1},{6,2},{7,3},{8,12},{9,13},{10,... | collective-permute-start | bytes 442376 | tf_op jit(solution)/shard_map/s_col4/ppermute | solution.py:25
  60.9 2.0 %collective-permute-start.17 = (bf16[576,128]{1,0:T(8,128)(2,1)S(1)}, bf16[576,128]{1,0:T(8,128)(2,1)S(1)}, u32[]{:S(2)}, u32[]{:S(2)}) collective-permute-start(bf16[576,128]{1,0:T(8,128)(2,1)S(1)} %concatenate.37), channel_id=1, source_target_pairs={{0,12},{1,13},{2,14},{3,15},{4,8},{5,9},{6,10},{7,11},{8,4},{9,5},... | collective-permute-start | bytes 442376 | tf_op jit(solution)/shard_map/s_col12/ppermute | solution.py:25
  62.9 0.8 collective-permute-start.16
  63.7 0.4 collective-permute-done.15
  64.1 0.1 collective-permute-done.13
  64.2 1.3 %collective-permute-done.14 = bf16[4,256,128]{2,1,0:T(8,128)(2,1)S(1)} collective-permute-done((bf16[4,256,128]{2,1,0:T(8,128)(2,1)S(1)}, bf16[4,256,128]{2,1,0:T(8,128)(2,1)S(1)}, u32[]{:S(2)}, u32[]{:S(2)}) %collective-permute-start.14) | collective-permute-done | bytes 262176 | tf_op jit(solution)/shard_map/s_row12/ppermute | solution.py:25
  65.5 0.1 convert_add_fusion.2
  65.6 2.3 %collective-permute-start.18 = (bf16[2,256,128]{2,1,0:T(8,128)(2,1)S(1)}, bf16[2,256,128]{2,1,0:T(8,128)(2,1)S(1)}, u32[]{:S(2)}, u32[]{:S(2)}) collective-permute-start(bf16[2,256,128]{2,1,0:T(8,128)(2,1)S(1)} %slice.106), channel_id=1, source_target_pairs={{0,192},{16,208},{32,224},{48,240},{64,128},{80,144},{96,160},{112... | collective-permute-start | bytes 393224 | tf_op jit(solution)/shard_map/s_row12/ppermute | solution.py:25
  68.0 0.1 convert_add_fusion.1
  68.1 0.1 collective-permute-start.19
  68.2 0.1 collective-permute-done.17
  68.3 1.6 %collective-permute-done.16 = bf16[576,128]{1,0:T(8,128)(2,1)S(1)} collective-permute-done((bf16[576,128]{1,0:T(8,128)(2,1)S(1)}, bf16[576,128]{1,0:T(8,128)(2,1)S(1)}, u32[]{:S(2)}, u32[]{:S(2)}) %collective-permute-start.16) | collective-permute-done | bytes 147488 | tf_op jit(solution)/shard_map/s_col8/ppermute | solution.py:25
  69.9 0.1 fusion
  70.0 1.1 %collective-permute-done.18 = bf16[2,256,128]{2,1,0:T(8,128)(2,1)S(1)} collective-permute-done((bf16[2,256,128]{2,1,0:T(8,128)(2,1)S(1)}, bf16[2,256,128]{2,1,0:T(8,128)(2,1)S(1)}, u32[]{:S(2)}, u32[]{:S(2)}) %collective-permute-start.18) | collective-permute-done | bytes 131104 | tf_op jit(solution)/shard_map/s_row12/ppermute | solution.py:25
  71.0 1.2 %collective-permute-done.19 = bf16[2,256,128]{2,1,0:T(8,128)(2,1)S(1)} collective-permute-done((bf16[2,256,128]{2,1,0:T(8,128)(2,1)S(1)}, bf16[2,256,128]{2,1,0:T(8,128)(2,1)S(1)}, u32[]{:S(2)}, u32[]{:S(2)}) %collective-permute-start.19) | collective-permute-done | bytes 131104 | tf_op jit(solution)/shard_map/s_row4/ppermute | solution.py:25
  72.3 4.4 %collective-permute-start.20 = (bf16[448,128]{1,0:T(8,128)(2,1)S(1)}, bf16[448,128]{1,0:T(8,128)(2,1)S(1)}, u32[]{:S(2)}, u32[]{:S(2)}) collective-permute-start(bf16[448,128]{1,0:T(8,128)(2,1)S(1)} %slice.107), channel_id=1, source_target_pairs={{0,2},{1,3},{2,0},{3,1},{4,6},{5,7},{6,4},{7,5},{8,10},{9,11},{10,... | collective-permute-start | bytes 344072 | tf_op jit(solution)/shard_map/s_col2/ppermute | solution.py:25
  76.6 0.1 fusion.1
  76.7 0.7 pad_maximum_fusion.2
  77.4 3.4 %all-to-all-start = ((bf16[4,256,128]{2,1,0:T(8,128)(2,1)}), bf16[4,256,128]{2,1,0:T(8,128)(2,1)S(1)}, u32[]{:S(2)}, u32[]{:S(2)}) async-start(bf16[4,256,128]{2,1,0:T(8,128)(2,1)} %pad_maximum_fusion.2), calls=%async_computation | async-start | bytes 524288 | tf_op jit(solution)/shard_map/all_to_all | solution.py:462
  80.9 0.8 collective-permute-start.23
  81.7 0.8 collective-permute-start.22
  82.5 1.8 %collective-permute-start.21 = (bf16[320,128]{1,0:T(8,128)(2,1)S(1)}, bf16[320,128]{1,0:T(8,128)(2,1)S(1)}, u32[]{:S(2)}, u32[]{:S(2)}) collective-permute-start(bf16[320,128]{1,0:T(8,128)(2,1)S(1)} %fusion.3), channel_id=1, source_target_pairs={{0,64},{16,80},{32,96},{48,112},{64,0},{80,16},{96,32},{112,48},{1... | collective-permute-start | bytes 245768 | tf_op jit(solution)/shard_map/s_row4/ppermute | solution.py:25
  84.3 1.2 %collective-permute-done.23 = bf16[320,128]{1,0:T(8,128)(2,1)S(1)} collective-permute-done((bf16[320,128]{1,0:T(8,128)(2,1)S(1)}, bf16[320,128]{1,0:T(8,128)(2,1)S(1)}, u32[]{:S(2)}, u32[]{:S(2)}) %collective-permute-start.23) | collective-permute-done | bytes 81952 | tf_op jit(solution)/shard_map/s_row12/ppermute | solution.py:25
  85.5 1.0 %collective-permute-done.22 = bf16[320,128]{1,0:T(8,128)(2,1)S(1)} collective-permute-done((bf16[320,128]{1,0:T(8,128)(2,1)S(1)}, bf16[320,128]{1,0:T(8,128)(2,1)S(1)}, u32[]{:S(2)}, u32[]{:S(2)}) %collective-permute-start.22) | collective-permute-done | bytes 81952 | tf_op jit(solution)/shard_map/s_row8/ppermute | solution.py:25
  86.5 0.7 collective-permute-done.21
  87.3 3.3 %collective-permute-start.26 = (bf16[320,128]{1,0:T(8,128)(2,1)S(1)}, bf16[320,128]{1,0:T(8,128)(2,1)S(1)}, u32[]{:S(2)}, u32[]{:S(2)}) collective-permute-start(bf16[320,128]{1,0:T(8,128)(2,1)S(1)} %add_convert_fusion.1), channel_id=1, source_target_pairs={{0,48},{16,32},{32,16},{48,0},{64,112},{80,96},{96,80},{112,64},{1... | collective-permute-start | bytes 245768 | tf_op jit(solution)/shard_map/s_row3/ppermute | solution.py:25
  90.6 0.4 collective-permute-start.24
  91.0 0.6 slice_add_fusion.3
  91.6 1.0 collective-permute-done.26
  92.6 2.2 %collective-permute-done.25 = bf16[320,128]{1,0:T(8,128)(2,1)S(1)} collective-permute-done((bf16[320,128]{1,0:T(8,128)(2,1)S(1)}, bf16[320,128]{1,0:T(8,128)(2,1)S(1)}, u32[]{:S(2)}, u32[]{:S(2)}) %collective-permute-start.25) | collective-permute-done | bytes 81952 | tf_op jit(solution)/shard_map/s_row2/ppermute | solution.py:25
  94.9 6.5 %collective-permute-start.27 = (bf16[320,128]{1,0:T(8,128)(2,1)S(1)}, bf16[320,128]{1,0:T(8,128)(2,1)S(1)}, u32[]{:S(2)}, u32[]{:S(2)}) collective-permute-start(bf16[320,128]{1,0:T(8,128)(2,1)S(1)} %add_convert_fusion), channel_id=1, source_target_pairs={{0,1},{1,0},{2,3},{3,2},{4,5},{5,4},{6,7},{7,6},{8,9},{9,8},{10,11... | collective-permute-start | bytes 245768 | tf_op jit(solution)/shard_map/s_col1/ppermute | solution.py:25
  101.4 0.7 copy.18
  102.1 0.2 collective-permute-done.27
  102.3 0.6 maximum_convert_fusion.1
  102.9 0.7 slice.88
  (55 shorter events, 0.6 us)
Async XLA Ops:
  0.6 0.9 copy-start.6
  1.6 5.6 %copy-start.8 = (s32[8,16]{1,0:T(8,128)S(1)}, s32[8,16]{1,0:T(8,128)}, u32[]{:S(2)}) copy-start(s32[8,16]{1,0:T(8,128)} %param.12) | copy-start | bytes 1540
  1.6 5.7 %copy-start.7 = (bf16[8,16,128]{2,1,0:T(8,128)(2,1)S(1)}, bf16[8,16,128]{2,1,0:T(8,128)(2,1)}, u32[]{:S(2)}) copy-start(bf16[8,16,128]{2,1,0:T(8,128)(2,1)} %param.10) | copy-start | bytes 98308
  1.6 5.7 %collective-permute-start.1 = (bf16[272,128]{1,0:T(8,128)(2,1)S(1)}, bf16[272,128]{1,0:T(8,128)(2,1)S(1)}, u32[]{:S(2)}, u32[]{:S(2)}) collective-permute-start(bf16[272,128]{1,0:T(8,128)(2,1)S(1)} %get-tuple-element.63), channel_id=1, source_target_pairs={{0,32},{16,48},{32,0},{48,16},{64,96},{80,112},{96,64},{112,80},{1... | collective-permute-start | bytes 208904 | tf_op jit(solution)/shard_map/s_row2/ppermute | solution.py:25
  5.5 3.8 %collective-permute-start = (bf16[272,128]{1,0:T(8,128)(2,1)S(1)}, bf16[272,128]{1,0:T(8,128)(2,1)S(1)}, u32[]{:S(2)}, u32[]{:S(2)}) collective-permute-start(bf16[272,128]{1,0:T(8,128)(2,1)S(1)} %get-tuple-element.63), channel_id=1, source_target_pairs={{0,16},{16,0},{32,48},{48,32},{64,80},{80,64},{96,112},{112,96},{1... | collective-permute-start | bytes 208904 | tf_op jit(solution)/shard_map/s_row1/ppermute | solution.py:25
  7.2 5.1 %collective-permute-start.2 = (bf16[272,128]{1,0:T(8,128)(2,1)S(1)}, bf16[272,128]{1,0:T(8,128)(2,1)S(1)}, u32[]{:S(2)}, u32[]{:S(2)}) collective-permute-start(bf16[272,128]{1,0:T(8,128)(2,1)S(1)} %get-tuple-element.63), channel_id=1, source_target_pairs={{0,48},{16,32},{32,16},{48,0},{64,112},{80,96},{96,80},{112,64},{1... | collective-permute-start | bytes 208904 | tf_op jit(solution)/shard_map/s_row3/ppermute | solution.py:25
  12.3 9.3 %collective-permute-start.4 = (bf16[4,272,128]{2,1,0:T(8,128)(2,1)S(1)}, bf16[4,272,128]{2,1,0:T(8,128)(2,1)S(1)}, u32[]{:S(2)}, u32[]{:S(2)}) collective-permute-start(bf16[4,272,128]{2,1,0:T(8,128)(2,1)S(1)} %pad_maximum_fusion.1.right0), channel_id=1, source_target_pairs={{0,192},{16,208},{32,224},{48,240},{64,128},{80,144},{96,160},{112... | collective-permute-start | bytes 835592 | tf_op jit(solution)/shard_map/s_row12/ppermute | solution.py:25
  14.9 6.7 %collective-permute-start.3 = (bf16[4,272,128]{2,1,0:T(8,128)(2,1)S(1)}, bf16[4,272,128]{2,1,0:T(8,128)(2,1)S(1)}, u32[]{:S(2)}, u32[]{:S(2)}) collective-permute-start(bf16[4,272,128]{2,1,0:T(8,128)(2,1)S(1)} %pad_maximum_fusion.1.right0), channel_id=1, source_target_pairs={{0,64},{16,80},{32,96},{48,112},{64,0},{80,16},{96,32},{112,48},{1... | collective-permute-start | bytes 835592 | tf_op jit(solution)/shard_map/s_row4/ppermute | solution.py:25
  14.9 6.7 %collective-permute-start.5 = (bf16[144,128]{1,0:T(8,128)(2,1)S(1)}, bf16[144,128]{1,0:T(8,128)(2,1)S(1)}, u32[]{:S(2)}, u32[]{:S(2)}) collective-permute-start(bf16[144,128]{1,0:T(8,128)(2,1)S(1)} %fusion.5), channel_id=1, source_target_pairs={{0,2},{1,3},{2,0},{3,1},{4,6},{5,7},{6,4},{7,5},{8,10},{9,11},{10,... | collective-permute-start | bytes 110600 | tf_op jit(solution)/shard_map/s_col2/ppermute | solution.py:25
  21.6 5.3 %collective-permute-start.10 = (bf16[2,144,128]{2,1,0:T(8,128)(2,1)S(1)}, bf16[2,144,128]{2,1,0:T(8,128)(2,1)S(1)}, u32[]{:S(2)}, u32[]{:S(2)}) collective-permute-start(bf16[2,144,128]{2,1,0:T(8,128)(2,1)S(1)} %pad_maximum_fusion.5), channel_id=1, source_target_pairs={{0,12},{1,13},{2,14},{3,15},{4,8},{5,9},{6,10},{7,11},{8,4},{9,5},... | collective-permute-start | bytes 221192 | tf_op jit(solution)/shard_map/s_col12/ppermute | solution.py:25
  24.4 4.7 %collective-permute-start.9 = (bf16[2,144,128]{2,1,0:T(8,128)(2,1)S(1)}, bf16[2,144,128]{2,1,0:T(8,128)(2,1)S(1)}, u32[]{:S(2)}, u32[]{:S(2)}) collective-permute-start(bf16[2,144,128]{2,1,0:T(8,128)(2,1)S(1)} %pad_maximum_fusion.5), channel_id=1, source_target_pairs={{0,8},{1,9},{2,10},{3,11},{4,12},{5,13},{6,14},{7,15},{8,0},{9,1},... | collective-permute-start | bytes 221192 | tf_op jit(solution)/shard_map/s_col8/ppermute | solution.py:25
  24.8 4.4 %collective-permute-start.8 = (bf16[2,144,128]{2,1,0:T(8,128)(2,1)S(1)}, bf16[2,144,128]{2,1,0:T(8,128)(2,1)S(1)}, u32[]{:S(2)}, u32[]{:S(2)}) collective-permute-start(bf16[2,144,128]{2,1,0:T(8,128)(2,1)S(1)} %pad_maximum_fusion.5), channel_id=1, source_target_pairs={{0,4},{1,5},{2,6},{3,7},{4,0},{5,1},{6,2},{7,3},{8,12},{9,13},{10,... | collective-permute-start | bytes 221192 | tf_op jit(solution)/shard_map/s_col4/ppermute | solution.py:25
  25.1 12.3 %copy-start = (bf16[8,16,128]{2,1,0:T(8,128)(2,1)S(1)}, bf16[8,16,128]{2,1,0:T(8,128)(2,1)}, u32[]{:S(2)}) copy-start(bf16[8,16,128]{2,1,0:T(8,128)(2,1)} %param.14) | copy-start | bytes 98308
  25.2 12.2 %copy-start.1 = (bf16[128,128]{1,0:T(8,128)(2,1)S(1)}, bf16[128,128]{1,0:T(8,128)(2,1)}, u32[]{:S(2)}) copy-start(bf16[128,128]{1,0:T(8,128)(2,1)} %wq_hbm.1) | copy-start | bytes 98308
  25.2 12.2 %copy-start.2 = (bf16[128,128]{1,0:T(8,128)(2,1)S(1)}, bf16[128,128]{1,0:T(8,128)(2,1)}, u32[]{:S(2)}) copy-start(bf16[128,128]{1,0:T(8,128)(2,1)} %wk_hbm.1) | copy-start | bytes 98308
  25.2 12.2 %copy-start.3 = (bf16[128,128]{1,0:T(8,128)(2,1)S(1)}, bf16[128,128]{1,0:T(8,128)(2,1)}, u32[]{:S(2)}) copy-start(bf16[128,128]{1,0:T(8,128)(2,1)} %wl_hbm.1) | copy-start | bytes 98308
  25.2 12.2 %copy-start.4 = (bf16[128,128]{1,0:T(8,128)(2,1)S(1)}, bf16[128,128]{1,0:T(8,128)(2,1)}, u32[]{:S(2)}) copy-start(bf16[128,128]{1,0:T(8,128)(2,1)} %wr_hbm.1) | copy-start | bytes 98308
  25.2 12.2 %copy-start.5 = (bf16[128,128]{1,0:T(8,128)(2,1)S(1)}, bf16[128,128]{1,0:T(8,128)(2,1)}, u32[]{:S(2)}) copy-start(bf16[128,128]{1,0:T(8,128)(2,1)} %wo_hbm.1) | copy-start | bytes 98308
  25.2 5.5 %collective-permute-start.7 = (bf16[2,272,128]{2,1,0:T(8,128)(2,1)S(1)}, bf16[2,272,128]{2,1,0:T(8,128)(2,1)S(1)}, u32[]{:S(2)}, u32[]{:S(2)}) collective-permute-start(bf16[2,272,128]{2,1,0:T(8,128)(2,1)S(1)} %slice.60), channel_id=1, source_target_pairs={{0,192},{16,208},{32,224},{48,240},{64,128},{80,144},{96,160},{112... | collective-permute-start | bytes 417800 | tf_op jit(solution)/shard_map/s_row12/ppermute | solution.py:25
  26.1 4.6 %collective-permute-start.6 = (bf16[2,272,128]{2,1,0:T(8,128)(2,1)S(1)}, bf16[2,272,128]{2,1,0:T(8,128)(2,1)S(1)}, u32[]{:S(2)}, u32[]{:S(2)}) collective-permute-start(bf16[2,272,128]{2,1,0:T(8,128)(2,1)S(1)} %slice.59), channel_id=1, source_target_pairs={{0,64},{16,80},{32,96},{48,112},{64,0},{80,16},{96,32},{112,48},{1... | collective-permute-start | bytes 417800 | tf_op jit(solution)/shard_map/s_row4/ppermute | solution.py:25
  30.7 6.7 %collective-permute-start.11 = (bf16[8,144,128]{2,1,0:T(8,128)(2,1)S(1)}, bf16[8,144,128]{2,1,0:T(8,128)(2,1)S(1)}, u32[]{:S(2)}, u32[]{:S(2)}) collective-permute-start(bf16[8,144,128]{2,1,0:T(8,128)(2,1)S(1)} %pad_maximum_fusion.left0), channel_id=1, source_target_pairs={{0,1},{1,0},{2,3},{3,2},{4,5},{5,4},{6,7},{7,6},{8,9},{9,8},{10,11... | collective-permute-start | bytes 884744 | tf_op jit(solution)/shard_map/s_col1/ppermute | solution.py:25
  56.2 3.1 %collective-permute-start.12 = (bf16[1344,128]{1,0:T(8,128)(2,1)S(1)}, bf16[1344,128]{1,0:T(8,128)(2,1)S(1)}, u32[]{:S(2)}, u32[]{:S(2)}) collective-permute-start(bf16[1344,128]{1,0:T(8,128)(2,1)S(1)} %get-tuple-element.35), channel_id=1, source_target_pairs={{0,1},{1,0},{2,3},{3,2},{4,5},{5,4},{6,7},{7,6},{8,9},{9,8},{10,11... | collective-permute-start | bytes 1032200 | tf_op jit(solution)/shard_map/s_col1/ppermute | solution.py:25
  56.6 7.6 %collective-permute-start.13 = (bf16[4,256,128]{2,1,0:T(8,128)(2,1)S(1)}, bf16[4,256,128]{2,1,0:T(8,128)(2,1)S(1)}, u32[]{:S(2)}, u32[]{:S(2)}) collective-permute-start(bf16[4,256,128]{2,1,0:T(8,128)(2,1)S(1)} %get-tuple-element.36), channel_id=1, source_target_pairs={{0,64},{16,80},{32,96},{48,112},{64,0},{80,16},{96,32},{112,48},{1... | collective-permute-start | bytes 786440 | tf_op jit(solution)/shard_map/s_row4/ppermute | solution.py:25
  57.0 8.5 %collective-permute-start.14 = (bf16[4,256,128]{2,1,0:T(8,128)(2,1)S(1)}, bf16[4,256,128]{2,1,0:T(8,128)(2,1)S(1)}, u32[]{:S(2)}, u32[]{:S(2)}) collective-permute-start(bf16[4,256,128]{2,1,0:T(8,128)(2,1)S(1)} %get-tuple-element.37), channel_id=1, source_target_pairs={{0,192},{16,208},{32,224},{48,240},{64,128},{80,144},{96,160},{112... | collective-permute-start | bytes 786440 | tf_op jit(solution)/shard_map/s_row12/ppermute | solution.py:25
  59.5 4.6 %collective-permute-start.15 = (bf16[576,128]{1,0:T(8,128)(2,1)S(1)}, bf16[576,128]{1,0:T(8,128)(2,1)S(1)}, u32[]{:S(2)}, u32[]{:S(2)}) collective-permute-start(bf16[576,128]{1,0:T(8,128)(2,1)S(1)} %get-tuple-element.61), channel_id=1, source_target_pairs={{0,4},{1,5},{2,6},{3,7},{4,0},{5,1},{6,2},{7,3},{8,12},{9,13},{10,... | collective-permute-start | bytes 442376 | tf_op jit(solution)/shard_map/s_col4/ppermute | solution.py:25
  60.9 7.4 %collective-permute-start.17 = (bf16[576,128]{1,0:T(8,128)(2,1)S(1)}, bf16[576,128]{1,0:T(8,128)(2,1)S(1)}, u32[]{:S(2)}, u32[]{:S(2)}) collective-permute-start(bf16[576,128]{1,0:T(8,128)(2,1)S(1)} %concatenate.37), channel_id=1, source_target_pairs={{0,12},{1,13},{2,14},{3,15},{4,8},{5,9},{6,10},{7,11},{8,4},{9,5},... | collective-permute-start | bytes 442376 | tf_op jit(solution)/shard_map/s_col12/ppermute | solution.py:25
  62.9 7.1 %collective-permute-start.16 = (bf16[576,128]{1,0:T(8,128)(2,1)S(1)}, bf16[576,128]{1,0:T(8,128)(2,1)S(1)}, u32[]{:S(2)}, u32[]{:S(2)}) collective-permute-start(bf16[576,128]{1,0:T(8,128)(2,1)S(1)} %get-tuple-element.60), channel_id=1, source_target_pairs={{0,8},{1,9},{2,10},{3,11},{4,12},{5,13},{6,14},{7,15},{8,0},{9,1},... | collective-permute-start | bytes 442376 | tf_op jit(solution)/shard_map/s_col8/ppermute | solution.py:25
  65.6 5.4 %collective-permute-start.18 = (bf16[2,256,128]{2,1,0:T(8,128)(2,1)S(1)}, bf16[2,256,128]{2,1,0:T(8,128)(2,1)S(1)}, u32[]{:S(2)}, u32[]{:S(2)}) collective-permute-start(bf16[2,256,128]{2,1,0:T(8,128)(2,1)S(1)} %slice.106), channel_id=1, source_target_pairs={{0,192},{16,208},{32,224},{48,240},{64,128},{80,144},{96,160},{112... | collective-permute-start | bytes 393224 | tf_op jit(solution)/shard_map/s_row12/ppermute | solution.py:25
  68.1 4.2 %collective-permute-start.19 = (bf16[2,256,128]{2,1,0:T(8,128)(2,1)S(1)}, bf16[2,256,128]{2,1,0:T(8,128)(2,1)S(1)}, u32[]{:S(2)}, u32[]{:S(2)}) collective-permute-start(bf16[2,256,128]{2,1,0:T(8,128)(2,1)S(1)} %slice.105), channel_id=1, source_target_pairs={{0,64},{16,80},{32,96},{48,112},{64,0},{80,16},{96,32},{112,48},{1... | collective-permute-start | bytes 393224 | tf_op jit(solution)/shard_map/s_row4/ppermute | solution.py:25
  72.3 8.6 %collective-permute-start.20 = (bf16[448,128]{1,0:T(8,128)(2,1)S(1)}, bf16[448,128]{1,0:T(8,128)(2,1)S(1)}, u32[]{:S(2)}, u32[]{:S(2)}) collective-permute-start(bf16[448,128]{1,0:T(8,128)(2,1)S(1)} %slice.107), channel_id=1, source_target_pairs={{0,2},{1,3},{2,0},{3,1},{4,6},{5,7},{6,4},{7,5},{8,10},{9,11},{10,... | collective-permute-start | bytes 344072 | tf_op jit(solution)/shard_map/s_col2/ppermute | solution.py:25
  77.4 9.9 %all-to-all-start = ((bf16[4,256,128]{2,1,0:T(8,128)(2,1)}), bf16[4,256,128]{2,1,0:T(8,128)(2,1)S(1)}, u32[]{:S(2)}, u32[]{:S(2)}) async-start(bf16[4,256,128]{2,1,0:T(8,128)(2,1)} %pad_maximum_fusion.2), calls=%async_computation | async-start | bytes 524288 | tf_op jit(solution)/shard_map/all_to_all | solution.py:462
  80.9 4.6 %collective-permute-start.23 = (bf16[320,128]{1,0:T(8,128)(2,1)S(1)}, bf16[320,128]{1,0:T(8,128)(2,1)S(1)}, u32[]{:S(2)}, u32[]{:S(2)}) collective-permute-start(bf16[320,128]{1,0:T(8,128)(2,1)S(1)} %fusion.3), channel_id=1, source_target_pairs={{0,192},{16,208},{32,224},{48,240},{64,128},{80,144},{96,160},{112... | collective-permute-start | bytes 245768 | tf_op jit(solution)/shard_map/s_row12/ppermute | solution.py:25
  81.7 4.8 %collective-permute-start.22 = (bf16[320,128]{1,0:T(8,128)(2,1)S(1)}, bf16[320,128]{1,0:T(8,128)(2,1)S(1)}, u32[]{:S(2)}, u32[]{:S(2)}) collective-permute-start(bf16[320,128]{1,0:T(8,128)(2,1)S(1)} %fusion.3), channel_id=1, source_target_pairs={{0,128},{16,144},{32,160},{48,176},{64,192},{80,208},{96,224},{112... | collective-permute-start | bytes 245768 | tf_op jit(solution)/shard_map/s_row8/ppermute | solution.py:25
  82.5 4.8 %collective-permute-start.21 = (bf16[320,128]{1,0:T(8,128)(2,1)S(1)}, bf16[320,128]{1,0:T(8,128)(2,1)S(1)}, u32[]{:S(2)}, u32[]{:S(2)}) collective-permute-start(bf16[320,128]{1,0:T(8,128)(2,1)S(1)} %fusion.3), channel_id=1, source_target_pairs={{0,64},{16,80},{32,96},{48,112},{64,0},{80,16},{96,32},{112,48},{1... | collective-permute-start | bytes 245768 | tf_op jit(solution)/shard_map/s_row4/ppermute | solution.py:25
  87.3 5.3 %collective-permute-start.26 = (bf16[320,128]{1,0:T(8,128)(2,1)S(1)}, bf16[320,128]{1,0:T(8,128)(2,1)S(1)}, u32[]{:S(2)}, u32[]{:S(2)}) collective-permute-start(bf16[320,128]{1,0:T(8,128)(2,1)S(1)} %add_convert_fusion.1), channel_id=1, source_target_pairs={{0,48},{16,32},{32,16},{48,0},{64,112},{80,96},{96,80},{112,64},{1... | collective-permute-start | bytes 245768 | tf_op jit(solution)/shard_map/s_row3/ppermute | solution.py:25
  90.6 4.2 %collective-permute-start.25 = (bf16[320,128]{1,0:T(8,128)(2,1)S(1)}, bf16[320,128]{1,0:T(8,128)(2,1)S(1)}, u32[]{:S(2)}, u32[]{:S(2)}) collective-permute-start(bf16[320,128]{1,0:T(8,128)(2,1)S(1)} %add_convert_fusion.1), channel_id=1, source_target_pairs={{0,32},{16,48},{32,0},{48,16},{64,96},{80,112},{96,64},{112,80},{1... | collective-permute-start | bytes 245768 | tf_op jit(solution)/shard_map/s_row2/ppermute | solution.py:25
  90.6 4.2 %collective-permute-start.24 = (bf16[320,128]{1,0:T(8,128)(2,1)S(1)}, bf16[320,128]{1,0:T(8,128)(2,1)S(1)}, u32[]{:S(2)}, u32[]{:S(2)}) collective-permute-start(bf16[320,128]{1,0:T(8,128)(2,1)S(1)} %add_convert_fusion.1), channel_id=1, source_target_pairs={{0,16},{16,0},{32,48},{48,32},{64,80},{80,64},{96,112},{112,96},{1... | collective-permute-start | bytes 245768 | tf_op jit(solution)/shard_map/s_row1/ppermute | solution.py:25
  94.9 7.4 %collective-permute-start.27 = (bf16[320,128]{1,0:T(8,128)(2,1)S(1)}, bf16[320,128]{1,0:T(8,128)(2,1)S(1)}, u32[]{:S(2)}, u32[]{:S(2)}) collective-permute-start(bf16[320,128]{1,0:T(8,128)(2,1)S(1)} %add_convert_fusion), channel_id=1, source_target_pairs={{0,1},{1,0},{2,3},{3,2},{4,5},{5,4},{6,7},{7,6},{8,9},{9,8},{10,11... | collective-permute-start | bytes 245768 | tf_op jit(solution)/shard_map/s_col1/ppermute | solution.py:25

commit v3 on v2

--- a/solution.py
+++ b/solution.py
@@ -130,6 +130,8 @@
     rp,
     vr,
     up,
+    vb,
+    wb,
     cot_ref,
     weights,
     arrived,
@@ -193,13 +195,17 @@
     wr = jnp.concatenate([weights[2].T, weights[3].T])
 
     def project_left(i, _):
-        ql[i] = nt(wl, xl[i].reshape(256, 128)).astype(BF).astype(F32)
+        both = nt(wl, xl[i].reshape(256, 128)).astype(BF)
+        ql[i] = both.astype(F32)
+        vb[i] = both[128:]
         return 0
 
     lax.fori_loop(0, 8, project_left, 0, unroll=8)
 
     def project_right(j, _):
-        kr[j] = nt(wr, xr[j].reshape(256, 128)).astype(BF).astype(F32)
+        both = nt(wr, xr[j].reshape(256, 128)).astype(BF)
+        kr[j] = both.astype(F32)
+        wb[j] = both[128:]
         return 0
 
     lax.fori_loop(0, 16, project_right, 0, unroll=8)
@@ -236,14 +242,14 @@
         for h in range(4):
             tiles = [pl.ds(h * 32 + 8 * e, 8) for e in range(4)]
             q = [ql[i, r, :] for r in tiles]
-            v = ql[i, pl.ds(128 + h * 32, 32), :]
+            v = vb[i, pl.ds(h * 32, 32), :]
             for half in range(2):
                 scores = []
                 for j in range(8 * half, 8 * half + 8):
                     k = [kr[j, r, :] for r in tiles]
                     scores.append((q[0] * k[0] + q[1] * k[1]) + (q[2] * k[2] + q[3] * k[3]))
-                    w = kr[j, pl.ds(128 + h * 32, 32), :]
-                    vr[i, j // 2, pl.ds(j % 2 * 128 + h * 32, 32), :] = (v * w).astype(BF)
+                    w = wb[j, pl.ds(h * 32, 32), :]
+                    vr[i, j // 2, pl.ds(j % 2 * 128 + h * 32, 32), :] = v * w
                 score = fold(scores)
                 for side in range(2):
                     ts[i, side, pl.ds(32 * half + h, 8, stride=4), :] = score[
@@ -251,7 +257,7 @@
                     ]
         return 0
 
-    lax.fori_loop(0, 8, score_row, 0)
+    lax.fori_loop(0, 8, score_row, 0, unroll=2)
     grad_row(7)
 
     for i in range(8):
@@ -332,7 +338,7 @@
                 out[z, rows, :] = rp[j, left_place(col, row // 4 * 4 ^ t)]
         return 0
 
-    lax.fori_loop(0, 8, finish, 0, unroll=4)
+    lax.fori_loop(0, 8, finish, 0, unroll=8)
     lsum = nn(lb[...], xl[...].reshape(2048, 128))
     rsum = nn(rb[...], xr[...].reshape(4096, 128))
     sums = jnp.concatenate(
@@ -383,6 +389,8 @@
             pltpu.VMEM((16, 16, 16, 128), BF),
             pltpu.VMEM((8, 8, 256, 256), BF),
             pltpu.VMEM((128, 128), F32),
+            pltpu.VMEM((8, 128, 256), BF),
+            pltpu.VMEM((16, 128, 256), BF),
             pltpu.VMEM((128, 128), BF),
             pltpu.VMEM((5, 128, 128), BF),
             pltpu.SemaphoreType.DMA((6,)),

time: 104 us -> 103 us (level)
  Pallas kernels: 18.7 us -> 17.4 us
    pallas_call x1, Pallas kernels: 18.7 us -> 17.4 us  [triples(): pl.pallas_call(triple_kernel, out_shape=(jax.ShapeDtypeStruct((1344, 128)...]
  transfers between devices with their start and end apart: 29 -> 29, of which waited for: 19 -> 18; matrix products, arithmetic and copies ran while one was open for 3% -> 3% of each run, Pallas kernels for 0% -> 0%
where the time goes in v3:
time: 103 us; the launch traced here: 102 us
  starting transfers between devices  54.3 us (53%)
  waiting for transfers between devices  24.3 us (24%)
  Pallas kernels  17.4 us (17%)
  other arithmetic  3.49 us (3%)
  local copies, waits for them, and re-layouts  1.89 us (2%)
    ppermute x28, starting transfers between devices, send(): return lax.ppermute(block, axis, flip(k))  50.9 us
    ppermute x28, waiting for transfers between devices, send(): return lax.ppermute(block, axis, flip(k))  24.3 us
    pallas_call x1, Pallas kernels, triples(): pl.pallas_call(triple_kernel, out_shape=(jax.ShapeDtypeStruct((1344, 128)...  17.4 us
    all_to_all x1, starting transfers between devices, body(): right_came = lax.all_to_all(low, 'row', 0, 0, axis_index_groups=LINES)  3.41 us
  transfers between devices with their start and end apart: 29, of which 18 were waited for; matrix products, arithmetic and copies ran while one was open for 3% of the time, Pallas kernels for 0%

profile of v3, /device:TPU:1, one launch (start us, length us, event | category | flops | bytes accessed | tf_op | source)
XLA Modules:
  0.0 102.3 jit_solution(7012472126661198039)
XLA Ops:
  0.6 0.7 convert_bitcast_fusion
  1.4 0.1 copy.17
  1.5 0.1 tile.9
  1.6 0.0 copy-start.8
  1.6 3.9 %collective-permute-start.1 = (bf16[272,128]{1,0:T(8,128)(2,1)S(1)}, bf16[272,128]{1,0:T(8,128)(2,1)S(1)}, u32[]{:S(2)}, u32[]{:S(2)}) collective-permute-start(bf16[272,128]{1,0:T(8,128)(2,1)S(1)} %get-tuple-element.63), channel_id=1, source_target_pairs={{0,32},{16,48},{32,0},{48,16},{64,96},{80,112},{96,64},{112,80},{1... | collective-permute-start | bytes 208904 | tf_op jit(solution)/shard_map/s_row2/ppermute | solution.py:25
  5.5 1.6 %collective-permute-start = (bf16[272,128]{1,0:T(8,128)(2,1)S(1)}, bf16[272,128]{1,0:T(8,128)(2,1)S(1)}, u32[]{:S(2)}, u32[]{:S(2)}) collective-permute-start(bf16[272,128]{1,0:T(8,128)(2,1)S(1)} %get-tuple-element.63), channel_id=1, source_target_pairs={{0,16},{16,0},{32,48},{48,32},{64,80},{80,64},{96,112},{112,96},{1... | collective-permute-start | bytes 208904 | tf_op jit(solution)/shard_map/s_row1/ppermute | solution.py:25
  7.2 0.1 tile.21
  7.3 2.0 %collective-permute-done = bf16[272,128]{1,0:T(8,128)(2,1)S(1)} collective-permute-done((bf16[272,128]{1,0:T(8,128)(2,1)S(1)}, bf16[272,128]{1,0:T(8,128)(2,1)S(1)}, u32[]{:S(2)}, u32[]{:S(2)}) %collective-permute-start) | collective-permute-done | bytes 69664 | tf_op jit(solution)/shard_map/s_row1/ppermute | solution.py:25
  9.3 2.9 %collective-permute-done.2 = bf16[272,128]{1,0:T(8,128)(2,1)S(1)} collective-permute-done((bf16[272,128]{1,0:T(8,128)(2,1)S(1)}, bf16[272,128]{1,0:T(8,128)(2,1)S(1)}, u32[]{:S(2)}, u32[]{:S(2)}) %collective-permute-start.2) | collective-permute-done | bytes 69664 | tf_op jit(solution)/shard_map/s_row3/ppermute | solution.py:25
  12.3 2.6 %collective-permute-start.4 = (bf16[4,272,128]{2,1,0:T(8,128)(2,1)S(1)}, bf16[4,272,128]{2,1,0:T(8,128)(2,1)S(1)}, u32[]{:S(2)}, u32[]{:S(2)}) collective-permute-start(bf16[4,272,128]{2,1,0:T(8,128)(2,1)S(1)} %pad_maximum_fusion.1.right0), channel_id=1, source_target_pairs={{0,192},{16,208},{32,224},{48,240},{64,128},{80,144},{96,160},{112... | collective-permute-start | bytes 835592 | tf_op jit(solution)/shard_map/s_row12/ppermute | solution.py:25
  14.9 4.7 %collective-permute-start.5 = (bf16[144,128]{1,0:T(8,128)(2,1)S(1)}, bf16[144,128]{1,0:T(8,128)(2,1)S(1)}, u32[]{:S(2)}, u32[]{:S(2)}) collective-permute-start(bf16[144,128]{1,0:T(8,128)(2,1)S(1)} %fusion.5), channel_id=1, source_target_pairs={{0,2},{1,3},{2,0},{3,1},{4,6},{5,7},{6,4},{7,5},{8,10},{9,11},{10,... | collective-permute-start | bytes 110600 | tf_op jit(solution)/shard_map/s_col2/ppermute | solution.py:25
  19.6 2.0 %collective-permute-done.5 = bf16[144,128]{1,0:T(8,128)(2,1)S(1)} collective-permute-done((bf16[144,128]{1,0:T(8,128)(2,1)S(1)}, bf16[144,128]{1,0:T(8,128)(2,1)S(1)}, u32[]{:S(2)}, u32[]{:S(2)}) %collective-permute-start.5) | collective-permute-done | bytes 36896 | tf_op jit(solution)/shard_map/s_col2/ppermute | solution.py:25
  21.6 2.8 %collective-permute-start.10 = (bf16[2,144,128]{2,1,0:T(8,128)(2,1)S(1)}, bf16[2,144,128]{2,1,0:T(8,128)(2,1)S(1)}, u32[]{:S(2)}, u32[]{:S(2)}) collective-permute-start(bf16[2,144,128]{2,1,0:T(8,128)(2,1)S(1)} %pad_maximum_fusion.5), channel_id=1, source_target_pairs={{0,12},{1,13},{2,14},{3,15},{4,8},{5,9},{6,10},{7,11},{8,4},{9,5},... | collective-permute-start | bytes 221192 | tf_op jit(solution)/shard_map/s_col12/ppermute | solution.py:25
  24.4 0.3 collective-permute-start.9
  24.8 0.3 collective-permute-start.8
  25.2 0.0 copy-start.2
  25.2 0.0 copy-start.3
  25.2 0.9 collective-permute-start.7
  26.1 0.8 collective-permute-start.6
  26.9 2.3 %collective-permute-done.9 = bf16[2,144,128]{2,1,0:T(8,128)(2,1)S(1)} collective-permute-done((bf16[2,144,128]{2,1,0:T(8,128)(2,1)S(1)}, bf16[2,144,128]{2,1,0:T(8,128)(2,1)S(1)}, u32[]{:S(2)}, u32[]{:S(2)}) %collective-permute-start.9) | collective-permute-done | bytes 73760 | tf_op jit(solution)/shard_map/s_col8/ppermute | solution.py:25
  29.2 1.5 %collective-permute-done.7.right2b = bf16[2,272,128]{2,1,0:T(8,128)(2,1)S(1)} collective-permute-done((bf16[2,272,128]{2,1,0:T(8,128)(2,1)S(1)}, bf16[2,272,128]{2,1,0:T(8,128)(2,1)S(1)}, u32[]{:S(2)}, u32[]{:S(2)}) %collective-permute-start.7) | collective-permute-done | bytes 139296 | tf_op jit(solution)/shard_map/s_row12/ppermute | solution.py:25
  30.7 5.5 %collective-permute-start.11 = (bf16[8,144,128]{2,1,0:T(8,128)(2,1)S(1)}, bf16[8,144,128]{2,1,0:T(8,128)(2,1)S(1)}, u32[]{:S(2)}, u32[]{:S(2)}) collective-permute-start(bf16[8,144,128]{2,1,0:T(8,128)(2,1)S(1)} %pad_maximum_fusion.left0), channel_id=1, source_target_pairs={{0,1},{1,0},{2,3},{3,2},{4,5},{5,4},{6,7},{7,6},{8,9},{9,8},{10,11... | collective-permute-start | bytes 884744 | tf_op jit(solution)/shard_map/s_col1/ppermute | solution.py:25
  36.2 0.1 pad_add_fusion.at_ref
  36.3 1.1 %collective-permute-done.11.left1 = bf16[8,144,128]{2,1,0:T(8,128)(2,1)S(1)} collective-permute-done((bf16[8,144,128]{2,1,0:T(8,128)(2,1)S(1)}, bf16[8,144,128]{2,1,0:T(8,128)(2,1)S(1)}, u32[]{:S(2)}, u32[]{:S(2)}) %collective-permute-start.11) | collective-permute-done | bytes 294944 | tf_op jit(solution)/shard_map/s_col1/ppermute | solution.py:25
  37.4 17.4 %shard_map.129 = (bf16[1344,128]{1,0:T(8,128)(2,1)S(1)}, bf16[1344,128]{1,0:T(8,128)(2,1)S(1)}, bf16[4,256,128]{2,1,0:T(8,128)(2,1)S(1)}, bf16[4,256,128]{2,1,0:...) custom-call(s32[2]{0:T(128)S(1)} %pad_add_fusion.at_ref, ...), custom_call_target="tpu_custom_call" | custom-call | flops 800000000 | bytes 5000000 | tf_op jit(solution)/shard_map/pallas_call | solution.py:360
  54.8 0.6 collective-permute-start.12
  55.4 0.4 collective-permute-start.13
  55.9 2.3 %collective-permute-start.14 = (bf16[4,256,128]{2,1,0:T(8,128)(2,1)S(1)}, bf16[4,256,128]{2,1,0:T(8,128)(2,1)S(1)}, u32[]{:S(2)}, u32[]{:S(2)}) collective-permute-start(bf16[4,256,128]{2,1,0:T(8,128)(2,1)S(1)} %get-tuple-element.37), channel_id=1, source_target_pairs={{0,192},{16,208},{32,224},{48,240},{64,128},{80,144},{96,160},{112... | collective-permute-start | bytes 786440 | tf_op jit(solution)/shard_map/s_row12/ppermute | solution.py:25
  58.1 0.1 convert_add_fusion
  58.3 1.4 %collective-permute-start.15 = (bf16[576,128]{1,0:T(8,128)(2,1)S(1)}, bf16[576,128]{1,0:T(8,128)(2,1)S(1)}, u32[]{:S(2)}, u32[]{:S(2)}) collective-permute-start(bf16[576,128]{1,0:T(8,128)(2,1)S(1)} %get-tuple-element.61), channel_id=1, source_target_pairs={{0,4},{1,5},{2,6},{3,7},{4,0},{5,1},{6,2},{7,3},{8,12},{9,13},{10,... | collective-permute-start | bytes 442376 | tf_op jit(solution)/shard_map/s_col4/ppermute | solution.py:25
  59.7 2.0 %collective-permute-start.17 = (bf16[576,128]{1,0:T(8,128)(2,1)S(1)}, bf16[576,128]{1,0:T(8,128)(2,1)S(1)}, u32[]{:S(2)}, u32[]{:S(2)}) collective-permute-start(bf16[576,128]{1,0:T(8,128)(2,1)S(1)} %concatenate.37), channel_id=1, source_target_pairs={{0,12},{1,13},{2,14},{3,15},{4,8},{5,9},{6,10},{7,11},{8,4},{9,5},... | collective-permute-start | bytes 442376 | tf_op jit(solution)/shard_map/s_col12/ppermute | solution.py:25
  61.7 0.8 collective-permute-start.16
  62.5 0.5 collective-permute-done.15
  63.1 0.1 collective-permute-done.13
  63.2 1.3 %collective-permute-done.14 = bf16[4,256,128]{2,1,0:T(8,128)(2,1)S(1)} collective-permute-done((bf16[4,256,128]{2,1,0:T(8,128)(2,1)S(1)}, bf16[4,256,128]{2,1,0:T(8,128)(2,1)S(1)}, u32[]{:S(2)}, u32[]{:S(2)}) %collective-permute-start.14) | collective-permute-done | bytes 262176 | tf_op jit(solution)/shard_map/s_row12/ppermute | solution.py:25
  64.5 0.1 convert_add_fusion.2
  64.6 2.3 %collective-permute-start.18 = (bf16[2,256,128]{2,1,0:T(8,128)(2,1)S(1)}, bf16[2,256,128]{2,1,0:T(8,128)(2,1)S(1)}, u32[]{:S(2)}, u32[]{:S(2)}) collective-permute-start(bf16[2,256,128]{2,1,0:T(8,128)(2,1)S(1)} %slice.106), channel_id=1, source_target_pairs={{0,192},{16,208},{32,224},{48,240},{64,128},{80,144},{96,160},{112... | collective-permute-start | bytes 393224 | tf_op jit(solution)/shard_map/s_row12/ppermute | solution.py:25
  66.9 0.1 convert_add_fusion.1
  67.0 0.1 collective-permute-start.19
  67.1 0.0 collective-permute-done.17
  67.1 1.7 %collective-permute-done.16 = bf16[576,128]{1,0:T(8,128)(2,1)S(1)} collective-permute-done((bf16[576,128]{1,0:T(8,128)(2,1)S(1)}, bf16[576,128]{1,0:T(8,128)(2,1)S(1)}, u32[]{:S(2)}, u32[]{:S(2)}) %collective-permute-start.16) | collective-permute-done | bytes 147488 | tf_op jit(solution)/shard_map/s_col8/ppermute | solution.py:25
  68.9 0.1 fusion
  69.0 1.1 %collective-permute-done.18 = bf16[2,256,128]{2,1,0:T(8,128)(2,1)S(1)} collective-permute-done((bf16[2,256,128]{2,1,0:T(8,128)(2,1)S(1)}, bf16[2,256,128]{2,1,0:T(8,128)(2,1)S(1)}, u32[]{:S(2)}, u32[]{:S(2)}) %collective-permute-start.18) | collective-permute-done | bytes 131104 | tf_op jit(solution)/shard_map/s_row12/ppermute | solution.py:25
  70.0 1.2 %collective-permute-done.19 = bf16[2,256,128]{2,1,0:T(8,128)(2,1)S(1)} collective-permute-done((bf16[2,256,128]{2,1,0:T(8,128)(2,1)S(1)}, bf16[2,256,128]{2,1,0:T(8,128)(2,1)S(1)}, u32[]{:S(2)}, u32[]{:S(2)}) %collective-permute-start.19) | collective-permute-done | bytes 131104 | tf_op jit(solution)/shard_map/s_row4/ppermute | solution.py:25
  71.2 4.4 %collective-permute-start.20 = (bf16[448,128]{1,0:T(8,128)(2,1)S(1)}, bf16[448,128]{1,0:T(8,128)(2,1)S(1)}, u32[]{:S(2)}, u32[]{:S(2)}) collective-permute-start(bf16[448,128]{1,0:T(8,128)(2,1)S(1)} %slice.107), channel_id=1, source_target_pairs={{0,2},{1,3},{2,0},{3,1},{4,6},{5,7},{6,4},{7,5},{8,10},{9,11},{10,... | collective-permute-start | bytes 344072 | tf_op jit(solution)/shard_map/s_col2/ppermute | solution.py:25
  75.6 0.1 fusion.1
  75.7 0.7 pad_maximum_fusion.2
  76.4 3.4 %all-to-all-start = ((bf16[4,256,128]{2,1,0:T(8,128)(2,1)}), bf16[4,256,128]{2,1,0:T(8,128)(2,1)S(1)}, u32[]{:S(2)}, u32[]{:S(2)}) async-start(bf16[4,256,128]{2,1,0:T(8,128)(2,1)} %pad_maximum_fusion.2), calls=%async_computation | async-start | bytes 524288 | tf_op jit(solution)/shard_map/all_to_all | solution.py:470
  79.9 0.8 collective-permute-start.23
  80.7 0.8 collective-permute-start.22
  81.5 1.8 %collective-permute-start.21 = (bf16[320,128]{1,0:T(8,128)(2,1)S(1)}, bf16[320,128]{1,0:T(8,128)(2,1)S(1)}, u32[]{:S(2)}, u32[]{:S(2)}) collective-permute-start(bf16[320,128]{1,0:T(8,128)(2,1)S(1)} %fusion.3), channel_id=1, source_target_pairs={{0,64},{16,80},{32,96},{48,112},{64,0},{80,16},{96,32},{112,48},{1... | collective-permute-start | bytes 245768 | tf_op jit(solution)/shard_map/s_row4/ppermute | solution.py:25
  83.2 1.2 %collective-permute-done.23 = bf16[320,128]{1,0:T(8,128)(2,1)S(1)} collective-permute-done((bf16[320,128]{1,0:T(8,128)(2,1)S(1)}, bf16[320,128]{1,0:T(8,128)(2,1)S(1)}, u32[]{:S(2)}, u32[]{:S(2)}) %collective-permute-start.23) | collective-permute-done | bytes 81952 | tf_op jit(solution)/shard_map/s_row12/ppermute | solution.py:25
  84.5 1.0 %collective-permute-done.22 = bf16[320,128]{1,0:T(8,128)(2,1)S(1)} collective-permute-done((bf16[320,128]{1,0:T(8,128)(2,1)S(1)}, bf16[320,128]{1,0:T(8,128)(2,1)S(1)}, u32[]{:S(2)}, u32[]{:S(2)}) %collective-permute-start.22) | collective-permute-done | bytes 81952 | tf_op jit(solution)/shard_map/s_row8/ppermute | solution.py:25
  85.5 0.7 collective-permute-done.21
  86.3 3.2 %collective-permute-start.26 = (bf16[320,128]{1,0:T(8,128)(2,1)S(1)}, bf16[320,128]{1,0:T(8,128)(2,1)S(1)}, u32[]{:S(2)}, u32[]{:S(2)}) collective-permute-start(bf16[320,128]{1,0:T(8,128)(2,1)S(1)} %add_convert_fusion.1), channel_id=1, source_target_pairs={{0,48},{16,32},{32,16},{48,0},{64,112},{80,96},{96,80},{112,64},{1... | collective-permute-start | bytes 245768 | tf_op jit(solution)/shard_map/s_row3/ppermute | solution.py:25
  89.5 0.4 collective-permute-start.24
  89.9 0.6 slice_add_fusion.3
  90.6 1.0 collective-permute-done.26
  91.6 2.2 %collective-permute-done.25 = bf16[320,128]{1,0:T(8,128)(2,1)S(1)} collective-permute-done((bf16[320,128]{1,0:T(8,128)(2,1)S(1)}, bf16[320,128]{1,0:T(8,128)(2,1)S(1)}, u32[]{:S(2)}, u32[]{:S(2)}) %collective-permute-start.25) | collective-permute-done | bytes 81952 | tf_op jit(solution)/shard_map/s_row2/ppermute | solution.py:25
  93.8 6.2 %collective-permute-start.27 = (bf16[320,128]{1,0:T(8,128)(2,1)S(1)}, bf16[320,128]{1,0:T(8,128)(2,1)S(1)}, u32[]{:S(2)}, u32[]{:S(2)}) collective-permute-start(bf16[320,128]{1,0:T(8,128)(2,1)S(1)} %add_convert_fusion), channel_id=1, source_target_pairs={{0,1},{1,0},{2,3},{3,2},{4,5},{5,4},{6,7},{7,6},{8,9},{9,8},{10,11... | collective-permute-start | bytes 245768 | tf_op jit(solution)/shard_map/s_col1/ppermute | solution.py:25
  100.0 0.7 copy.18
  100.7 0.2 collective-permute-done.27
  100.9 0.6 maximum_convert_fusion.1
  101.6 0.7 slice.88
  (55 shorter events, 0.6 us)
Async XLA Ops:
  0.6 0.9 copy-start.6
  1.6 5.6 %copy-start.8 = (s32[8,16]{1,0:T(8,128)S(1)}, s32[8,16]{1,0:T(8,128)}, u32[]{:S(2)}) copy-start(s32[8,16]{1,0:T(8,128)} %param.12) | copy-start | bytes 1540
  1.6 5.7 %copy-start.7 = (bf16[8,16,128]{2,1,0:T(8,128)(2,1)S(1)}, bf16[8,16,128]{2,1,0:T(8,128)(2,1)}, u32[]{:S(2)}) copy-start(bf16[8,16,128]{2,1,0:T(8,128)(2,1)} %param.10) | copy-start | bytes 98308
  1.6 5.7 %collective-permute-start.1 = (bf16[272,128]{1,0:T(8,128)(2,1)S(1)}, bf16[272,128]{1,0:T(8,128)(2,1)S(1)}, u32[]{:S(2)}, u32[]{:S(2)}) collective-permute-start(bf16[272,128]{1,0:T(8,128)(2,1)S(1)} %get-tuple-element.63), channel_id=1, source_target_pairs={{0,32},{16,48},{32,0},{48,16},{64,96},{80,112},{96,64},{112,80},{1... | collective-permute-start | bytes 208904 | tf_op jit(solution)/shard_map/s_row2/ppermute | solution.py:25
  5.5 3.8 %collective-permute-start = (bf16[272,128]{1,0:T(8,128)(2,1)S(1)}, bf16[272,128]{1,0:T(8,128)(2,1)S(1)}, u32[]{:S(2)}, u32[]{:S(2)}) collective-permute-start(bf16[272,128]{1,0:T(8,128)(2,1)S(1)} %get-tuple-element.63), channel_id=1, source_target_pairs={{0,16},{16,0},{32,48},{48,32},{64,80},{80,64},{96,112},{112,96},{1... | collective-permute-start | bytes 208904 | tf_op jit(solution)/shard_map/s_row1/ppermute | solution.py:25
  7.2 5.1 %collective-permute-start.2 = (bf16[272,128]{1,0:T(8,128)(2,1)S(1)}, bf16[272,128]{1,0:T(8,128)(2,1)S(1)}, u32[]{:S(2)}, u32[]{:S(2)}) collective-permute-start(bf16[272,128]{1,0:T(8,128)(2,1)S(1)} %get-tuple-element.63), channel_id=1, source_target_pairs={{0,48},{16,32},{32,16},{48,0},{64,112},{80,96},{96,80},{112,64},{1... | collective-permute-start | bytes 208904 | tf_op jit(solution)/shard_map/s_row3/ppermute | solution.py:25
  12.3 9.3 %collective-permute-start.4 = (bf16[4,272,128]{2,1,0:T(8,128)(2,1)S(1)}, bf16[4,272,128]{2,1,0:T(8,128)(2,1)S(1)}, u32[]{:S(2)}, u32[]{:S(2)}) collective-permute-start(bf16[4,272,128]{2,1,0:T(8,128)(2,1)S(1)} %pad_maximum_fusion.1.right0), channel_id=1, source_target_pairs={{0,192},{16,208},{32,224},{48,240},{64,128},{80,144},{96,160},{112... | collective-permute-start | bytes 835592 | tf_op jit(solution)/shard_map/s_row12/ppermute | solution.py:25
  14.9 6.7 %collective-permute-start.3 = (bf16[4,272,128]{2,1,0:T(8,128)(2,1)S(1)}, bf16[4,272,128]{2,1,0:T(8,128)(2,1)S(1)}, u32[]{:S(2)}, u32[]{:S(2)}) collective-permute-start(bf16[4,272,128]{2,1,0:T(8,128)(2,1)S(1)} %pad_maximum_fusion.1.right0), channel_id=1, source_target_pairs={{0,64},{16,80},{32,96},{48,112},{64,0},{80,16},{96,32},{112,48},{1... | collective-permute-start | bytes 835592 | tf_op jit(solution)/shard_map/s_row4/ppermute | solution.py:25
  14.9 6.7 %collective-permute-start.5 = (bf16[144,128]{1,0:T(8,128)(2,1)S(1)}, bf16[144,128]{1,0:T(8,128)(2,1)S(1)}, u32[]{:S(2)}, u32[]{:S(2)}) collective-permute-start(bf16[144,128]{1,0:T(8,128)(2,1)S(1)} %fusion.5), channel_id=1, source_target_pairs={{0,2},{1,3},{2,0},{3,1},{4,6},{5,7},{6,4},{7,5},{8,10},{9,11},{10,... | collective-permute-start | bytes 110600 | tf_op jit(solution)/shard_map/s_col2/ppermute | solution.py:25
  21.6 5.3 %collective-permute-start.10 = (bf16[2,144,128]{2,1,0:T(8,128)(2,1)S(1)}, bf16[2,144,128]{2,1,0:T(8,128)(2,1)S(1)}, u32[]{:S(2)}, u32[]{:S(2)}) collective-permute-start(bf16[2,144,128]{2,1,0:T(8,128)(2,1)S(1)} %pad_maximum_fusion.5), channel_id=1, source_target_pairs={{0,12},{1,13},{2,14},{3,15},{4,8},{5,9},{6,10},{7,11},{8,4},{9,5},... | collective-permute-start | bytes 221192 | tf_op jit(solution)/shard_map/s_col12/ppermute | solution.py:25
  24.4 4.7 %collective-permute-start.9 = (bf16[2,144,128]{2,1,0:T(8,128)(2,1)S(1)}, bf16[2,144,128]{2,1,0:T(8,128)(2,1)S(1)}, u32[]{:S(2)}, u32[]{:S(2)}) collective-permute-start(bf16[2,144,128]{2,1,0:T(8,128)(2,1)S(1)} %pad_maximum_fusion.5), channel_id=1, source_target_pairs={{0,8},{1,9},{2,10},{3,11},{4,12},{5,13},{6,14},{7,15},{8,0},{9,1},... | collective-permute-start | bytes 221192 | tf_op jit(solution)/shard_map/s_col8/ppermute | solution.py:25
  24.8 4.4 %collective-permute-start.8 = (bf16[2,144,128]{2,1,0:T(8,128)(2,1)S(1)}, bf16[2,144,128]{2,1,0:T(8,128)(2,1)S(1)}, u32[]{:S(2)}, u32[]{:S(2)}) collective-permute-start(bf16[2,144,128]{2,1,0:T(8,128)(2,1)S(1)} %pad_maximum_fusion.5), channel_id=1, source_target_pairs={{0,4},{1,5},{2,6},{3,7},{4,0},{5,1},{6,2},{7,3},{8,12},{9,13},{10,... | collective-permute-start | bytes 221192 | tf_op jit(solution)/shard_map/s_col4/ppermute | solution.py:25
  25.1 12.3 %copy-start = (bf16[8,16,128]{2,1,0:T(8,128)(2,1)S(1)}, bf16[8,16,128]{2,1,0:T(8,128)(2,1)}, u32[]{:S(2)}) copy-start(bf16[8,16,128]{2,1,0:T(8,128)(2,1)} %param.14) | copy-start | bytes 98308
  25.2 12.2 %copy-start.1 = (bf16[128,128]{1,0:T(8,128)(2,1)S(1)}, bf16[128,128]{1,0:T(8,128)(2,1)}, u32[]{:S(2)}) copy-start(bf16[128,128]{1,0:T(8,128)(2,1)} %wq_hbm.1) | copy-start | bytes 98308
  25.2 12.2 %copy-start.2 = (bf16[128,128]{1,0:T(8,128)(2,1)S(1)}, bf16[128,128]{1,0:T(8,128)(2,1)}, u32[]{:S(2)}) copy-start(bf16[128,128]{1,0:T(8,128)(2,1)} %wk_hbm.1) | copy-start | bytes 98308
  25.2 12.2 %copy-start.3 = (bf16[128,128]{1,0:T(8,128)(2,1)S(1)}, bf16[128,128]{1,0:T(8,128)(2,1)}, u32[]{:S(2)}) copy-start(bf16[128,128]{1,0:T(8,128)(2,1)} %wl_hbm.1) | copy-start | bytes 98308
  25.2 12.2 %copy-start.4 = (bf16[128,128]{1,0:T(8,128)(2,1)S(1)}, bf16[128,128]{1,0:T(8,128)(2,1)}, u32[]{:S(2)}) copy-start(bf16[128,128]{1,0:T(8,128)(2,1)} %wr_hbm.1) | copy-start | bytes 98308
  25.2 12.2 %copy-start.5 = (bf16[128,128]{1,0:T(8,128)(2,1)S(1)}, bf16[128,128]{1,0:T(8,128)(2,1)}, u32[]{:S(2)}) copy-start(bf16[128,128]{1,0:T(8,128)(2,1)} %wo_hbm.1) | copy-start | bytes 98308
  25.2 5.5 %collective-permute-start.7 = (bf16[2,272,128]{2,1,0:T(8,128)(2,1)S(1)}, bf16[2,272,128]{2,1,0:T(8,128)(2,1)S(1)}, u32[]{:S(2)}, u32[]{:S(2)}) collective-permute-start(bf16[2,272,128]{2,1,0:T(8,128)(2,1)S(1)} %slice.60), channel_id=1, source_target_pairs={{0,192},{16,208},{32,224},{48,240},{64,128},{80,144},{96,160},{112... | collective-permute-start | bytes 417800 | tf_op jit(solution)/shard_map/s_row12/ppermute | solution.py:25
  26.1 4.6 %collective-permute-start.6 = (bf16[2,272,128]{2,1,0:T(8,128)(2,1)S(1)}, bf16[2,272,128]{2,1,0:T(8,128)(2,1)S(1)}, u32[]{:S(2)}, u32[]{:S(2)}) collective-permute-start(bf16[2,272,128]{2,1,0:T(8,128)(2,1)S(1)} %slice.59), channel_id=1, source_target_pairs={{0,64},{16,80},{32,96},{48,112},{64,0},{80,16},{96,32},{112,48},{1... | collective-permute-start | bytes 417800 | tf_op jit(solution)/shard_map/s_row4/ppermute | solution.py:25
  30.7 6.7 %collective-permute-start.11 = (bf16[8,144,128]{2,1,0:T(8,128)(2,1)S(1)}, bf16[8,144,128]{2,1,0:T(8,128)(2,1)S(1)}, u32[]{:S(2)}, u32[]{:S(2)}) collective-permute-start(bf16[8,144,128]{2,1,0:T(8,128)(2,1)S(1)} %pad_maximum_fusion.left0), channel_id=1, source_target_pairs={{0,1},{1,0},{2,3},{3,2},{4,5},{5,4},{6,7},{7,6},{8,9},{9,8},{10,11... | collective-permute-start | bytes 884744 | tf_op jit(solution)/shard_map/s_col1/ppermute | solution.py:25
  54.8 3.3 %collective-permute-start.12 = (bf16[1344,128]{1,0:T(8,128)(2,1)S(1)}, bf16[1344,128]{1,0:T(8,128)(2,1)S(1)}, u32[]{:S(2)}, u32[]{:S(2)}) collective-permute-start(bf16[1344,128]{1,0:T(8,128)(2,1)S(1)} %get-tuple-element.35), channel_id=1, source_target_pairs={{0,1},{1,0},{2,3},{3,2},{4,5},{5,4},{6,7},{7,6},{8,9},{9,8},{10,11... | collective-permute-start | bytes 1032200 | tf_op jit(solution)/shard_map/s_col1/ppermute | solution.py:25
  55.4 7.8 %collective-permute-start.13 = (bf16[4,256,128]{2,1,0:T(8,128)(2,1)S(1)}, bf16[4,256,128]{2,1,0:T(8,128)(2,1)S(1)}, u32[]{:S(2)}, u32[]{:S(2)}) collective-permute-start(bf16[4,256,128]{2,1,0:T(8,128)(2,1)S(1)} %get-tuple-element.36), channel_id=1, source_target_pairs={{0,64},{16,80},{32,96},{48,112},{64,0},{80,16},{96,32},{112,48},{1... | collective-permute-start | bytes 786440 | tf_op jit(solution)/shard_map/s_row4/ppermute | solution.py:25
  55.9 8.7 %collective-permute-start.14 = (bf16[4,256,128]{2,1,0:T(8,128)(2,1)S(1)}, bf16[4,256,128]{2,1,0:T(8,128)(2,1)S(1)}, u32[]{:S(2)}, u32[]{:S(2)}) collective-permute-start(bf16[4,256,128]{2,1,0:T(8,128)(2,1)S(1)} %get-tuple-element.37), channel_id=1, source_target_pairs={{0,192},{16,208},{32,224},{48,240},{64,128},{80,144},{96,160},{112... | collective-permute-start | bytes 786440 | tf_op jit(solution)/shard_map/s_row12/ppermute | solution.py:25
  58.3 4.8 %collective-permute-start.15 = (bf16[576,128]{1,0:T(8,128)(2,1)S(1)}, bf16[576,128]{1,0:T(8,128)(2,1)S(1)}, u32[]{:S(2)}, u32[]{:S(2)}) collective-permute-start(bf16[576,128]{1,0:T(8,128)(2,1)S(1)} %get-tuple-element.61), channel_id=1, source_target_pairs={{0,4},{1,5},{2,6},{3,7},{4,0},{5,1},{6,2},{7,3},{8,12},{9,13},{10,... | collective-permute-start | bytes 442376 | tf_op jit(solution)/shard_map/s_col4/ppermute | solution.py:25
  59.7 7.4 %collective-permute-start.17 = (bf16[576,128]{1,0:T(8,128)(2,1)S(1)}, bf16[576,128]{1,0:T(8,128)(2,1)S(1)}, u32[]{:S(2)}, u32[]{:S(2)}) collective-permute-start(bf16[576,128]{1,0:T(8,128)(2,1)S(1)} %concatenate.37), channel_id=1, source_target_pairs={{0,12},{1,13},{2,14},{3,15},{4,8},{5,9},{6,10},{7,11},{8,4},{9,5},... | collective-permute-start | bytes 442376 | tf_op jit(solution)/shard_map/s_col12/ppermute | solution.py:25
  61.7 7.2 %collective-permute-start.16 = (bf16[576,128]{1,0:T(8,128)(2,1)S(1)}, bf16[576,128]{1,0:T(8,128)(2,1)S(1)}, u32[]{:S(2)}, u32[]{:S(2)}) collective-permute-start(bf16[576,128]{1,0:T(8,128)(2,1)S(1)} %get-tuple-element.60), channel_id=1, source_target_pairs={{0,8},{1,9},{2,10},{3,11},{4,12},{5,13},{6,14},{7,15},{8,0},{9,1},... | collective-permute-start | bytes 442376 | tf_op jit(solution)/shard_map/s_col8/ppermute | solution.py:25
  64.6 5.4 %collective-permute-start.18 = (bf16[2,256,128]{2,1,0:T(8,128)(2,1)S(1)}, bf16[2,256,128]{2,1,0:T(8,128)(2,1)S(1)}, u32[]{:S(2)}, u32[]{:S(2)}) collective-permute-start(bf16[2,256,128]{2,1,0:T(8,128)(2,1)S(1)} %slice.106), channel_id=1, source_target_pairs={{0,192},{16,208},{32,224},{48,240},{64,128},{80,144},{96,160},{112... | collective-permute-start | bytes 393224 | tf_op jit(solution)/shard_map/s_row12/ppermute | solution.py:25
  67.0 4.2 %collective-permute-start.19 = (bf16[2,256,128]{2,1,0:T(8,128)(2,1)S(1)}, bf16[2,256,128]{2,1,0:T(8,128)(2,1)S(1)}, u32[]{:S(2)}, u32[]{:S(2)}) collective-permute-start(bf16[2,256,128]{2,1,0:T(8,128)(2,1)S(1)} %slice.105), channel_id=1, source_target_pairs={{0,64},{16,80},{32,96},{48,112},{64,0},{80,16},{96,32},{112,48},{1... | collective-permute-start | bytes 393224 | tf_op jit(solution)/shard_map/s_row4/ppermute | solution.py:25
  71.2 8.6 %collective-permute-start.20 = (bf16[448,128]{1,0:T(8,128)(2,1)S(1)}, bf16[448,128]{1,0:T(8,128)(2,1)S(1)}, u32[]{:S(2)}, u32[]{:S(2)}) collective-permute-start(bf16[448,128]{1,0:T(8,128)(2,1)S(1)} %slice.107), channel_id=1, source_target_pairs={{0,2},{1,3},{2,0},{3,1},{4,6},{5,7},{6,4},{7,5},{8,10},{9,11},{10,... | collective-permute-start | bytes 344072 | tf_op jit(solution)/shard_map/s_col2/ppermute | solution.py:25
  76.4 9.9 %all-to-all-start = ((bf16[4,256,128]{2,1,0:T(8,128)(2,1)}), bf16[4,256,128]{2,1,0:T(8,128)(2,1)S(1)}, u32[]{:S(2)}, u32[]{:S(2)}) async-start(bf16[4,256,128]{2,1,0:T(8,128)(2,1)} %pad_maximum_fusion.2), calls=%async_computation | async-start | bytes 524288 | tf_op jit(solution)/shard_map/all_to_all | solution.py:470
  79.9 4.6 %collective-permute-start.23 = (bf16[320,128]{1,0:T(8,128)(2,1)S(1)}, bf16[320,128]{1,0:T(8,128)(2,1)S(1)}, u32[]{:S(2)}, u32[]{:S(2)}) collective-permute-start(bf16[320,128]{1,0:T(8,128)(2,1)S(1)} %fusion.3), channel_id=1, source_target_pairs={{0,192},{16,208},{32,224},{48,240},{64,128},{80,144},{96,160},{112... | collective-permute-start | bytes 245768 | tf_op jit(solution)/shard_map/s_row12/ppermute | solution.py:25
  80.7 4.8 %collective-permute-start.22 = (bf16[320,128]{1,0:T(8,128)(2,1)S(1)}, bf16[320,128]{1,0:T(8,128)(2,1)S(1)}, u32[]{:S(2)}, u32[]{:S(2)}) collective-permute-start(bf16[320,128]{1,0:T(8,128)(2,1)S(1)} %fusion.3), channel_id=1, source_target_pairs={{0,128},{16,144},{32,160},{48,176},{64,192},{80,208},{96,224},{112... | collective-permute-start | bytes 245768 | tf_op jit(solution)/shard_map/s_row8/ppermute | solution.py:25
  81.5 4.8 %collective-permute-start.21 = (bf16[320,128]{1,0:T(8,128)(2,1)S(1)}, bf16[320,128]{1,0:T(8,128)(2,1)S(1)}, u32[]{:S(2)}, u32[]{:S(2)}) collective-permute-start(bf16[320,128]{1,0:T(8,128)(2,1)S(1)} %fusion.3), channel_id=1, source_target_pairs={{0,64},{16,80},{32,96},{48,112},{64,0},{80,16},{96,32},{112,48},{1... | collective-permute-start | bytes 245768 | tf_op jit(solution)/shard_map/s_row4/ppermute | solution.py:25
  86.3 5.3 %collective-permute-start.26 = (bf16[320,128]{1,0:T(8,128)(2,1)S(1)}, bf16[320,128]{1,0:T(8,128)(2,1)S(1)}, u32[]{:S(2)}, u32[]{:S(2)}) collective-permute-start(bf16[320,128]{1,0:T(8,128)(2,1)S(1)} %add_convert_fusion.1), channel_id=1, source_target_pairs={{0,48},{16,32},{32,16},{48,0},{64,112},{80,96},{96,80},{112,64},{1... | collective-permute-start | bytes 245768 | tf_op jit(solution)/shard_map/s_row3/ppermute | solution.py:25
  89.5 4.2 %collective-permute-start.25 = (bf16[320,128]{1,0:T(8,128)(2,1)S(1)}, bf16[320,128]{1,0:T(8,128)(2,1)S(1)}, u32[]{:S(2)}, u32[]{:S(2)}) collective-permute-start(bf16[320,128]{1,0:T(8,128)(2,1)S(1)} %add_convert_fusion.1), channel_id=1, source_target_pairs={{0,32},{16,48},{32,0},{48,16},{64,96},{80,112},{96,64},{112,80},{1... | collective-permute-start | bytes 245768 | tf_op jit(solution)/shard_map/s_row2/ppermute | solution.py:25
  89.5 4.2 %collective-permute-start.24 = (bf16[320,128]{1,0:T(8,128)(2,1)S(1)}, bf16[320,128]{1,0:T(8,128)(2,1)S(1)}, u32[]{:S(2)}, u32[]{:S(2)}) collective-permute-start(bf16[320,128]{1,0:T(8,128)(2,1)S(1)} %add_convert_fusion.1), channel_id=1, source_target_pairs={{0,16},{16,0},{32,48},{48,32},{64,80},{80,64},{96,112},{112,96},{1... | collective-permute-start | bytes 245768 | tf_op jit(solution)/shard_map/s_row1/ppermute | solution.py:25
  93.8 7.1 %collective-permute-start.27 = (bf16[320,128]{1,0:T(8,128)(2,1)S(1)}, bf16[320,128]{1,0:T(8,128)(2,1)S(1)}, u32[]{:S(2)}, u32[]{:S(2)}) collective-permute-start(bf16[320,128]{1,0:T(8,128)(2,1)S(1)} %add_convert_fusion), channel_id=1, source_target_pairs={{0,1},{1,0},{2,3},{3,2},{4,5},{5,4},{6,7},{7,6},{8,9},{9,8},{10,11... | collective-permute-start | bytes 245768 | tf_op jit(solution)/shard_map/s_col1/ppermute | solution.py:25

commit v4 on v3

--- a/solution.py
+++ b/solution.py
@@ -26,12 +26,13 @@
 
 
 def gather(left, right):
-    line = jnp.stack([right] + [send(right, "row", k) for k in (1, 2, 3)])
-    line, left = lax.optimization_barrier((line, left))
+    came = [send(right, "row", k) for k in (1, 2, 3)]
+    came[0], left = lax.optimization_barrier((came[0], left))
+    line = jnp.stack([right] + came)
     near = send(line, "row", 4)
     far = send(line, "row", 12)
     pair = jnp.stack([left, send(left, "col", 2)])
-    near, far, pair = lax.optimization_barrier((near, far, pair))
+    near, pair = lax.optimization_barrier((near, pair))
     first = send(far[:2], "row", 4)
     second = send(near[2:], "row", 12)
     quads = jnp.concatenate([pair] + [send(pair, "col", k) for k in (4, 8, 12)])
@@ -257,7 +258,7 @@
                     ]
         return 0
 
-    lax.fori_loop(0, 8, score_row, 0, unroll=2)
+    lax.fori_loop(0, 8, score_row, 0, unroll=4)
     grad_row(7)
 
     for i in range(8):
@@ -318,7 +319,7 @@
                 gql[i, lower, :] = gl[n]
         return 0
 
-    lax.fori_loop(0, 16, gradients, 0)
+    lax.fori_loop(0, 16, gradients, 0, unroll=2)
 
     def finish(n, _):
         g = gql[n].astype(BF)

time: 103 us -> 102 us (level)
  starting transfers between devices: 54.3 us -> 52.7 us
  waiting for transfers between devices: 24.3 us -> 25.5 us
    ppermute x28, starting transfers between devices: 50.9 us -> 49.3 us  [send(): return lax.ppermute(block, axis, flip(k))]
    ppermute x28, waiting for transfers between devices: 24.3 us -> 25.5 us  [send(): return lax.ppermute(block, axis, flip(k))]
  transfers between devices with their start and end apart: 29 -> 29, of which waited for: 18 -> 19; matrix products, arithmetic and copies ran while one was open for 3% -> 3% of each run, Pallas kernels for 0% -> 0%
where the time goes in v4:
time: 102 us; the launch traced here: 101 us
  starting transfers between devices  52.7 us (52%)
  waiting for transfers between devices  25.5 us (25%)
  Pallas kernels  17 us (17%)
  other arithmetic  3.49 us (3%)
  local copies, waits for them, and re-layouts  1.89 us (2%)
    ppermute x28, starting transfers between devices, send(): return lax.ppermute(block, axis, flip(k))  49.3 us
    ppermute x28, waiting for transfers between devices, send(): return lax.ppermute(block, axis, flip(k))  25.5 us
    pallas_call x1, Pallas kernels, triples(): pl.pallas_call(triple_kernel, out_shape=(jax.ShapeDtypeStruct((1344, 128)...  17 us
    all_to_all x1, starting transfers between devices, body(): right_came = lax.all_to_all(low, 'row', 0, 0, axis_index_groups=LINES)  3.41 us
  transfers between devices with their start and end apart: 29, of which 19 were waited for; matrix products, arithmetic and copies ran while one was open for 3% of the time, Pallas kernels for 0%

profile of v4, /device:TPU:1, one launch (start us, length us, event | category | flops | bytes accessed | tf_op | source)
XLA Modules:
  0.0 101.5 jit_solution(10685032711955579029)
XLA Ops:
  0.6 0.7 convert_bitcast_fusion
  1.4 0.1 copy.17
  1.5 0.1 tile.9
  1.6 0.0 copy-start.8
  1.6 3.9 %collective-permute-start.1 = (bf16[272,128]{1,0:T(8,128)(2,1)S(1)}, bf16[272,128]{1,0:T(8,128)(2,1)S(1)}, u32[]{:S(2)}, u32[]{:S(2)}) collective-permute-start(bf16[272,128]{1,0:T(8,128)(2,1)S(1)} %get-tuple-element.61), channel_id=1, source_target_pairs={{0,32},{16,48},{32,0},{48,16},{64,96},{80,112},{96,64},{112,80},{1... | collective-permute-start | bytes 208904 | tf_op jit(solution)/shard_map/s_row2/ppermute | solution.py:25
  5.5 1.6 %collective-permute-start = (bf16[272,128]{1,0:T(8,128)(2,1)S(1)}, bf16[272,128]{1,0:T(8,128)(2,1)S(1)}, u32[]{:S(2)}, u32[]{:S(2)}) collective-permute-start(bf16[272,128]{1,0:T(8,128)(2,1)S(1)} %get-tuple-element.61), channel_id=1, source_target_pairs={{0,16},{16,0},{32,48},{48,32},{64,80},{80,64},{96,112},{112,96},{1... | collective-permute-start | bytes 208904 | tf_op jit(solution)/shard_map/s_row1/ppermute | solution.py:25
  7.2 0.1 tile.21
  7.3 2.0 %collective-permute-done = bf16[272,128]{1,0:T(8,128)(2,1)S(1)} collective-permute-done((bf16[272,128]{1,0:T(8,128)(2,1)S(1)}, bf16[272,128]{1,0:T(8,128)(2,1)S(1)}, u32[]{:S(2)}, u32[]{:S(2)}) %collective-permute-start) | collective-permute-done | bytes 69664 | tf_op jit(solution)/shard_map/s_row1/ppermute | solution.py:25
  9.3 2.9 %collective-permute-done.2 = bf16[272,128]{1,0:T(8,128)(2,1)S(1)} collective-permute-done((bf16[272,128]{1,0:T(8,128)(2,1)S(1)}, bf16[272,128]{1,0:T(8,128)(2,1)S(1)}, u32[]{:S(2)}, u32[]{:S(2)}) %collective-permute-start.2) | collective-permute-done | bytes 69664 | tf_op jit(solution)/shard_map/s_row3/ppermute | solution.py:25
  12.3 1.3 %collective-permute-start.5 = (bf16[4,272,128]{2,1,0:T(8,128)(2,1)S(1)}, bf16[4,272,128]{2,1,0:T(8,128)(2,1)S(1)}, u32[]{:S(2)}, u32[]{:S(2)}) collective-permute-start(bf16[4,272,128]{2,1,0:T(8,128)(2,1)S(1)} %pad_maximum_fusion.1.right0), channel_id=1, source_target_pairs={{0,64},{16,80},{32,96},{48,112},{64,0},{80,16},{96,32},{112,48},{1... | collective-permute-start | bytes 835592 | tf_op jit(solution)/shard_map/s_row4/ppermute | solution.py:25
  13.6 1.8 %collective-permute-start.3 = (bf16[4,272,128]{2,1,0:T(8,128)(2,1)S(1)}, bf16[4,272,128]{2,1,0:T(8,128)(2,1)S(1)}, u32[]{:S(2)}, u32[]{:S(2)}) collective-permute-start(bf16[4,272,128]{2,1,0:T(8,128)(2,1)S(1)} %pad_maximum_fusion.1.right0), channel_id=1, source_target_pairs={{0,192},{16,208},{32,224},{48,240},{64,128},{80,144},{96,160},{112... | collective-permute-start | bytes 835592 | tf_op jit(solution)/shard_map/s_row12/ppermute | solution.py:25
  15.4 4.7 %collective-permute-start.6 = (bf16[144,128]{1,0:T(8,128)(2,1)S(1)}, bf16[144,128]{1,0:T(8,128)(2,1)S(1)}, u32[]{:S(2)}, u32[]{:S(2)}) collective-permute-start(bf16[144,128]{1,0:T(8,128)(2,1)S(1)} %fusion.5), channel_id=1, source_target_pairs={{0,2},{1,3},{2,0},{3,1},{4,6},{5,7},{6,4},{7,5},{8,10},{9,11},{10,... | collective-permute-start | bytes 110600 | tf_op jit(solution)/shard_map/s_col2/ppermute | solution.py:25
  20.1 2.0 %collective-permute-done.6 = bf16[144,128]{1,0:T(8,128)(2,1)S(1)} collective-permute-done((bf16[144,128]{1,0:T(8,128)(2,1)S(1)}, bf16[144,128]{1,0:T(8,128)(2,1)S(1)}, u32[]{:S(2)}, u32[]{:S(2)}) %collective-permute-start.6) | collective-permute-done | bytes 36896 | tf_op jit(solution)/shard_map/s_col2/ppermute | solution.py:25
  22.1 2.8 %collective-permute-start.10 = (bf16[2,144,128]{2,1,0:T(8,128)(2,1)S(1)}, bf16[2,144,128]{2,1,0:T(8,128)(2,1)S(1)}, u32[]{:S(2)}, u32[]{:S(2)}) collective-permute-start(bf16[2,144,128]{2,1,0:T(8,128)(2,1)S(1)} %pad_maximum_fusion.5), channel_id=1, source_target_pairs={{0,12},{1,13},{2,14},{3,15},{4,8},{5,9},{6,10},{7,11},{8,4},{9,5},... | collective-permute-start | bytes 221192 | tf_op jit(solution)/shard_map/s_col12/ppermute | solution.py:25
  25.0 0.3 collective-permute-start.9
  25.3 0.3 collective-permute-start.8
  25.7 0.9 collective-permute-start.7
  26.6 0.0 copy-start
  26.7 0.0 copy-start.3
  26.7 0.1 collective-permute-start.4
  26.8 0.3 collective-permute-done.10
  27.1 2.6 %collective-permute-done.9 = bf16[2,144,128]{2,1,0:T(8,128)(2,1)S(1)} collective-permute-done((bf16[2,144,128]{2,1,0:T(8,128)(2,1)S(1)}, bf16[2,144,128]{2,1,0:T(8,128)(2,1)S(1)}, u32[]{:S(2)}, u32[]{:S(2)}) %collective-permute-start.9) | collective-permute-done | bytes 73760 | tf_op jit(solution)/shard_map/s_col8/ppermute | solution.py:25
  29.7 1.4 %collective-permute-done.7.right2b = bf16[2,272,128]{2,1,0:T(8,128)(2,1)S(1)} collective-permute-done((bf16[2,272,128]{2,1,0:T(8,128)(2,1)S(1)}, bf16[2,272,128]{2,1,0:T(8,128)(2,1)S(1)}, u32[]{:S(2)}, u32[]{:S(2)}) %collective-permute-start.7) | collective-permute-done | bytes 139296 | tf_op jit(solution)/shard_map/s_row12/ppermute | solution.py:25
  31.2 5.6 %collective-permute-start.11 = (bf16[8,144,128]{2,1,0:T(8,128)(2,1)S(1)}, bf16[8,144,128]{2,1,0:T(8,128)(2,1)S(1)}, u32[]{:S(2)}, u32[]{:S(2)}) collective-permute-start(bf16[8,144,128]{2,1,0:T(8,128)(2,1)S(1)} %pad_maximum_fusion.left0), channel_id=1, source_target_pairs={{0,1},{1,0},{2,3},{3,2},{4,5},{5,4},{6,7},{7,6},{8,9},{9,8},{10,11... | collective-permute-start | bytes 884744 | tf_op jit(solution)/shard_map/s_col1/ppermute | solution.py:25
  36.8 0.1 pad_add_fusion.at_ref
  36.9 1.1 %collective-permute-done.11.left1 = bf16[8,144,128]{2,1,0:T(8,128)(2,1)S(1)} collective-permute-done((bf16[8,144,128]{2,1,0:T(8,128)(2,1)S(1)}, bf16[8,144,128]{2,1,0:T(8,128)(2,1)S(1)}, u32[]{:S(2)}, u32[]{:S(2)}) %collective-permute-start.11) | collective-permute-done | bytes 294944 | tf_op jit(solution)/shard_map/s_col1/ppermute | solution.py:25
  38.0 17.0 %shard_map.129 = (bf16[1344,128]{1,0:T(8,128)(2,1)S(1)}, bf16[1344,128]{1,0:T(8,128)(2,1)S(1)}, bf16[4,256,128]{2,1,0:T(8,128)(2,1)S(1)}, bf16[4,256,128]{2,1,0:...) custom-call(s32[2]{0:T(128)S(1)} %pad_add_fusion.at_ref, ...), custom_call_target="tpu_custom_call" | custom-call | flops 800000000 | bytes 5000000 | tf_op jit(solution)/shard_map/pallas_call | solution.py:361
  55.0 0.5 collective-permute-start.12
  55.5 1.8 %collective-permute-start.14 = (bf16[4,256,128]{2,1,0:T(8,128)(2,1)S(1)}, bf16[4,256,128]{2,1,0:T(8,128)(2,1)S(1)}, u32[]{:S(2)}, u32[]{:S(2)}) collective-permute-start(bf16[4,256,128]{2,1,0:T(8,128)(2,1)S(1)} %get-tuple-element.35), channel_id=1, source_target_pairs={{0,192},{16,208},{32,224},{48,240},{64,128},{80,144},{96,160},{112... | collective-permute-start | bytes 786440 | tf_op jit(solution)/shard_map/s_row12/ppermute | solution.py:25
  57.3 0.1 convert_add_fusion
  57.5 1.4 %collective-permute-start.15 = (bf16[576,128]{1,0:T(8,128)(2,1)S(1)}, bf16[576,128]{1,0:T(8,128)(2,1)S(1)}, u32[]{:S(2)}, u32[]{:S(2)}) collective-permute-start(bf16[576,128]{1,0:T(8,128)(2,1)S(1)} %get-tuple-element.59), channel_id=1, source_target_pairs={{0,4},{1,5},{2,6},{3,7},{4,0},{5,1},{6,2},{7,3},{8,12},{9,13},{10,... | collective-permute-start | bytes 442376 | tf_op jit(solution)/shard_map/s_col4/ppermute | solution.py:25
  58.9 2.0 %collective-permute-start.17 = (bf16[576,128]{1,0:T(8,128)(2,1)S(1)}, bf16[576,128]{1,0:T(8,128)(2,1)S(1)}, u32[]{:S(2)}, u32[]{:S(2)}) collective-permute-start(bf16[576,128]{1,0:T(8,128)(2,1)S(1)} %concatenate.37), channel_id=1, source_target_pairs={{0,12},{1,13},{2,14},{3,15},{4,8},{5,9},{6,10},{7,11},{8,4},{9,5},... | collective-permute-start | bytes 442376 | tf_op jit(solution)/shard_map/s_col12/ppermute | solution.py:25
  60.9 0.8 collective-permute-start.16
  61.7 0.8 collective-permute-done.15
  62.6 0.7 collective-permute-done.13
  63.3 1.2 %collective-permute-done.14 = bf16[4,256,128]{2,1,0:T(8,128)(2,1)S(1)} collective-permute-done((bf16[4,256,128]{2,1,0:T(8,128)(2,1)S(1)}, bf16[4,256,128]{2,1,0:T(8,128)(2,1)S(1)}, u32[]{:S(2)}, u32[]{:S(2)}) %collective-permute-start.14) | collective-permute-done | bytes 262176 | tf_op jit(solution)/shard_map/s_row12/ppermute | solution.py:25
  64.4 0.1 convert_add_fusion.2
  64.5 1.9 %collective-permute-start.18 = (bf16[2,256,128]{2,1,0:T(8,128)(2,1)S(1)}, bf16[2,256,128]{2,1,0:T(8,128)(2,1)S(1)}, u32[]{:S(2)}, u32[]{:S(2)}) collective-permute-start(bf16[2,256,128]{2,1,0:T(8,128)(2,1)S(1)} %slice.107), channel_id=1, source_target_pairs={{0,192},{16,208},{32,224},{48,240},{64,128},{80,144},{96,160},{112... | collective-permute-start | bytes 393224 | tf_op jit(solution)/shard_map/s_row12/ppermute | solution.py:25
  66.4 0.1 convert_add_fusion.1
  66.5 0.1 collective-permute-start.19
  66.6 1.7 %collective-permute-done.16 = bf16[576,128]{1,0:T(8,128)(2,1)S(1)} collective-permute-done((bf16[576,128]{1,0:T(8,128)(2,1)S(1)}, bf16[576,128]{1,0:T(8,128)(2,1)S(1)}, u32[]{:S(2)}, u32[]{:S(2)}) %collective-permute-start.16) | collective-permute-done | bytes 147488 | tf_op jit(solution)/shard_map/s_col8/ppermute | solution.py:25
  68.4 0.1 fusion
  68.4 1.2 %collective-permute-done.18 = bf16[2,256,128]{2,1,0:T(8,128)(2,1)S(1)} collective-permute-done((bf16[2,256,128]{2,1,0:T(8,128)(2,1)S(1)}, bf16[2,256,128]{2,1,0:T(8,128)(2,1)S(1)}, u32[]{:S(2)}, u32[]{:S(2)}) %collective-permute-start.18) | collective-permute-done | bytes 131104 | tf_op jit(solution)/shard_map/s_row12/ppermute | solution.py:25
  69.6 1.1 %collective-permute-done.19 = bf16[2,256,128]{2,1,0:T(8,128)(2,1)S(1)} collective-permute-done((bf16[2,256,128]{2,1,0:T(8,128)(2,1)S(1)}, bf16[2,256,128]{2,1,0:T(8,128)(2,1)S(1)}, u32[]{:S(2)}, u32[]{:S(2)}) %collective-permute-start.19) | collective-permute-done | bytes 131104 | tf_op jit(solution)/shard_map/s_row4/ppermute | solution.py:25
  70.7 4.4 %collective-permute-start.20 = (bf16[448,128]{1,0:T(8,128)(2,1)S(1)}, bf16[448,128]{1,0:T(8,128)(2,1)S(1)}, u32[]{:S(2)}, u32[]{:S(2)}) collective-permute-start(bf16[448,128]{1,0:T(8,128)(2,1)S(1)} %slice.108), channel_id=1, source_target_pairs={{0,2},{1,3},{2,0},{3,1},{4,6},{5,7},{6,4},{7,5},{8,10},{9,11},{10,... | collective-permute-start | bytes 344072 | tf_op jit(solution)/shard_map/s_col2/ppermute | solution.py:25
  75.1 0.1 fusion.1
  75.2 0.7 pad_maximum_fusion.2
  75.9 3.4 %all-to-all-start = ((bf16[4,256,128]{2,1,0:T(8,128)(2,1)}), bf16[4,256,128]{2,1,0:T(8,128)(2,1)S(1)}, u32[]{:S(2)}, u32[]{:S(2)}) async-start(bf16[4,256,128]{2,1,0:T(8,128)(2,1)} %pad_maximum_fusion.2), calls=%async_computation | async-start | bytes 524288 | tf_op jit(solution)/shard_map/all_to_all | solution.py:471
  79.4 1.1 %collective-permute-start.23 = (bf16[320,128]{1,0:T(8,128)(2,1)S(1)}, bf16[320,128]{1,0:T(8,128)(2,1)S(1)}, u32[]{:S(2)}, u32[]{:S(2)}) collective-permute-start(bf16[320,128]{1,0:T(8,128)(2,1)S(1)} %fusion.3), channel_id=1, source_target_pairs={{0,192},{16,208},{32,224},{48,240},{64,128},{80,144},{96,160},{112... | collective-permute-start | bytes 245768 | tf_op jit(solution)/shard_map/s_row12/ppermute | solution.py:25
  80.4 0.8 collective-permute-start.22
  81.2 1.8 %collective-permute-start.21 = (bf16[320,128]{1,0:T(8,128)(2,1)S(1)}, bf16[320,128]{1,0:T(8,128)(2,1)S(1)}, u32[]{:S(2)}, u32[]{:S(2)}) collective-permute-start(bf16[320,128]{1,0:T(8,128)(2,1)S(1)} %fusion.3), channel_id=1, source_target_pairs={{0,64},{16,80},{32,96},{48,112},{64,0},{80,16},{96,32},{112,48},{1... | collective-permute-start | bytes 245768 | tf_op jit(solution)/shard_map/s_row4/ppermute | solution.py:25
  82.9 1.2 %collective-permute-done.23 = bf16[320,128]{1,0:T(8,128)(2,1)S(1)} collective-permute-done((bf16[320,128]{1,0:T(8,128)(2,1)S(1)}, bf16[320,128]{1,0:T(8,128)(2,1)S(1)}, u32[]{:S(2)}, u32[]{:S(2)}) %collective-permute-start.23) | collective-permute-done | bytes 81952 | tf_op jit(solution)/shard_map/s_row12/ppermute | solution.py:25
  84.2 1.0 %collective-permute-done.22 = bf16[320,128]{1,0:T(8,128)(2,1)S(1)} collective-permute-done((bf16[320,128]{1,0:T(8,128)(2,1)S(1)}, bf16[320,128]{1,0:T(8,128)(2,1)S(1)}, u32[]{:S(2)}, u32[]{:S(2)}) %collective-permute-start.22) | collective-permute-done | bytes 81952 | tf_op jit(solution)/shard_map/s_row8/ppermute | solution.py:25
  85.2 0.7 collective-permute-done.21
  86.0 3.0 %collective-permute-start.26 = (bf16[320,128]{1,0:T(8,128)(2,1)S(1)}, bf16[320,128]{1,0:T(8,128)(2,1)S(1)}, u32[]{:S(2)}, u32[]{:S(2)}) collective-permute-start(bf16[320,128]{1,0:T(8,128)(2,1)S(1)} %add_convert_fusion.1), channel_id=1, source_target_pairs={{0,48},{16,32},{32,16},{48,0},{64,112},{80,96},{96,80},{112,64},{1... | collective-permute-start | bytes 245768 | tf_op jit(solution)/shard_map/s_row3/ppermute | solution.py:25
  89.0 0.6 collective-permute-start.24
  89.6 0.6 slice_add_fusion.3
  90.2 0.9 collective-permute-done.26
  91.1 2.3 %collective-permute-done.25 = bf16[320,128]{1,0:T(8,128)(2,1)S(1)} collective-permute-done((bf16[320,128]{1,0:T(8,128)(2,1)S(1)}, bf16[320,128]{1,0:T(8,128)(2,1)S(1)}, u32[]{:S(2)}, u32[]{:S(2)}) %collective-permute-start.25) | collective-permute-done | bytes 81952 | tf_op jit(solution)/shard_map/s_row2/ppermute | solution.py:25
  93.5 5.6 %collective-permute-start.27 = (bf16[320,128]{1,0:T(8,128)(2,1)S(1)}, bf16[320,128]{1,0:T(8,128)(2,1)S(1)}, u32[]{:S(2)}, u32[]{:S(2)}) collective-permute-start(bf16[320,128]{1,0:T(8,128)(2,1)S(1)} %add_convert_fusion), channel_id=1, source_target_pairs={{0,1},{1,0},{2,3},{3,2},{4,5},{5,4},{6,7},{7,6},{8,9},{9,8},{10,11... | collective-permute-start | bytes 245768 | tf_op jit(solution)/shard_map/s_col1/ppermute | solution.py:25
  99.2 0.7 copy.18
  99.9 0.2 collective-permute-done.27
  100.1 0.6 maximum_convert_fusion.1
  100.8 0.7 slice.89
  (55 shorter events, 0.6 us)
Async XLA Ops:
  0.6 0.9 copy-start.6
  1.6 5.6 %copy-start.8 = (s32[8,16]{1,0:T(8,128)S(1)}, s32[8,16]{1,0:T(8,128)}, u32[]{:S(2)}) copy-start(s32[8,16]{1,0:T(8,128)} %param.12) | copy-start | bytes 1540
  1.6 5.7 %copy-start.7 = (bf16[8,16,128]{2,1,0:T(8,128)(2,1)S(1)}, bf16[8,16,128]{2,1,0:T(8,128)(2,1)}, u32[]{:S(2)}) copy-start(bf16[8,16,128]{2,1,0:T(8,128)(2,1)} %param.10) | copy-start | bytes 98308
  1.6 7.7 %collective-permute-start.1 = (bf16[272,128]{1,0:T(8,128)(2,1)S(1)}, bf16[272,128]{1,0:T(8,128)(2,1)S(1)}, u32[]{:S(2)}, u32[]{:S(2)}) collective-permute-start(bf16[272,128]{1,0:T(8,128)(2,1)S(1)} %get-tuple-element.61), channel_id=1, source_target_pairs={{0,32},{16,48},{32,0},{48,16},{64,96},{80,112},{96,64},{112,80},{1... | collective-permute-start | bytes 208904 | tf_op jit(solution)/shard_map/s_row2/ppermute | solution.py:25
  5.5 3.8 %collective-permute-start = (bf16[272,128]{1,0:T(8,128)(2,1)S(1)}, bf16[272,128]{1,0:T(8,128)(2,1)S(1)}, u32[]{:S(2)}, u32[]{:S(2)}) collective-permute-start(bf16[272,128]{1,0:T(8,128)(2,1)S(1)} %get-tuple-element.61), channel_id=1, source_target_pairs={{0,16},{16,0},{32,48},{48,32},{64,80},{80,64},{96,112},{112,96},{1... | collective-permute-start | bytes 208904 | tf_op jit(solution)/shard_map/s_row1/ppermute | solution.py:25
  7.2 5.1 %collective-permute-start.2 = (bf16[272,128]{1,0:T(8,128)(2,1)S(1)}, bf16[272,128]{1,0:T(8,128)(2,1)S(1)}, u32[]{:S(2)}, u32[]{:S(2)}) collective-permute-start(bf16[272,128]{1,0:T(8,128)(2,1)S(1)} %get-tuple-element.61), channel_id=1, source_target_pairs={{0,48},{16,32},{32,16},{48,0},{64,112},{80,96},{96,80},{112,64},{1... | collective-permute-start | bytes 208904 | tf_op jit(solution)/shard_map/s_row3/ppermute | solution.py:25
  12.3 9.8 %collective-permute-start.5 = (bf16[4,272,128]{2,1,0:T(8,128)(2,1)S(1)}, bf16[4,272,128]{2,1,0:T(8,128)(2,1)S(1)}, u32[]{:S(2)}, u32[]{:S(2)}) collective-permute-start(bf16[4,272,128]{2,1,0:T(8,128)(2,1)S(1)} %pad_maximum_fusion.1.right0), channel_id=1, source_target_pairs={{0,64},{16,80},{32,96},{48,112},{64,0},{80,16},{96,32},{112,48},{1... | collective-permute-start | bytes 835592 | tf_op jit(solution)/shard_map/s_row4/ppermute | solution.py:25
  13.6 13.0 %collective-permute-start.3 = (bf16[4,272,128]{2,1,0:T(8,128)(2,1)S(1)}, bf16[4,272,128]{2,1,0:T(8,128)(2,1)S(1)}, u32[]{:S(2)}, u32[]{:S(2)}) collective-permute-start(bf16[4,272,128]{2,1,0:T(8,128)(2,1)S(1)} %pad_maximum_fusion.1.right0), channel_id=1, source_target_pairs={{0,192},{16,208},{32,224},{48,240},{64,128},{80,144},{96,160},{112... | collective-permute-start | bytes 835592 | tf_op jit(solution)/shard_map/s_row12/ppermute | solution.py:25
  15.4 6.7 %collective-permute-start.6 = (bf16[144,128]{1,0:T(8,128)(2,1)S(1)}, bf16[144,128]{1,0:T(8,128)(2,1)S(1)}, u32[]{:S(2)}, u32[]{:S(2)}) collective-permute-start(bf16[144,128]{1,0:T(8,128)(2,1)S(1)} %fusion.5), channel_id=1, source_target_pairs={{0,2},{1,3},{2,0},{3,1},{4,6},{5,7},{6,4},{7,5},{8,10},{9,11},{10,... | collective-permute-start | bytes 110600 | tf_op jit(solution)/shard_map/s_col2/ppermute | solution.py:25
  22.1 4.9 %collective-permute-start.10 = (bf16[2,144,128]{2,1,0:T(8,128)(2,1)S(1)}, bf16[2,144,128]{2,1,0:T(8,128)(2,1)S(1)}, u32[]{:S(2)}, u32[]{:S(2)}) collective-permute-start(bf16[2,144,128]{2,1,0:T(8,128)(2,1)S(1)} %pad_maximum_fusion.5), channel_id=1, source_target_pairs={{0,12},{1,13},{2,14},{3,15},{4,8},{5,9},{6,10},{7,11},{8,4},{9,5},... | collective-permute-start | bytes 221192 | tf_op jit(solution)/shard_map/s_col12/ppermute | solution.py:25
  25.0 4.7 %collective-permute-start.9 = (bf16[2,144,128]{2,1,0:T(8,128)(2,1)S(1)}, bf16[2,144,128]{2,1,0:T(8,128)(2,1)S(1)}, u32[]{:S(2)}, u32[]{:S(2)}) collective-permute-start(bf16[2,144,128]{2,1,0:T(8,128)(2,1)S(1)} %pad_maximum_fusion.5), channel_id=1, source_target_pairs={{0,8},{1,9},{2,10},{3,11},{4,12},{5,13},{6,14},{7,15},{8,0},{9,1},... | collective-permute-start | bytes 221192 | tf_op jit(solution)/shard_map/s_col8/ppermute | solution.py:25
  25.3 4.4 %collective-permute-start.8 = (bf16[2,144,128]{2,1,0:T(8,128)(2,1)S(1)}, bf16[2,144,128]{2,1,0:T(8,128)(2,1)S(1)}, u32[]{:S(2)}, u32[]{:S(2)}) collective-permute-start(bf16[2,144,128]{2,1,0:T(8,128)(2,1)S(1)} %pad_maximum_fusion.5), channel_id=1, source_target_pairs={{0,4},{1,5},{2,6},{3,7},{4,0},{5,1},{6,2},{7,3},{8,12},{9,13},{10,... | collective-permute-start | bytes 221192 | tf_op jit(solution)/shard_map/s_col4/ppermute | solution.py:25
  25.7 5.5 %collective-permute-start.7 = (bf16[2,272,128]{2,1,0:T(8,128)(2,1)S(1)}, bf16[2,272,128]{2,1,0:T(8,128)(2,1)S(1)}, u32[]{:S(2)}, u32[]{:S(2)}) collective-permute-start(bf16[2,272,128]{2,1,0:T(8,128)(2,1)S(1)} %slice.60), channel_id=1, source_target_pairs={{0,192},{16,208},{32,224},{48,240},{64,128},{80,144},{96,160},{112... | collective-permute-start | bytes 417800 | tf_op jit(solution)/shard_map/s_row12/ppermute | solution.py:25
  26.6 11.4 %copy-start = (bf16[8,16,128]{2,1,0:T(8,128)(2,1)S(1)}, bf16[8,16,128]{2,1,0:T(8,128)(2,1)}, u32[]{:S(2)}) copy-start(bf16[8,16,128]{2,1,0:T(8,128)(2,1)} %param.14) | copy-start | bytes 98308
  26.6 11.4 %copy-start.1 = (bf16[128,128]{1,0:T(8,128)(2,1)S(1)}, bf16[128,128]{1,0:T(8,128)(2,1)}, u32[]{:S(2)}) copy-start(bf16[128,128]{1,0:T(8,128)(2,1)} %wq_hbm.1) | copy-start | bytes 98308
  26.6 11.4 %copy-start.2 = (bf16[128,128]{1,0:T(8,128)(2,1)S(1)}, bf16[128,128]{1,0:T(8,128)(2,1)}, u32[]{:S(2)}) copy-start(bf16[128,128]{1,0:T(8,128)(2,1)} %wk_hbm.1) | copy-start | bytes 98308
  26.7 11.4 %copy-start.3 = (bf16[128,128]{1,0:T(8,128)(2,1)S(1)}, bf16[128,128]{1,0:T(8,128)(2,1)}, u32[]{:S(2)}) copy-start(bf16[128,128]{1,0:T(8,128)(2,1)} %wl_hbm.1) | copy-start | bytes 98308
  26.7 11.3 %copy-start.4 = (bf16[128,128]{1,0:T(8,128)(2,1)S(1)}, bf16[128,128]{1,0:T(8,128)(2,1)}, u32[]{:S(2)}) copy-start(bf16[128,128]{1,0:T(8,128)(2,1)} %wr_hbm.1) | copy-start | bytes 98308
  26.7 11.3 %copy-start.5 = (bf16[128,128]{1,0:T(8,128)(2,1)S(1)}, bf16[128,128]{1,0:T(8,128)(2,1)}, u32[]{:S(2)}) copy-start(bf16[128,128]{1,0:T(8,128)(2,1)} %wo_hbm.1) | copy-start | bytes 98308
  26.7 4.5 %collective-permute-start.4 = (bf16[2,272,128]{2,1,0:T(8,128)(2,1)S(1)}, bf16[2,272,128]{2,1,0:T(8,128)(2,1)S(1)}, u32[]{:S(2)}, u32[]{:S(2)}) collective-permute-start(bf16[2,272,128]{2,1,0:T(8,128)(2,1)S(1)} %slice.76), channel_id=1, source_target_pairs={{0,64},{16,80},{32,96},{48,112},{64,0},{80,16},{96,32},{112,48},{1... | collective-permute-start | bytes 417800 | tf_op jit(solution)/shard_map/s_row4/ppermute | solution.py:25
  31.2 6.8 %collective-permute-start.11 = (bf16[8,144,128]{2,1,0:T(8,128)(2,1)S(1)}, bf16[8,144,128]{2,1,0:T(8,128)(2,1)S(1)}, u32[]{:S(2)}, u32[]{:S(2)}) collective-permute-start(bf16[8,144,128]{2,1,0:T(8,128)(2,1)S(1)} %pad_maximum_fusion.left0), channel_id=1, source_target_pairs={{0,1},{1,0},{2,3},{3,2},{4,5},{5,4},{6,7},{7,6},{8,9},{9,8},{10,11... | collective-permute-start | bytes 884744 | tf_op jit(solution)/shard_map/s_col1/ppermute | solution.py:25
  55.0 2.3 %collective-permute-start.12 = (bf16[1344,128]{1,0:T(8,128)(2,1)S(1)}, bf16[1344,128]{1,0:T(8,128)(2,1)S(1)}, u32[]{:S(2)}, u32[]{:S(2)}) collective-permute-start(bf16[1344,128]{1,0:T(8,128)(2,1)S(1)} %get-tuple-element.33), channel_id=1, source_target_pairs={{0,1},{1,0},{2,3},{3,2},{4,5},{5,4},{6,7},{7,6},{8,9},{9,8},{10,11... | collective-permute-start | bytes 1032200 | tf_op jit(solution)/shard_map/s_col1/ppermute | solution.py:25
  55.5 7.8 %collective-permute-start.13 = (bf16[4,256,128]{2,1,0:T(8,128)(2,1)S(1)}, bf16[4,256,128]{2,1,0:T(8,128)(2,1)S(1)}, u32[]{:S(2)}, u32[]{:S(2)}) collective-permute-start(bf16[4,256,128]{2,1,0:T(8,128)(2,1)S(1)} %get-tuple-element.34), channel_id=1, source_target_pairs={{0,64},{16,80},{32,96},{48,112},{64,0},{80,16},{96,32},{112,48},{1... | collective-permute-start | bytes 786440 | tf_op jit(solution)/shard_map/s_row4/ppermute | solution.py:25
  55.5 8.9 %collective-permute-start.14 = (bf16[4,256,128]{2,1,0:T(8,128)(2,1)S(1)}, bf16[4,256,128]{2,1,0:T(8,128)(2,1)S(1)}, u32[]{:S(2)}, u32[]{:S(2)}) collective-permute-start(bf16[4,256,128]{2,1,0:T(8,128)(2,1)S(1)} %get-tuple-element.35), channel_id=1, source_target_pairs={{0,192},{16,208},{32,224},{48,240},{64,128},{80,144},{96,160},{112... | collective-permute-start | bytes 786440 | tf_op jit(solution)/shard_map/s_row12/ppermute | solution.py:25
  57.5 5.0 %collective-permute-start.15 = (bf16[576,128]{1,0:T(8,128)(2,1)S(1)}, bf16[576,128]{1,0:T(8,128)(2,1)S(1)}, u32[]{:S(2)}, u32[]{:S(2)}) collective-permute-start(bf16[576,128]{1,0:T(8,128)(2,1)S(1)} %get-tuple-element.59), channel_id=1, source_target_pairs={{0,4},{1,5},{2,6},{3,7},{4,0},{5,1},{6,2},{7,3},{8,12},{9,13},{10,... | collective-permute-start | bytes 442376 | tf_op jit(solution)/shard_map/s_col4/ppermute | solution.py:25
  58.9 7.7 %collective-permute-start.17 = (bf16[576,128]{1,0:T(8,128)(2,1)S(1)}, bf16[576,128]{1,0:T(8,128)(2,1)S(1)}, u32[]{:S(2)}, u32[]{:S(2)}) collective-permute-start(bf16[576,128]{1,0:T(8,128)(2,1)S(1)} %concatenate.37), channel_id=1, source_target_pairs={{0,12},{1,13},{2,14},{3,15},{4,8},{5,9},{6,10},{7,11},{8,4},{9,5},... | collective-permute-start | bytes 442376 | tf_op jit(solution)/shard_map/s_col12/ppermute | solution.py:25
  60.9 7.5 %collective-permute-start.16 = (bf16[576,128]{1,0:T(8,128)(2,1)S(1)}, bf16[576,128]{1,0:T(8,128)(2,1)S(1)}, u32[]{:S(2)}, u32[]{:S(2)}) collective-permute-start(bf16[576,128]{1,0:T(8,128)(2,1)S(1)} %get-tuple-element.58), channel_id=1, source_target_pairs={{0,8},{1,9},{2,10},{3,11},{4,12},{5,13},{6,14},{7,15},{8,0},{9,1},... | collective-permute-start | bytes 442376 | tf_op jit(solution)/shard_map/s_col8/ppermute | solution.py:25
  64.5 5.1 %collective-permute-start.18 = (bf16[2,256,128]{2,1,0:T(8,128)(2,1)S(1)}, bf16[2,256,128]{2,1,0:T(8,128)(2,1)S(1)}, u32[]{:S(2)}, u32[]{:S(2)}) collective-permute-start(bf16[2,256,128]{2,1,0:T(8,128)(2,1)S(1)} %slice.107), channel_id=1, source_target_pairs={{0,192},{16,208},{32,224},{48,240},{64,128},{80,144},{96,160},{112... | collective-permute-start | bytes 393224 | tf_op jit(solution)/shard_map/s_row12/ppermute | solution.py:25
  66.5 4.2 %collective-permute-start.19 = (bf16[2,256,128]{2,1,0:T(8,128)(2,1)S(1)}, bf16[2,256,128]{2,1,0:T(8,128)(2,1)S(1)}, u32[]{:S(2)}, u32[]{:S(2)}) collective-permute-start(bf16[2,256,128]{2,1,0:T(8,128)(2,1)S(1)} %slice.106), channel_id=1, source_target_pairs={{0,64},{16,80},{32,96},{48,112},{64,0},{80,16},{96,32},{112,48},{1... | collective-permute-start | bytes 393224 | tf_op jit(solution)/shard_map/s_row4/ppermute | solution.py:25
  70.7 8.6 %collective-permute-start.20 = (bf16[448,128]{1,0:T(8,128)(2,1)S(1)}, bf16[448,128]{1,0:T(8,128)(2,1)S(1)}, u32[]{:S(2)}, u32[]{:S(2)}) collective-permute-start(bf16[448,128]{1,0:T(8,128)(2,1)S(1)} %slice.108), channel_id=1, source_target_pairs={{0,2},{1,3},{2,0},{3,1},{4,6},{5,7},{6,4},{7,5},{8,10},{9,11},{10,... | collective-permute-start | bytes 344072 | tf_op jit(solution)/shard_map/s_col2/ppermute | solution.py:25
  75.9 10.1 %all-to-all-start = ((bf16[4,256,128]{2,1,0:T(8,128)(2,1)}), bf16[4,256,128]{2,1,0:T(8,128)(2,1)S(1)}, u32[]{:S(2)}, u32[]{:S(2)}) async-start(bf16[4,256,128]{2,1,0:T(8,128)(2,1)} %pad_maximum_fusion.2), calls=%async_computation | async-start | bytes 524288 | tf_op jit(solution)/shard_map/all_to_all | solution.py:471
  79.4 4.8 %collective-permute-start.23 = (bf16[320,128]{1,0:T(8,128)(2,1)S(1)}, bf16[320,128]{1,0:T(8,128)(2,1)S(1)}, u32[]{:S(2)}, u32[]{:S(2)}) collective-permute-start(bf16[320,128]{1,0:T(8,128)(2,1)S(1)} %fusion.3), channel_id=1, source_target_pairs={{0,192},{16,208},{32,224},{48,240},{64,128},{80,144},{96,160},{112... | collective-permute-start | bytes 245768 | tf_op jit(solution)/shard_map/s_row12/ppermute | solution.py:25
  80.4 4.8 %collective-permute-start.22 = (bf16[320,128]{1,0:T(8,128)(2,1)S(1)}, bf16[320,128]{1,0:T(8,128)(2,1)S(1)}, u32[]{:S(2)}, u32[]{:S(2)}) collective-permute-start(bf16[320,128]{1,0:T(8,128)(2,1)S(1)} %fusion.3), channel_id=1, source_target_pairs={{0,128},{16,144},{32,160},{48,176},{64,192},{80,208},{96,224},{112... | collective-permute-start | bytes 245768 | tf_op jit(solution)/shard_map/s_row8/ppermute | solution.py:25
  81.2 4.7 %collective-permute-start.21 = (bf16[320,128]{1,0:T(8,128)(2,1)S(1)}, bf16[320,128]{1,0:T(8,128)(2,1)S(1)}, u32[]{:S(2)}, u32[]{:S(2)}) collective-permute-start(bf16[320,128]{1,0:T(8,128)(2,1)S(1)} %fusion.3), channel_id=1, source_target_pairs={{0,64},{16,80},{32,96},{48,112},{64,0},{80,16},{96,32},{112,48},{1... | collective-permute-start | bytes 245768 | tf_op jit(solution)/shard_map/s_row4/ppermute | solution.py:25
  86.0 5.2 %collective-permute-start.26 = (bf16[320,128]{1,0:T(8,128)(2,1)S(1)}, bf16[320,128]{1,0:T(8,128)(2,1)S(1)}, u32[]{:S(2)}, u32[]{:S(2)}) collective-permute-start(bf16[320,128]{1,0:T(8,128)(2,1)S(1)} %add_convert_fusion.1), channel_id=1, source_target_pairs={{0,48},{16,32},{32,16},{48,0},{64,112},{80,96},{96,80},{112,64},{1... | collective-permute-start | bytes 245768 | tf_op jit(solution)/shard_map/s_row3/ppermute | solution.py:25
  89.0 4.5 %collective-permute-start.25 = (bf16[320,128]{1,0:T(8,128)(2,1)S(1)}, bf16[320,128]{1,0:T(8,128)(2,1)S(1)}, u32[]{:S(2)}, u32[]{:S(2)}) collective-permute-start(bf16[320,128]{1,0:T(8,128)(2,1)S(1)} %add_convert_fusion.1), channel_id=1, source_target_pairs={{0,32},{16,48},{32,0},{48,16},{64,96},{80,112},{96,64},{112,80},{1... | collective-permute-start | bytes 245768 | tf_op jit(solution)/shard_map/s_row2/ppermute | solution.py:25
  89.0 4.5 %collective-permute-start.24 = (bf16[320,128]{1,0:T(8,128)(2,1)S(1)}, bf16[320,128]{1,0:T(8,128)(2,1)S(1)}, u32[]{:S(2)}, u32[]{:S(2)}) collective-permute-start(bf16[320,128]{1,0:T(8,128)(2,1)S(1)} %add_convert_fusion.1), channel_id=1, source_target_pairs={{0,16},{16,0},{32,48},{48,32},{64,80},{80,64},{96,112},{112,96},{1... | collective-permute-start | bytes 245768 | tf_op jit(solution)/shard_map/s_row1/ppermute | solution.py:25
  93.5 6.6 %collective-permute-start.27 = (bf16[320,128]{1,0:T(8,128)(2,1)S(1)}, bf16[320,128]{1,0:T(8,128)(2,1)S(1)}, u32[]{:S(2)}, u32[]{:S(2)}) collective-permute-start(bf16[320,128]{1,0:T(8,128)(2,1)S(1)} %add_convert_fusion), channel_id=1, source_target_pairs={{0,1},{1,0},{2,3},{3,2},{4,5},{5,4},{6,7},{7,6},{8,9},{9,8},{10,11... | collective-permute-start | bytes 245768 | tf_op jit(solution)/shard_map/s_col1/ppermute | solution.py:25
